TPU v7x, 128 devices: a whole 4x4x4 slice. The times are simulated.
128 devices in a mesh: fsdp: 16 (over x_lo, z, core), tp: 8 (over x_hi, y).
Axes of the slice: x: 4 (x_hi: 2, x_lo: 2; x = x_hi * 2 + x_lo), y: 4, z: 4, core: 2. Of those that a mesh axis runs over, the one named last changes fastest.
Arguments:
- inputs: bfloat16 [2, 128, 8192], P(None, 'tp'), may hold values from -6 to 6
- w_xz: bfloat16 [8192, 128, 128], P('fsdp', 'tp'), may hold values from -0.0625 to 0.0625
- w_dt: bfloat16 [8192, 128], P('fsdp', 'tp'), may hold values from -0.0625 to 0.0625
- w_bc: bfloat16 [8192, 2048], P('fsdp', 'tp'), may hold values from -0.0625 to 0.0625
- w_out: bfloat16 [128, 64, 8192], P('tp', None, 'fsdp'), may hold values from -0.0625 to 0.0625
- head_map: int32 [16], replicated, may hold values from 0 to 15, each once
- a_log: float32 [128], replicated, may hold values from 0 to 2.77
- dt_bias: float32 [128], replicated, may hold values from -4 to -1
- skip_coef: float32 [128], replicated, may hold values from 0.5 to 2.5
- conv_x: float32 [5, 8192], replicated, may hold values from -3 to 3
- conv_bc: float32 [5, 2048], replicated, may hold values from -3 to 3
- norm_gain: float32 [8192], replicated, may hold values from 0.25 to 1.75
- ssm_state: float32 [128, 128, 64, 256], P('tp', 'fsdp'), may hold values from -26 to 26, as said below
- conv_x_state: float32 [128, 3, 8192], P('tp', None, 'fsdp'), may hold values from -6 to 6
- conv_bc_state: float32 [128, 3, 2048], P('tp'), may hold values from -6 to 6
Outputs:
- mixed: bfloat16 [2, 128, 8192], P(None, 'tp', 'fsdp')
- ssm_state_out: float32 [128, 128, 64, 256], P('tp', 'fsdp')
- conv_x_state_out: float32 [128, 3, 8192], P('tp', None, 'fsdp')
- conv_bc_state_out: float32 [128, 3, 2048], P('tp')
Inputs may be any that keep to these rules, and one draw needn't show every extreme that they name: `ssm_state`: the rollout's recurrent states.
All inputs are finite; a program needn't handle non-finite values.
Results may differ from a plain program's by a relative error of at most 0.0052.
Values may be sent and summed in bfloat16 or wider, within the bound.
No kernel may reach another device: no remote copies, remote signals or barrier semaphores. Data moves between devices by JAX's collectives and lax.ppermute only.
A program may use at most 192 MiB of HBM per device.

v0:
```python
import jax
import jax.numpy as jnp
from jax import lax
from jax.sharding import PartitionSpec as P

STATE = 256
GROUPS = 4
KERNEL = 4


EPSILON = 1e-05
HIGHEST = lax.Precision.HIGHEST


def conv_apply(history, fresh_in, conv_taps):
    window = jnp.concatenate([history, fresh_in[:, None, :]], axis=1)
    summed = jnp.sum(window * conv_taps[None, :-1, :], axis=1) + conv_taps[None, -1, :]
    return (jax.nn.silu(summed), window[:, 1:, :])


def per_device(
    inputs,
    w_xz,
    w_dt,
    w_bc,
    w_out,
    head_map,
    a_log,
    dt_bias,
    skip_coef,
    conv_x,
    conv_bc,
    norm_gain,
    ssm_state,
    conv_x_state,
    conv_bc_state,
):
    slices = lax.axis_size("fsdp")
    replicas = lax.axis_size("tp")
    chosen = head_map[lax.axis_index("fsdp")]
    d_part, heads_tp, width_xz = w_xz.shape
    head_dim = width_xz // 2
    per_class = heads_tp // slices
    head_total = a_log.shape[0]
    head_slots = head_total // slices
    bc_piece = w_bc.shape[1] // slices
    row_count = inputs.shape[1]
    steps_total = inputs.shape[0]
    xz_send = jnp.moveaxis(
        jnp.take(w_xz.reshape(d_part, per_class, slices, width_xz), head_map, axis=2), 2, 0
    )
    dt_send = jnp.moveaxis(
        jnp.take(w_dt.reshape(d_part, per_class, slices), head_map, axis=2), 2, 0
    )
    bc_send = jnp.moveaxis(w_bc.reshape(d_part, slices, bc_piece), 1, 0)
    out_send = jnp.moveaxis(
        jnp.take(w_out.reshape(per_class, slices, head_dim, d_part), head_map, axis=1), 1, 0
    )

    def widen_all(portion):
        copies = jnp.broadcast_to(portion[:, None], (slices, replicas) + portion.shape[1:])
        return copies.reshape((slices * replicas,) + portion.shape[1:])

    received = (
        lax.all_to_all(widen_all(xz_send), ("fsdp", "tp"), split_axis=0, concat_axis=0, tiled=True),
        lax.all_to_all(widen_all(dt_send), ("fsdp", "tp"), split_axis=0, concat_axis=0, tiled=True),
        lax.all_to_all(widen_all(bc_send), ("fsdp", "tp"), split_axis=0, concat_axis=0, tiled=True),
        lax.all_to_all(
            widen_all(out_send), ("fsdp", "tp"), split_axis=0, concat_axis=0, tiled=True
        ),
    )
    xz_roll, dt_roll, bc_roll, out_roll = [
        portion.reshape((slices, replicas) + portion.shape[1:]) for portion in received
    ]
    a_local = lax.dynamic_index_in_dim(a_log.reshape(head_slots, slices), chosen, 1, keepdims=False)
    bias_local = lax.dynamic_index_in_dim(
        dt_bias.reshape(head_slots, slices), chosen, 1, keepdims=False
    )
    skip_local = lax.dynamic_index_in_dim(
        skip_coef.reshape(head_slots, slices), chosen, 1, keepdims=False
    )
    gain_local = lax.dynamic_index_in_dim(
        norm_gain.reshape(head_slots, slices, head_dim), chosen, 1, keepdims=False
    )
    taps_x = lax.dynamic_index_in_dim(
        conv_x.reshape(KERNEL + 1, head_slots, slices, head_dim), chosen, 2, keepdims=False
    ).reshape(KERNEL + 1, head_slots * head_dim)
    head_ids = chosen + slices * jnp.arange(head_slots, dtype=jnp.int32)
    group_ids = head_ids // (head_total // GROUPS)
    onehot = (group_ids[:, None] == jnp.arange(GROUPS, dtype=jnp.int32)[None, :]).astype(
        jnp.float32
    )
    group_width = head_total // GROUPS * head_dim
    ssm_now = ssm_state
    x_hist = conv_x_state
    bc_hist = conv_bc_state
    outputs = []
    for turn_index in range(steps_total):
        x_split = inputs[turn_index].reshape(row_count, slices, d_part)
        proj_xz = jnp.einsum(
            "tir,ijrup->tjup", x_split, xz_roll, preferred_element_type=jnp.float32
        ).reshape(row_count, head_slots, width_xz)
        dt_raw = jnp.einsum(
            "tir,ijru->tju", x_split, dt_roll, preferred_element_type=jnp.float32
        ).reshape(row_count, head_slots)
        bc_local = jnp.einsum(
            "tir,ijrv->tjv", x_split, bc_roll, preferred_element_type=jnp.float32
        ).astype(jnp.bfloat16)
        bc_all = lax.all_gather(bc_local[:, :, None, :], "fsdp", axis=2, tiled=True)
        bc_full = lax.optimization_barrier(bc_all.reshape(row_count, -1)).astype(jnp.float32)
        bc_act, bc_hist = conv_apply(bc_hist, bc_full, conv_bc)
        bc_split = bc_act.reshape(row_count, GROUPS, 2, STATE)
        b_head = jnp.einsum("tgn,hg->thn", bc_split[:, :, 0], onehot, precision=HIGHEST)
        c_head = jnp.einsum("tgn,hg->thn", bc_split[:, :, 1], onehot, precision=HIGHEST)
        x_act, x_hist = conv_apply(
            x_hist, proj_xz[:, :, :head_dim].reshape(row_count, head_slots * head_dim), taps_x
        )
        x_act = x_act.reshape(row_count, head_slots, head_dim)
        gate_in = proj_xz[:, :, head_dim:]
        step_size = jax.nn.softplus(dt_raw + bias_local[None, :])
        decay_rate = jnp.exp(-step_size * jnp.exp(a_local)[None, :])
        ssm_now = (
            decay_rate[:, :, None, None] * ssm_now
            + (step_size[:, :, None] * x_act)[:, :, :, None] * b_head[:, :, None, :]
        )
        y_read = (
            jnp.einsum("thpn,thn->thp", ssm_now, c_head, precision=HIGHEST)
            + skip_local[None, :, None] * x_act
        )
        gated_out = y_read * jax.nn.silu(gate_in)
        squares = jnp.sum(gated_out * gated_out, axis=2)
        group_sums = lax.psum(jnp.dot(squares, onehot, precision=HIGHEST), "fsdp")
        inv_rms = lax.rsqrt(group_sums / group_width + EPSILON)
        per_head = jnp.dot(inv_rms, onehot.T, precision=HIGHEST)
        normed = (gated_out * per_head[:, :, None] * gain_local[None]).astype(jnp.bfloat16)
        partial_value = jnp.einsum(
            "tjup,ijupr->tir",
            normed.reshape(row_count, replicas, per_class, head_dim),
            out_roll,
            preferred_element_type=jnp.float32,
        ).reshape(row_count, slices * d_part)
        outputs.append(
            lax.psum_scatter(partial_value, "fsdp", scatter_dimension=1, tiled=True).astype(
                jnp.bfloat16
            )
        )
    return (jnp.stack(outputs), ssm_now, x_hist, bc_hist)


def solution(mesh):
    return jax.shard_map(
        per_device,
        mesh=mesh,
        in_specs=(
            P(None, "tp", None),
            P("fsdp", "tp", None),
            P("fsdp", "tp"),
            P("fsdp", "tp"),
            P("tp", None, "fsdp"),
            P(),
            P(),
            P(),
            P(),
            P(),
            P(),
            P(),
            P("tp", "fsdp", None, None),
            P("tp", None, "fsdp"),
            P("tp", None, None),
        ),
        out_specs=(
            P(None, "tp", "fsdp"),
            P("tp", "fsdp", None, None),
            P("tp", None, "fsdp"),
            P("tp", None, None),
        ),
        check_vma=False,
    )
```

profile of v0, /device:TPU:0, one launch (start us, length us, event | category | flops | bytes accessed | tf_op | source)
XLA Modules:
  0.0 710.0 jit_solution(18300703600080697398)
XLA Ops:
  8.7 1.3 gather_fusion
  10.9 1.4 reduce.10
  13.0 11.1 %all-to-all-start = ((bf16[128,2,256]{2,1,0:T(2,128)(2,1)}), bf16[128,2,256]{2,1,0:T(2,128)(2,1)S(1)}, u32[]{:S(2)}, u32[]{:S(2)}) async-start(bf16[128,2,256]{2,1,0:T(2,128)(2,1)} %reshape.430), calls=%async_computation | async-start | bytes 262144 | tf_op jit(solution)/shard_map/all_to_all | solution.py:66
  25.2 8.4 %all-to-all-done = bf16[128,2,256]{2,1,0:T(2,128)(2,1)S(1)} async-done(((bf16[128,2,256]{2,1,0:T(2,128)(2,1)}), bf16[128,2,256]{2,1,0:T(2,128)(2,1)S(1)}, u32[]{:S(2)}, u32[]{:S(2)}) %all-to-all-start) | async-done | bytes 131104 | tf_op jit(solution)/shard_map/all_to_all | solution.py:66
  33.6 1.6 broadcast_in_dim.118
  35.2 5.8 all-to-all-start.2
  41.0 1.7 gather_fusion.2
  42.7 1.4 broadcast_select_fusion
  44.1 25.1 %all-to-all-done.2 = bf16[128,512,16]{1,2,0:T(8,128)(2,1)} async-done(((bf16[128,512,16]{1,2,0:T(8,128)(2,1)}), bf16[128,512,16]{1,2,0:T(8,128)(2,1)}, u32[]{:S(2)}, u32[]{:S(2)}) %all-to-all-start.2) | async-done | bytes 2097184 | tf_op jit(solution)/shard_map/all_to_all | solution.py:67
  69.2 4.5 broadcast_in_dim.124
  73.6 7.2 %all-to-all-start.3 = ((bf16[128,1,64,512]{3,2,1,0:T(8,128)(2,1)}), bf16[128,1,64,512]{3,2,1,0:T(8,128)(2,1)}, u32[]{:S(2)}, u32[]{:S(2)}) async-start(bf16[128,1,64,512]{3,2,1,0:T(8,128)(2,1)} %bitcast.199), calls=%async_computation.3 | async-start | bytes 16777216 | tf_op jit(solution)/shard_map/all_to_all | solution.py:68
  80.8 8.1 %gather_fusion.1 = bf16[16,512,128]{2,0,1:T(8,128)(2,1)} fusion(bf16[512,16,128]{2,1,0:T(8,128)(2,1)S(1)} %copy-done, s32[1024]{0:T(1024)} %copy-done.10), kind=kCustom, calls=%fused_computation.1 | custom fusion | bytes 4194368 | tf_op jit(solution)/shard_map/jit(_take)/gather | solution.py:50
  89.0 1.8 fusion.4
  91.3 95.1 %all-to-all-done.3 = bf16[128,1,64,512]{3,2,1,0:T(8,128)(2,1)} async-done(((bf16[128,1,64,512]{3,2,1,0:T(8,128)(2,1)}), bf16[128,1,64,512]{3,2,1,0:T(8,128)(2,1)}, u32[]{:S(2)}, u32[]{:S(2)}) %all-to-all-start.3) | async-done | bytes 8388640 | tf_op jit(solution)/shard_map/all_to_all | solution.py:68
  186.5 6.1 broadcast_in_dim.116
  192.7 10.2 %all-to-all-start.1 = ((bf16[128,512,1,128]{3,1,2,0:T(8,128)(2,1)}), bf16[128,512,1,128]{3,1,2,0:T(8,128)(2,1)}, u32[]{:S(2)}, u32[]{:S(2)}) async-start(bf16[128,512,1,128]{3,1,2,0:T(8,128)(2,1)} %bitcast.198), calls=%async_computation.1 | async-start | bytes 33554432 | tf_op jit(solution)/shard_map/all_to_all | solution.py:65
  208.3 4.1 fusion.5
  212.6 228.2 %all-gather = bf16[16,8,256]{0,1,2:T(8,128)(2,1)S(1)} all-gather(bf16[16,8,16]{0,1,2:T(8,128)(2,1)S(1)} %copy.93), channel_id=2, replica_groups=mesh['fsdp'=16,'tp'=8] {'fsdp'}, dimensions={2}, use_global_device_ids=true | all-gather | bytes 69632 | tf_op jit(solution)/shard_map/all_gather | solution.py:109
  441.2 4.1 fusion.6
  445.4 28.8 %all-gather.1 = bf16[16,8,256]{0,1,2:T(8,128)(2,1)S(1)} all-gather(bf16[16,8,16]{0,1,2:T(8,128)(2,1)S(1)} %copy.106), channel_id=3, replica_groups=mesh['fsdp'=16,'tp'=8] {'fsdp'}, dimensions={2}, use_global_device_ids=true | all-gather | bytes 69632 | tf_op jit(solution)/shard_map/all_gather | solution.py:109
  476.2 7.8 %copy.125 = bf16[16,8,8,8,512]{4,3,0,2,1:T(8,128)(2,1)} copy(bf16[16,8,8,8,512]{4,3,2,1,0:T(8,128)(2,1)} %bitcast.81) | data formatting | bytes 16777216 | tf_op jit(solution)/shard_map/tjup,ijupr->tir/dot_general | solution.py:136
  484.1 8.2 %convolution_bitcast_fusion.9 = f32[16,8,128]{2,0,1:T(8,128)S(1)} fusion(bf16[16,8,512,128]{3,2,1,0:T(8,128)(2,1)} %bitcast.13, bf16[16,16,512,1]{2,1,0,3:T(8,128)(2,1)S(1)} %bitcast.206), kind=kOutput, calls=%fused_computation.20 | convolution fusion | flops 268435456 | bytes 17104896 | tf_op jit(solution)/shard_map/tir,ijrup->tjup/dot_general | solution.py:100
  492.4 8.2 %convolution_bitcast_fusion.8 = f32[16,8,128]{2,0,1:T(8,128)S(1)} fusion(bf16[16,8,512,128]{3,2,1,0:T(8,128)(2,1)} %bitcast.13, bf16[16,16,512,1]{2,1,0,3:T(8,128)(2,1)S(1)} %bitcast.203), kind=kOutput, calls=%fused_computation.19 | convolution fusion | flops 268435456 | bytes 17104896 | tf_op jit(solution)/shard_map/tir,ijrup->tjup/dot_general | solution.py:100
  501.1 10.5 %fusion = f32[16,8,1,64]{3,2,1,0:T(1,128)S(1)} fusion(f32[16,8,64,256]{3,2,1,0:T(8,128)} %param.27, f32[16,8,256]{2,1,0:T(8,128)S(1)} %convolution_bitcast_fusion.5, f32[16,8,64]{2,1,0:T(8,128)S(1)} %copy.89, f32[16,8]{1,0:T(8,128)S(1)} %copy.83, f32[16,8,256,1]{2,1,0,3:T(8,128)S(1)} %convolution_bitcast_fusion.4), kind=kOutput, calls=%fused_computation.7 | convolution fusion | flops 31457280 | bytes 8716800 | tf_op jit(solution)/shard_map/thpn,thn->thp/dot_general | solution.py:127
  511.6 7.2 %multiply_add_fusion = f32[16,8,64,256]{3,2,1,0:T(8,128)S(1)} fusion(f32[16,8,64,256]{3,2,1,0:T(8,128)} %param.27, f32[16,8,256]{2,1,0:T(8,128)S(1)} %convolution_bitcast_fusion.3, f32[16,8,64]{2,1,0:T(8,128)S(1)} %copy.103, f32[16,8]{1,0:T(8,128)S(1)} %copy.99, f32[16,8,256]{2,1,0:T(8,128)S(1)} %convolution_bitcast_fusion.5, f32[16,8,64]{2,1,0:T(8,128)S(1)} %copy.89, ...), kind=kLoop, calls=%fused_computation.5 | loop fusion | flops 12582912 | bytes 17105920 | tf_op jit(solution)/shard_map/add | solution.py:123
  518.9 3.4 copy-done.2
  522.3 7.2 %fusion.29 = f32[16,8,1,64]{3,2,1,0:T(1,128)S(1)} fusion(f32[16,8,64,256]{3,2,1,0:T(8,128)S(1)} %multiply_add_fusion, f32[16,8,256,1]{2,1,0,3:T(8,128)S(1)} %convolution_bitcast_fusion.2), kind=kOutput, calls=%fused_computation.59 | convolution fusion | flops 25165824 | bytes 8552448 | tf_op jit(solution)/shard_map/thpn,thn->thp/dot_general | solution.py:127
  530.0 30.9 %all-reduce = (f32[16,4]{0,1:T(4,128)S(1)}, f32[16,4]{0,1:T(4,128)S(1)}) all-reduce(f32[16,4]{0,1:T(4,128)S(1)} %fusion.58, f32[16,4]{0,1:T(4,128)S(1)} %fusion.59), channel_id=1, replica_groups=mesh['fsdp'=16,'tp'=8] {'fsdp'}, use_global_device_ids=true, to_apply=%region_8.9 | all-reduce | flops 128 | bytes 1024 | tf_op jit(solution)/shard_map/psum | solution.py:132
  561.0 5.6 convolution_bitcast_fusion.1
  566.9 5.5 convolution_bitcast_fusion
  573.8 66.1 %reduce-scatter.3.cloned.1.call-done = f32[16,512]{1,0:T(8,128)} async-done(((f32[16,8192]{1,0:T(8,128)}), f32[16,512]{1,0:T(8,128)}) %reduce-scatter.3.cloned.1.call-update) | async-done | bytes 32784 | tf_op jit(solution)/shard_map/reduce_scatter | solution.py:143
  640.7 60.9 %reduce-scatter.5.cloned.1.call-done = f32[16,512]{1,0:T(8,128)} async-done(((f32[16,8192]{1,0:T(8,128)}), f32[16,512]{1,0:T(8,128)}) %reduce-scatter.5.cloned.1.call-update) | async-done | bytes 32784 | tf_op jit(solution)/shard_map/reduce_scatter | solution.py:143
  (113 shorter events, 15.7 us)
Async XLA Ops:
  7.2 73.6 %copy-start = (bf16[512,16,128]{2,1,0:T(8,128)(2,1)S(1)}, bf16[512,16,128]{2,1,0:T(8,128)(2,1)}, u32[]{:S(2)}) copy-start(bf16[512,16,128]{2,1,0:T(8,128)(2,1)} %param.16) | copy-start | bytes 6291460
  7.2 33.8 %copy-start.4 = (bf16[16,64,512]{2,1,0:T(8,128)(2,1)S(1)}, bf16[16,64,512]{2,1,0:T(8,128)(2,1)}, u32[]{:S(2)}) copy-start(bf16[16,64,512]{2,1,0:T(8,128)(2,1)} %param.19) | copy-start | bytes 3145732
  8.7 1.4 copy-start.11
  8.7 1.4 copy-start.10
  13.0 20.6 %all-to-all-start = ((bf16[128,2,256]{2,1,0:T(2,128)(2,1)}), bf16[128,2,256]{2,1,0:T(2,128)(2,1)S(1)}, u32[]{:S(2)}, u32[]{:S(2)}) async-start(bf16[128,2,256]{2,1,0:T(2,128)(2,1)} %reshape.430), calls=%async_computation | async-start | bytes 262144 | tf_op jit(solution)/shard_map/all_to_all | solution.py:66
  35.2 34.0 %all-to-all-start.2 = ((bf16[128,512,16]{1,2,0:T(8,128)(2,1)}), bf16[128,512,16]{1,2,0:T(8,128)(2,1)}, u32[]{:S(2)}, u32[]{:S(2)}) async-start(bf16[128,512,16]{1,2,0:T(8,128)(2,1)} %bitcast.200), calls=%async_computation.2 | async-start | bytes 4194304 | tf_op jit(solution)/shard_map/all_to_all | solution.py:67
  73.6 112.8 %all-to-all-start.3 = ((bf16[128,1,64,512]{3,2,1,0:T(8,128)(2,1)}), bf16[128,1,64,512]{3,2,1,0:T(8,128)(2,1)}, u32[]{:S(2)}, u32[]{:S(2)}) async-start(bf16[128,1,64,512]{3,2,1,0:T(8,128)(2,1)} %bitcast.199), calls=%async_computation.3 | async-start | bytes 16777216 | tf_op jit(solution)/shard_map/all_to_all | solution.py:68
  80.8 8.1 %copy-start.12 = (pred[16]{0:T(512)(128)(4,1)S(1)}, pred[16]{0:T(512)(128)(4,1)}, u32[]{:S(2)}) copy-start(pred[16]{0:T(512)(128)(4,1)} %copy-done.11) | copy-start | bytes 52
  192.6 10.3 %copy-start.16 = (s32[16]{0:T(128)S(1)}, s32[16]{0:T(128)}, u32[]{:S(2)}) copy-start(s32[16]{0:T(128)} %param.20) | copy-start | bytes 196
  192.6 12.2 %copy-start.13 = (f32[128]{0:T(128)S(1)}, f32[128]{0:T(128)}, u32[]{:S(2)}) copy-start(f32[128]{0:T(128)} %param.22) | copy-start | bytes 1540
  192.6 12.3 %copy-start.14 = (f32[128]{0:T(128)S(1)}, f32[128]{0:T(128)}, u32[]{:S(2)}) copy-start(f32[128]{0:T(128)} %param.21) | copy-start | bytes 1540
  192.6 12.4 %copy-start.5 = (bf16[2,16,8192]{2,1,0:T(8,128)(2,1)S(1)}, bf16[2,16,8192]{2,1,0:T(8,128)(2,1)}, u32[]{:S(2)}) copy-start(bf16[2,16,8192]{2,1,0:T(8,128)(2,1)} %param.15) | copy-start | bytes 1572868
  192.6 12.6 %copy-start.6 = (f32[5,8192]{1,0:T(8,128)S(1)}, f32[5,8192]{1,0:T(8,128)}, u32[]{:S(2)}) copy-start(f32[5,8192]{1,0:T(8,128)} %param.24) | copy-start | bytes 491524
  192.6 13.5 %copy-start.7 = (f32[5,2048]{1,0:T(8,128)S(1)}, f32[5,2048]{1,0:T(8,128)}, u32[]{:S(2)}) copy-start(f32[5,2048]{1,0:T(8,128)} %param.25) | copy-start | bytes 122884
  192.6 13.5 %copy-start.15 = (f32[128]{0:T(128)S(1)}, f32[128]{0:T(128)}, u32[]{:S(2)}) copy-start(f32[128]{0:T(128)} %param.23) | copy-start | bytes 1540
  192.6 13.8 %copy-start.9 = (f32[8192]{0:T(1024)S(1)}, f32[8192]{0:T(1024)}, u32[]{:S(2)}) copy-start(f32[8192]{0:T(1024)} %param.26) | copy-start | bytes 98308
  192.6 14.8 %copy-start.8 = (f32[16,3,512]{2,0,1:T(8,128)S(1)}, f32[16,3,512]{2,0,1:T(8,128)}, u32[]{:S(2)}) copy-start(f32[16,3,512]{2,0,1:T(8,128)} %param.28) | copy-start | bytes 294916
  192.7 291.4 %all-to-all-start.1 = ((bf16[128,512,1,128]{3,1,2,0:T(8,128)(2,1)}), bf16[128,512,1,128]{3,1,2,0:T(8,128)(2,1)}, u32[]{:S(2)}, u32[]{:S(2)}) async-start(bf16[128,512,1,128]{3,1,2,0:T(8,128)(2,1)} %bitcast.198), calls=%async_computation.1 | async-start | bytes 33554432 | tf_op jit(solution)/shard_map/all_to_all | solution.py:65
  202.8 271.8 %copy-start.3 = (f32[16,3,2048]{2,0,1:T(8,128)S(1)}, f32[16,3,2048]{2,0,1:T(8,128)}, u32[]{:S(2)}) copy-start(f32[16,3,2048]{2,0,1:T(8,128)} %param.29) | copy-start | bytes 1179652
  202.8 271.8 %slice-start = ((f32[5,2048]{1,0:T(8,128)}), f32[4,2048]{1,0:T(4,128)S(1)}, s32[]{:S(2)}) async-start(f32[5,2048]{1,0:T(8,128)} %param.25), calls=%async_computation.8 | async-start | bytes 65536 | tf_op jit(solution)/shard_map/slice | solution.py:17
  202.9 437.1 %reduce-scatter.3.cloned.1.call-start = ((), (), s32[]{:S(2)}) async-start(), calls=%async_computation.6 | async-start | bytes 557056 | tf_op jit(solution)/shard_map/reduce_scatter | solution.py:143
  518.9 3.4 copy-start.2
  561.0 141.9 %copy-start.1 = (bf16[512,16,128]{2,1,0:T(8,128)(2,1)S(1)}, bf16[512,16,128]{2,1,0:T(8,128)(2,1)}, u32[]{:S(2)}) copy-start(bf16[512,16,128]{2,1,0:T(8,128)(2,1)} %param.16) | copy-start | bytes 6291460
  566.7 134.9 %reduce-scatter.5.cloned.1.call-start = ((), (), s32[]{:S(2)}) async-start(), calls=%async_computation.7 | async-start | bytes 557056 | tf_op jit(solution)/shard_map/reduce_scatter | solution.py:143
Sparse Core Ops, SparseCore 0:
  566.8 73.0 reduce-scatter.2
  642.4 59.1 reduce-scatter.4
where the time goes:
time: 715 us; the launch traced here: 710 us
  blocking collectives  288 us (40%)
  waiting for transfers between devices  256 us (36%)
  matrix products  55.7 us (8%)
  local copies, waits for them, and re-layouts  41.4 us (6%)
  starting transfers between devices  34.4 us (5%)
  other arithmetic  18.4 us (3%)
  between operations  16.8 us (2%)
    all_gather x2, blocking collectives, per_device(): bc_all = lax.all_gather(bc_local[:, :, None, :], 'fsdp', axis=2, tiled=True)  257 us
    reduce_scatter x2, waiting for transfers between devices, per_device(): lax.psum_scatter(partial_value, 'fsdp', scatter_dimension=1, tiled=True)  127 us
    all_to_all x1, waiting for transfers between devices, per_device(): lax.all_to_all(widen_all(out_send), ('fsdp', 'tp'), split_axis=0, concat_...  95.1 us
    psum x1, blocking collectives, per_device(): group_sums = lax.psum(jnp.dot(squares, onehot, precision=HIGHEST), 'fsdp')  30.9 us
    all_to_all x1, waiting for transfers between devices, per_device(): lax.all_to_all(widen_all(bc_send), ('fsdp', 'tp'), split_axis=0, concat_a...  25.1 us
    dot_general x2, matrix products, per_device(): jnp.einsum('thpn,thn->thp', ssm_now, c_head, precision=HIGHEST)  17.7 us
    dot_general x2, matrix products, per_device(): jnp.einsum('tir,ijrup->tjup', x_split, xz_roll, preferred_element_type=jn...  16.4 us
  transfers between devices with their start and end apart: 6, of which 5 were waited for; matrix products, arithmetic and copies ran while one was open for 6% of the time, Pallas kernels for 0%

commit v1 on v0

v1 whole, which is shorter than its diff:
```python
import jax
import jax.numpy as jnp
from jax import lax
from jax.experimental import pallas as pl
from jax.experimental.pallas import tpu as pltpu
from jax.sharding import PartitionSpec as P

EPSILON = 1e-05
BOTH = ("fsdp", "tp")
F32 = jnp.float32
BF16 = jnp.bfloat16
VMEM_BYTES = 48 * 2**20


def silu(v):
    return v * jax.nn.sigmoid(v)


def project_kernel(map_ref, x_ref, w_ref, wdt_ref, wbc_ref, o_ref, dt_scr, bc_scr):
    part = pl.program_id(0)
    x = x_ref[...]

    @pl.when(part == 0)
    def _():
        bc_scr[...] = jnp.dot(x, wbc_ref[...], preferred_element_type=F32)
        dt_scr[...] = jnp.dot(x, wdt_ref[...], preferred_element_type=F32).T

    per = o_ref.shape[0]
    for k in range(per):
        s = part * per + k
        head = map_ref[s]
        w = w_ref[:, pl.ds(pl.multiple_of(head * 128, 128), 128)]
        y = jnp.dot(x, w, preferred_element_type=F32)
        dt_row = dt_scr[pl.ds(head, 1), :]
        for t in range(8):
            o_ref[k, t, 0:32, :] = y[32 * t : 32 * t + 32, :]
            rows = bc_scr[pl.ds(pl.multiple_of(32 * t + 8 * part, 8), 8), :][2 * k : 2 * k + 2]
            dt = jnp.concatenate(
                [dt_row[:, 32 * t : 32 * t + 32], jnp.zeros((1, 96), F32)], axis=1
            )
            o_ref[k, t, 32:40, :] = jnp.concatenate(
                [rows[:, 0:128], rows[:, 128:256], dt, jnp.zeros((3, 128), F32)], axis=0
            )


def project(head_map, x, w, w_dt, w_bc):
    def whole(*shape):
        return pl.BlockSpec(shape, lambda i, m: (0,) * len(shape))

    return pl.pallas_call(
        project_kernel,
        grid_spec=pltpu.PrefetchScalarGridSpec(
            num_scalar_prefetch=1,
            grid=(4,),
            in_specs=[whole(256, 512), whole(512, 2048), whole(512, 16), whole(512, 256)],
            out_specs=pl.BlockSpec((4, 8, 40, 128), lambda i, m: (i, 0, 0, 0)),
            scratch_shapes=[pltpu.VMEM((16, 256), F32), pltpu.VMEM((256, 256), F32)],
        ),
        out_shape=jax.ShapeDtypeStruct((16, 8, 40, 128), F32),
        compiler_params=pltpu.CompilerParams(vmem_limit_bytes=VMEM_BYTES),
        cost_estimate=pl.CostEstimate(flops=600_000_000, bytes_accessed=5_500_000, transcendentals=0),
        name="project",
    )(head_map, x, w, w_dt, w_bc)


def mixer_kernel(
    coef_ref, par_ref, xz_ref, bc_ref, bc_taps_ref, x_hist_ref, bc_hist_ref, s_ref,
    g_ref, s_out_ref, x_out_ref, bc_out_ref,
):
    group = pl.program_id(0)

    def conv(hist_ref, out_ref, one, two, taps):
        h0, h1, h2 = hist_ref[:, 0, :], hist_ref[:, 1, :], hist_ref[:, 2, :]
        k0, k1, k2, k3, bias = (taps[i : i + 1, :] for i in range(5))
        out_ref[:, 0, :] = h2
        out_ref[:, 1, :] = one
        out_ref[:, 2, :] = two
        first = (h0 * k0 + h1 * k1 + h2 * k2 + one * k3) + bias
        second = (h1 * k0 + h2 * k1 + one * k2 + two * k3) + bias
        return silu(first), silu(second)

    bc = bc_ref[...].astype(F32)
    act1, act2 = conv(bc_hist_ref, bc_out_ref, bc[0:16], bc[16:32], bc_taps_ref[...])
    b1, c1 = act1[:, 0:256], act1[:, 256:512]
    b2, c2 = act2[:, 0:256], act2[:, 256:512]
    lane = lax.broadcasted_iota(jnp.int32, (16, 128), 1)

    def dots(a, b):
        return jnp.sum(a * b, axis=1, keepdims=True)

    pairs = jnp.where(lane == 0, dots(b1, c1), jnp.where(lane == 1, dots(b1, c2), dots(b2, c2))).T
    b1c1, b1c2, b2c2 = pairs[0:1, :], pairs[1:2, :], pairs[2:3, :]

    xz0, xz1 = xz_ref[0, 0:32, :], xz_ref[1, 0:32, :]
    par = par_ref[...]
    x = jnp.concatenate([xz0[:, 0:64], xz1[:, 0:64]], axis=1)
    z = jnp.concatenate([xz0[:, 64:128], xz1[:, 64:128]], axis=1)
    x_act1, x_act2 = conv(x_hist_ref, x_out_ref, x[0:16], x[16:32], par)
    x_act1, x_act2 = x_act1.T, x_act2.T
    gate = silu(z)
    gate1, gate2 = gate[0:16].T, gate[16:32].T
    column = lax.broadcasted_iota(jnp.int32, (64, 16), 1)

    gated = []
    for j in range(2):
        slot = 2 * group + j
        raw = xz_ref[j, 36:37, 0:32] + coef_ref[1, slot]
        step = jnp.maximum(raw, 0.0) + jnp.log1p(jnp.exp(-jnp.abs(raw)))
        rate = jnp.exp(jnp.full((1, 32), coef_ref[0, slot], F32))
        decay = jnp.exp(-step * rate)
        d1, d2 = decay[:, 0:16], decay[:, 16:32]
        half = slice(64 * j, 64 * j + 64)
        xa1, xa2 = x_act1[half], x_act2[half]
        u1, u2 = step[:, 0:16] * xa1, step[:, 16:32] * xa2
        both = d1 * d2
        v1 = d2 * u1
        q1 = jnp.zeros((64, 16), F32)
        q2 = jnp.zeros((64, 16), F32)
        for r in range(16):
            state = s_ref[r, j]
            q1 = jnp.where(column == r, dots(state, c1[r : r + 1, :]), q1)
            q2 = jnp.where(column == r, dots(state, c2[r : r + 1, :]), q2)
            s_out_ref[r, j] = (
                both[:, r : r + 1] * state
                + v1[:, r : r + 1] * b1[r : r + 1, :]
                + u2[:, r : r + 1] * b2[r : r + 1, :]
            )
        y1 = d1 * q1 + u1 * b1c1
        y2 = both * q2 + v1 * b1c2 + u2 * b2c2
        skip = coef_ref[2, slot]
        gated.append(((y1 + skip * xa1) * gate1[half], (y2 + skip * xa2) * gate2[half]))

    sums = [
        sum(jnp.sum(gated[j][i] * gated[j][i], axis=0, keepdims=True) for j in range(2))
        for i in range(2)
    ]
    total = jnp.concatenate(sums + [jnp.zeros((1, 96), F32)], axis=1)
    high = total.astype(BF16).astype(F32)
    tail = jnp.concatenate([high, total - high, jnp.zeros((6, 128), F32)], axis=0)
    for j in range(2):
        gain = par[5:6, 64 * j : 64 * j + 64]
        rows = jnp.concatenate([gated[j][0].T * gain, gated[j][1].T * gain], axis=1)
        g_ref[j] = jnp.concatenate([rows, tail], axis=0).astype(BF16)


def mixer(coef, par, xz, bc, bc_taps, x_hist, bc_hist, state):
    return pl.pallas_call(
        mixer_kernel,
        grid=(4,),
        in_specs=[
            pl.BlockSpec(memory_space=pltpu.SMEM),
            pl.BlockSpec((6, 128), lambda g: (0, g)),
            pl.BlockSpec((2, 40, 128), lambda g: (g, 0, 0)),
            pl.BlockSpec((32, 512), lambda g: (0, g)),
            pl.BlockSpec((5, 512), lambda g: (0, g)),
            pl.BlockSpec((16, 3, 128), lambda g: (0, 0, g)),
            pl.BlockSpec((16, 3, 512), lambda g: (0, 0, g)),
            pl.BlockSpec((16, 2, 64, 256), lambda g: (0, g, 0, 0)),
        ],
        out_specs=(
            pl.BlockSpec((2, 24, 128), lambda g: (g, 0, 0)),
            pl.BlockSpec((16, 2, 64, 256), lambda g: (0, g, 0, 0)),
            pl.BlockSpec((16, 3, 128), lambda g: (0, 0, g)),
            pl.BlockSpec((16, 3, 512), lambda g: (0, 0, g)),
        ),
        out_shape=(
            jax.ShapeDtypeStruct((8, 24, 128), BF16),
            jax.ShapeDtypeStruct(state.shape, F32),
            jax.ShapeDtypeStruct(x_hist.shape, F32),
            jax.ShapeDtypeStruct(bc_hist.shape, F32),
        ),
        compiler_params=pltpu.CompilerParams(vmem_limit_bytes=VMEM_BYTES),
        cost_estimate=pl.CostEstimate(flops=30_000_000, bytes_accessed=17_000_000, transcendentals=100_000),
        name="mixer",
    )(coef, par, xz, bc, bc_taps, x_hist, bc_hist, state)


def output_kernel(map_ref, g_ref, w_ref, o_ref, w_scr, l_scr):
    sums = jnp.zeros((8, 8, 128), F32)
    for s in range(16):
        w_scr[64 * s : 64 * s + 64, :] = w_ref[map_ref[s]]
    for m in range(8):
        even, odd = g_ref[2 * m].astype(F32), g_ref[2 * m + 1].astype(F32)
        sums += even[:, 16:24, :] + odd[:, 16:24, :]
        even = even[:, 0:16, :].reshape(128, 128)
        odd = odd[:, 0:16, :].reshape(128, 128)
        cols = slice(128 * m, 128 * m + 128)
        l_scr[0:128, cols] = jnp.concatenate([even[:, 0:64], odd[:, 0:64]], axis=1).astype(BF16)
        l_scr[128:256, cols] = jnp.concatenate([even[:, 64:], odd[:, 64:]], axis=1).astype(BF16)
    total = sums[:, 0, :] + sums[:, 1, :]
    scale = lax.rsqrt(total / 2048.0 + EPSILON).T
    out = jnp.dot(l_scr[...], w_scr[...], preferred_element_type=F32)
    for t in range(8):
        one = slice(16 * t, 16 * t + 16)
        two = slice(128 + 16 * t, 144 + 16 * t)
        o_ref[t, 0:16, :] = out[one] * scale[0:16, t : t + 1]
        o_ref[t, 16:32, :] = out[two] * scale[16:32, t : t + 1]


def output(head_map, gathered, w_out):
    return pl.pallas_call(
        output_kernel,
        in_specs=[
            pl.BlockSpec(memory_space=pltpu.SMEM),
            pl.BlockSpec(memory_space=pltpu.VMEM),
            pl.BlockSpec(memory_space=pltpu.VMEM),
        ],
        out_specs=pl.BlockSpec(memory_space=pltpu.VMEM),
        out_shape=jax.ShapeDtypeStruct((8, 32, 512), F32),
        scratch_shapes=[pltpu.VMEM((1024, 512), BF16), pltpu.VMEM((256, 1024), BF16)],
        compiler_params=pltpu.CompilerParams(vmem_limit_bytes=VMEM_BYTES),
        cost_estimate=pl.CostEstimate(flops=270_000_000, bytes_accessed=2_500_000, transcendentals=0),
        name="output",
    )(head_map, gathered, w_out)


def per_device(
    inputs, w_xz, w_dt, w_bc, w_out, head_map, a_log, dt_bias, skip_coef,
    conv_x, conv_bc, norm_gain, ssm_state, conv_x_state, conv_bc_state,
):
    me = lax.axis_index("fsdp")
    chosen = head_map[me]
    mine = lax.dynamic_slice_in_dim(inputs.reshape(32, 8192), me * 512, 512, axis=1)
    x = lax.all_to_all(jnp.broadcast_to(mine[None], (8, 32, 512)), "tp", 0, 0, tiled=True)
    partial = project(head_map, x.reshape(256, 512), w_xz.reshape(512, 2048), w_dt, w_bc)
    received = lax.all_to_all(partial.reshape(128, 40, 128), BOTH, 0, 0, tiled=True)
    summed = jnp.sum(received.reshape(16, 8, 40, 128), axis=0)
    low = summed[:, 32:36, :].astype(BF16).reshape(32, 128)
    low = lax.all_to_all(jnp.broadcast_to(low[None], (16, 32, 128)), "fsdp", 0, 0, tiled=True)
    bc = low.reshape(16, 8, 2, 2, 128).transpose(0, 3, 1, 2, 4).reshape(32, 2048)

    table = jnp.concatenate([conv_x, norm_gain[None]], axis=0).reshape(6, 8, 16, 64)
    par = lax.dynamic_index_in_dim(table, chosen, 2, keepdims=False).reshape(6, 512)
    coef = jnp.stack([a_log, dt_bias, skip_coef]).reshape(3, 8, 16)
    coef = lax.dynamic_index_in_dim(coef, chosen, 2, keepdims=False)
    gated, state, x_hist, bc_hist = mixer(
        coef, par, summed, bc, conv_bc, conv_x_state, conv_bc_state, ssm_state
    )
    wide = jnp.broadcast_to(gated[None], (16, 8, 24, 128)).reshape(128, 24, 128)
    gathered = lax.all_to_all(wide, BOTH, 0, 0, tiled=True).reshape(16, 8, 24, 128)
    shares = lax.all_to_all(output(head_map, gathered, w_out), "tp", 0, 0, tiled=True)
    mixed = jnp.sum(shares, axis=0).astype(BF16).reshape(2, 16, 512)
    return mixed, state, x_hist, bc_hist


def solution(mesh):
    return jax.shard_map(
        per_device,
        mesh=mesh,
        in_specs=(
            P(None, "tp", None),
            P("fsdp", "tp", None),
            P("fsdp", "tp"),
            P("fsdp", "tp"),
            P("tp", None, "fsdp"),
            P(), P(), P(), P(), P(), P(), P(),
            P("tp", "fsdp", None, None),
            P("tp", None, "fsdp"),
            P("tp", None, None),
        ),
        out_specs=(
            P(None, "tp", "fsdp"),
            P("tp", "fsdp", None, None),
            P("tp", None, "fsdp"),
            P("tp", None, None),
        ),
        check_vma=False,
    )
```

time: 715 us -> 127 us (0.18)
  waiting for transfers between devices: 256 us -> 17.2 us
  blocking collectives: 288 us -> 61.5 us
  matrix products: 55.7 us -> 0 us
  local copies, waits for them, and re-layouts: 41.4 us -> 10 us
  starting transfers between devices: 34.4 us -> 15.3 us
  Pallas kernels: 0 us -> 18.8 us
  other arithmetic: 18.4 us -> 0.95 us
  between operations: 16.8 us -> 2.78 us
    all_gather x2 -> x0, blocking collectives: 257 us -> none  [per_device(): bc_all = lax.all_gather(bc_local[:, :, None, :], 'fsdp', axis=2, tiled=True)]
    reduce_scatter x2 -> x0, waiting for transfers between devices: 127 us -> none  [per_device(): lax.psum_scatter(partial_value, 'fsdp', scatter_dimension=1, tiled=True)]
    all_to_all x4 -> x3, waiting for transfers between devices: 129 us -> 17.2 us  [the longest x1 9.5 us: per_device(): lax.all_to_all(output(head_map, gathered, w_out), 'tp', 0, 0, tiled=True)]
    all_to_all x0 -> x2, blocking collectives: none -> 61.5 us  [the longest x1 40.9 us: per_device(): lax.all_to_all(partial.reshape(128, 40, 128), BOTH, 0, 0, tiled=True)]
    dot_general x18 -> x0, matrix products: 55.7 us -> none  [the longest x2 17.7 us: per_device(): jnp.einsum('thpn,thn->thp', ssm_now, c_head, precision=HIGHEST)]
    psum x1 -> x0, blocking collectives: 30.9 us -> none  [per_device(): group_sums = lax.psum(jnp.dot(squares, onehot, precision=HIGHEST), 'fsdp')]
    all_to_all x4 -> x3, starting transfers between devices: 34.3 us -> 15.3 us  [the longest x1 7.01 us: per_device(): lax.all_to_all(jnp.broadcast_to(mine[None], (8, 32, 512)), 'tp', 0, 0, ti...]
    pallas_call x0 -> x3, Pallas kernels: none -> 18.8 us  [the longest x1 14.1 us: mixer(): pl.pallas_call(mixer_kernel, grid=(4,), in_specs=[pl.BlockSpec(memory_spa...]
  transfers between devices with their start and end apart: 6 -> 3, of which waited for: 5 -> 3; matrix products, arithmetic and copies ran while one was open for 6% -> 6% of each run, Pallas kernels for 0% -> 0%
where the time goes in v1:
time: 127 us
  blocking collectives  61.5 us (48%)
  Pallas kernels  18.8 us (15%)
  waiting for transfers between devices  17.2 us (14%)
  starting transfers between devices  15.3 us (12%)
  local copies, waits for them, and re-layouts  10 us (8%)
  between operations  2.78 us (2%)
    all_to_all x1, blocking collectives, per_device(): lax.all_to_all(partial.reshape(128, 40, 128), BOTH, 0, 0, tiled=True)  40.9 us
    all_to_all x1, blocking collectives, per_device(): lax.all_to_all(wide, BOTH, 0, 0, tiled=True).reshape(16, 8, 24, 128)  20.6 us
    pallas_call x1, Pallas kernels, mixer(): pl.pallas_call(mixer_kernel, grid=(4,), in_specs=[pl.BlockSpec(memory_spa...  14.1 us
    all_to_all x1, waiting for transfers between devices, per_device(): lax.all_to_all(output(head_map, gathered, w_out), 'tp', 0, 0, tiled=True)  9.5 us
    all_to_all x1, starting transfers between devices, per_device(): lax.all_to_all(jnp.broadcast_to(mine[None], (8, 32, 512)), 'tp', 0, 0, ti...  7.01 us
    unnamed x28, local copies, waits for them, and re-layouts  6.03 us
    all_to_all x1, waiting for transfers between devices, per_device(): lax.all_to_all(jnp.broadcast_to(mine[None], (8, 32, 512)), 'tp', 0, 0, ti...  5.74 us
    all_to_all x1, starting transfers between devices, per_device(): lax.all_to_all(jnp.broadcast_to(low[None], (16, 32, 128)), 'fsdp', 0, 0,...  4.39 us
  transfers between devices with their start and end apart: 3, of which 3 were waited for; matrix products, arithmetic and copies ran while one was open for 6% of the time, Pallas kernels for 0%

profile of v1, /device:TPU:0, one launch (start us, length us, event | category | flops | bytes accessed | tf_op | source)
XLA Modules:
  0.0 126.6 jit_solution(1018739824351267167)
XLA Ops:
  0.7 1.0 copy-done
  1.7 0.7 broadcast_in_dim.8
  2.4 7.0 %all-to-all-start = ((bf16[8,32,512]{2,1,0:T(8,128)(2,1)}), bf16[8,32,512]{2,1,0:T(8,128)(2,1)S(1)}, u32[]{:S(2)}, u32[]{:S(2)}) async-start(bf16[8,32,512]{2,1,0:T(8,128)(2,1)} %broadcast_in_dim.8), calls=%async_computation | async-start | bytes 524288 | tf_op jit(solution)/shard_map/all_to_all | solution.py:224
  9.4 0.8 copy.35.wdt_ref
  10.3 2.1 %copy.44 = bf16[64,8,16,128]{3,1,2,0:T(8,128)(2,1)S(1)} copy(bf16[64,8,16,128]{3,2,1,0:T(8,128)(2,1)} %bitcast.27) | data formatting | bytes 4194304
  12.4 5.7 %all-to-all-done = bf16[8,32,512]{2,1,0:T(8,128)(2,1)S(1)} async-done(((bf16[8,32,512]{2,1,0:T(8,128)(2,1)}), bf16[8,32,512]{2,1,0:T(8,128)(2,1)S(1)}, u32[]{:S(2)}, u32[]{:S(2)}) %all-to-all-start) | async-done | bytes 262176 | tf_op jit(solution)/shard_map/all_to_all | solution.py:224
  18.2 2.8 %project.1 = f32[16,8,40,128]{3,2,1,0:T(8,128)S(1)} custom-call(s32[16]{0:T(128)S(1)} %copy-done.4, bf16[256,512]{1,0:T(8,128)(2,1)S(1)} %bitcast.24, bf16[512,2048]{1,0:T(8,128)(2,1)S(1)} %bitcast.22, bf16[512,16]{1,0:T(8,128)(2,1)S(1)} %copy.35.wdt_ref, bf16[512,256]{1,0:T(8,128)(2,1)S(1)} %copy-done.2), custom_call_target="tpu_custom_call" | custom-call | flops 600000000 | bytes 5500000 | tf_op jit(solution)/shard_map/project/pallas_call | solution.py:50
  21.0 40.9 %all_to_all.25 = f32[128,40,128]{2,1,0:T(8,128)S(1)} all-to-all(f32[128,40,128]{2,1,0:T(8,128)S(1)} %bitcast.21), channel_id=1, replica_groups=mesh['fsdp'=16,'tp'=8] {'fsdp','tp'}, dimensions={0} | all-to-all | bytes 5242880 | tf_op jit(solution)/shard_map/all_to_all | solution.py:226
  61.9 0.1 reduce_sum.18.xz_ref
  62.1 0.7 broadcast_in_dim.10
  62.8 4.4 %all-to-all-start.2 = ((bf16[16,32,128]{2,1,0:T(8,128)(2,1)}), bf16[16,32,128]{2,1,0:T(8,128)(2,1)S(1)}, u32[]{:S(2)}, u32[]{:S(2)}) async-start(bf16[16,32,128]{2,1,0:T(8,128)(2,1)} %broadcast_in_dim.10), calls=%async_computation.2 | async-start | bytes 262144 | tf_op jit(solution)/shard_map/all_to_all | solution.py:229
  67.2 0.6 dynamic_slice.14
  69.1 0.1 stack.12
  69.1 0.1 stack.13
  69.2 0.1 stack.14
  69.3 0.1 concatenate.10
  69.5 1.1 concatenate.9
  70.6 0.1 copy.33
  71.4 0.3 copy.39.bc_hist_ref
  71.7 0.2 fusion.1.coef_ref
  71.9 2.0 %all-to-all-done.2 = bf16[16,32,128]{2,1,0:T(8,128)(2,1)S(1)} async-done(((bf16[16,32,128]{2,1,0:T(8,128)(2,1)}), bf16[16,32,128]{2,1,0:T(8,128)(2,1)S(1)}, u32[]{:S(2)}, u32[]{:S(2)}) %all-to-all-start.2) | async-done | bytes 131104 | tf_op jit(solution)/shard_map/all_to_all | solution.py:229
  73.9 0.1 copy.37
  74.0 0.1 reshape.63.bc_ref
  74.1 14.1 %mixer.1 = (bf16[8,24,128]{2,1,0:T(8,128)(2,1)S(1)}, f32[16,8,64,256]{3,2,1,0:T(8,128)}, f32[16,3,512]{2,1,0:T(4,128)S(1)}, f32[16,3,2048]{2,1,0:T(4,128)S(1)}) custom-call(f32[3,8]{1,0:T(4,128)S(1)} %fusion.1.coef_ref, f32[6,512]{1,0:T(8,128)S(1)} %reshape.56.par_ref, f32[8,40,128]{2,1,0:T(8,128)S(1)} %reduce_sum.18.xz_ref, ...), custom_call_target="tpu_custom_call" | custom-call | flops 30000000 | bytes 17000000 | tf_op jit(solution)/shard_map/mixer/pallas_call | solution.py:147
  88.3 0.1 broadcast_in_dim.11
  88.4 20.6 %all_to_all.26 = bf16[128,24,128]{2,1,0:T(8,128)(2,1)S(1)} all-to-all(bf16[128,24,128]{2,1,0:T(8,128)(2,1)S(1)} %bitcast.26), channel_id=1, replica_groups=mesh['fsdp'=16,'tp'=8] {'fsdp','tp'}, dimensions={0} | all-to-all | bytes 1572864 | tf_op jit(solution)/shard_map/all_to_all | solution.py:240
  109.0 1.9 %output.1 = f32[8,32,512]{2,1,0:T(8,128)} custom-call(s32[16]{0:T(128)S(1)} %copy-done.4, bf16[16,8,24,128]{3,2,1,0:T(8,128)(2,1)S(1)} %bitcast.23, bf16[16,64,512]{2,1,0:T(8,128)(2,1)S(1)} %copy-done.1), custom_call_target="tpu_custom_call" | custom-call | flops 270000000 | bytes 2500000 | tf_op jit(solution)/shard_map/output/pallas_call | solution.py:201
  110.9 3.9 %all-to-all-start.4 = ((f32[8,32,512]{2,1,0:T(8,128)}), f32[8,32,512]{2,1,0:T(8,128)S(1)}, u32[]{:S(2)}, u32[]{:S(2)}) async-start(f32[8,32,512]{2,1,0:T(8,128)} %output.1), calls=%async_computation.4 | async-start | bytes 1048576 | tf_op jit(solution)/shard_map/all_to_all | solution.py:241
  114.8 0.7 copy.40
  115.5 1.0 copy.41
  116.5 9.5 %all-to-all-done.4 = f32[8,32,512]{2,1,0:T(8,128)S(1)} async-done(((f32[8,32,512]{2,1,0:T(8,128)}), f32[8,32,512]{2,1,0:T(8,128)S(1)}, u32[]{:S(2)}, u32[]{:S(2)}) %all-to-all-start.4) | async-done | bytes 524320 | tf_op jit(solution)/shard_map/all_to_all | solution.py:241
  126.0 0.7 reduce_sum.19
  (28 shorter events, 0.3 us)
Async XLA Ops:
  0.6 1.0 copy-start
  0.7 17.5 %copy-start.2 = (bf16[512,256]{1,0:T(8,128)(2,1)S(1)}, bf16[512,256]{1,0:T(8,128)(2,1)}, u32[]{:S(2)}) copy-start(bf16[512,256]{1,0:T(8,128)(2,1)} %wbc_ref.1) | copy-start | bytes 786436
  0.7 17.5 %copy-start.4 = (s32[16]{0:T(128)S(1)}, s32[16]{0:T(128)}, u32[]{:S(2)}) copy-start(s32[16]{0:T(128)} %map_ref.3) | copy-start | bytes 196
  2.4 15.7 %all-to-all-start = ((bf16[8,32,512]{2,1,0:T(8,128)(2,1)}), bf16[8,32,512]{2,1,0:T(8,128)(2,1)S(1)}, u32[]{:S(2)}, u32[]{:S(2)}) async-start(bf16[8,32,512]{2,1,0:T(8,128)(2,1)} %broadcast_in_dim.8), calls=%async_computation | async-start | bytes 524288 | tf_op jit(solution)/shard_map/all_to_all | solution.py:224
  61.9 7.2 %copy-start.8 = (f32[128]{0:T(128)S(1)}, f32[128]{0:T(128)}, u32[]{:S(2)}) copy-start(f32[128]{0:T(128)} %param.21) | copy-start | bytes 1540
  61.9 7.2 %copy-start.9 = (f32[128]{0:T(128)S(1)}, f32[128]{0:T(128)}, u32[]{:S(2)}) copy-start(f32[128]{0:T(128)} %param.22) | copy-start | bytes 1540
  61.9 7.3 %copy-start.10 = (f32[128]{0:T(128)S(1)}, f32[128]{0:T(128)}, u32[]{:S(2)}) copy-start(f32[128]{0:T(128)} %param.23) | copy-start | bytes 1540
  61.9 7.4 %copy-start.7 = (f32[8192]{0:T(1024)S(1)}, f32[8192]{0:T(1024)}, u32[]{:S(2)}) copy-start(f32[8192]{0:T(1024)} %param.26) | copy-start | bytes 98308
  61.9 7.5 %copy-start.6 = (f32[16,3,512]{2,0,1:T(8,128)S(1)}, f32[16,3,512]{2,0,1:T(8,128)}, u32[]{:S(2)}) copy-start(f32[16,3,512]{2,0,1:T(8,128)} %param.28) | copy-start | bytes 294916
  62.1 9.4 %copy-start.5 = (f32[16,3,2048]{2,0,1:T(8,128)S(1)}, f32[16,3,2048]{2,0,1:T(8,128)}, u32[]{:S(2)}) copy-start(f32[16,3,2048]{2,0,1:T(8,128)} %param.29) | copy-start | bytes 1179652
  62.1 12.0 %copy-start.3 = (f32[5,2048]{1,0:T(8,128)S(1)}, f32[5,2048]{1,0:T(8,128)}, u32[]{:S(2)}) copy-start(f32[5,2048]{1,0:T(8,128)} %bc_taps_ref.1) | copy-start | bytes 122884
  62.8 11.1 %all-to-all-start.2 = ((bf16[16,32,128]{2,1,0:T(8,128)(2,1)}), bf16[16,32,128]{2,1,0:T(8,128)(2,1)S(1)}, u32[]{:S(2)}, u32[]{:S(2)}) async-start(bf16[16,32,128]{2,1,0:T(8,128)(2,1)} %broadcast_in_dim.10), calls=%async_computation.2 | async-start | bytes 262144 | tf_op jit(solution)/shard_map/all_to_all | solution.py:229
  88.2 20.7 %copy-start.1 = (bf16[16,64,512]{2,1,0:T(8,128)(2,1)S(1)}, bf16[16,64,512]{2,1,0:T(8,128)(2,1)}, u32[]{:S(2)}) copy-start(bf16[16,64,512]{2,1,0:T(8,128)(2,1)} %w_ref.1) | copy-start | bytes 3145732
  110.9 15.1 %all-to-all-start.4 = ((f32[8,32,512]{2,1,0:T(8,128)}), f32[8,32,512]{2,1,0:T(8,128)S(1)}, u32[]{:S(2)}, u32[]{:S(2)}) async-start(f32[8,32,512]{2,1,0:T(8,128)} %output.1), calls=%async_computation.4 | async-start | bytes 1048576 | tf_op jit(solution)/shard_map/all_to_all | solution.py:241

commit v2 on v1

v2 whole, which is shorter than its diff:
```python
import functools

import jax
import jax.numpy as jnp
from jax import lax
from jax.experimental import pallas as pl
from jax.experimental.pallas import tpu as pltpu
from jax.sharding import Mesh
from jax.sharding import PartitionSpec as P

EPSILON = 1e-05
F32 = jnp.float32
BF16 = jnp.bfloat16
MIB = 2**20
STATE_MIB = 56
PART = 4


def silu(v):
    return v * jax.nn.sigmoid(v)


def project_kernel(map_ref, pos_ref, x_ref, w_ref, w2_ref, wbd_ref, wbd2_ref, o_ref, dt_scr):
    core = pos_ref[1]
    x1 = x_ref[:, pl.ds(pl.multiple_of(core * 512, 512), 512)]
    x2 = x_ref[:, pl.ds(pl.multiple_of((1 - core) * 512, 512), 512)]

    def dot(w1, w2):
        return jnp.dot(x1, w1, preferred_element_type=F32) + jnp.dot(
            x2, w2, preferred_element_type=F32
        )

    def split(v):
        high = v.astype(BF16).astype(F32)
        return high, v - high

    y = dot(wbd_ref[...], wbd2_ref[...])
    dt_scr[...] = y[:, 256:384].T
    bc_high, bc_low = split(y[:, 0:256])
    none = jnp.zeros((7, 128), F32)
    for i in range(0, 8, 2):
        heads = [map_ref[2 * k + core] for k in (i, i + 1)]
        cols = [pl.ds(pl.multiple_of(head * 128, 128), 128) for head in heads]
        both = dot(
            jnp.concatenate([w_ref[:, c] for c in cols], axis=1),
            jnp.concatenate([w2_ref[:, c] for c in cols], axis=1),
        ).astype(BF16)
        for k in range(2):
            dt_high, dt_low = split(dt_scr[pl.ds(heads[k], 1), :])
            for t in range(8):
                o_ref[i + k, t, 0:32, :] = both[32 * t : 32 * t + 32, 128 * k : 128 * k + 128]
                at = 32 * t + 2 * (i + k)
                high, low = (
                    jnp.concatenate(
                        [
                            jnp.where(core == 0, v[b : b + 1], v[b + 1 : b + 2])
                            for b in (at, at + 16)
                        ],
                        axis=0,
                    )
                    for v in (bc_high, bc_low)
                )
                lanes = slice(32 * t, 32 * t + 32)
                dt = jnp.concatenate([dt_high[:, lanes], dt_low[:, lanes], none[0:1, 0:64]], axis=1)
                o_ref[i + k, t, 32:48, :] = jnp.concatenate(
                    [high[:, 0:128], high[:, 128:256], low[:, 0:128], low[:, 128:256], dt, none],
                    axis=0,
                ).astype(BF16)


HBM = pl.BlockSpec(memory_space=pltpu.HBM)
SMEM = pl.BlockSpec(memory_space=pltpu.SMEM)
VMEM = pl.BlockSpec(memory_space=pltpu.VMEM)


def project(head_map, pos, x, w, w2, wbd, wbd2):
    return pl.pallas_call(
        project_kernel,
        in_specs=[SMEM] * 2 + [VMEM] * 5,
        out_specs=VMEM,
        out_shape=jax.ShapeDtypeStruct((8, 8, 48, 128), BF16),
        scratch_shapes=[pltpu.VMEM((128, 256), F32)],
        compiler_params=pltpu.CompilerParams(vmem_limit_bytes=16 * MIB),
        cost_estimate=pl.CostEstimate(flops=600_000_000, bytes_accessed=5_500_000, transcendentals=0),
        name="project",
    )(head_map, pos, x, w, w2, wbd, wbd2)


def conv(hist_ref, one, two, taps):
    h0, h1, h2 = hist_ref[0], hist_ref[1], hist_ref[2]
    k0, k1, k2, k3, bias = (taps[i : i + 1, :] for i in range(5))
    first = (h0 * k0 + h1 * k1 + h2 * k2 + one * k3) + bias
    second = (h1 * k0 + h2 * k1 + one * k2 + two * k3) + bias
    return silu(first), silu(second)


DECAY, FIRST, SECOND, SKIP, GATE = range(0, 160, 32)


def heads_kernel(
    map_ref, pos_ref, a_ref, bias_ref, skip_ref, taps_ref, gain_ref, xz_ref, x_hist_ref,
    col_ref, x_out_ref, gain_out_ref,
):
    head = map_ref[2 * pos_ref[0] + pos_ref[1]]

    def local(ref):
        parts = []
        for j in range(8):
            block = ref[:, pl.ds(pl.multiple_of(1024 * j + 128 * (head // 2), 128), 128)]
            parts.append(jnp.where(head % 2 == 0, block[:, 0:64], block[:, 64:128]))
        return jnp.concatenate(parts, axis=1)

    def scalars(ref):
        return jnp.concatenate([jnp.full((1, 32), ref[head + 16 * j], F32) for j in range(8)], axis=0)

    gain_out_ref[...] = local(gain_ref)
    rows = [xz_ref[j, 0:32, :] for j in range(8)]
    x = jnp.concatenate([v[:, 0:64] for v in rows], axis=1)
    z = jnp.concatenate([v[:, 64:128] for v in rows], axis=1)
    x_out_ref[0] = x_hist_ref[2]
    x_out_ref[1] = x[0:16]
    x_out_ref[2] = x[16:32]
    x_act = jnp.concatenate(conv(x_hist_ref, x[0:16], x[16:32], local(taps_ref)), axis=0)
    both = jnp.concatenate([x_act, silu(z)], axis=0).T
    raw = jnp.concatenate([xz_ref[j, 40:41, 0:32] + xz_ref[j, 40:41, 32:64] for j in range(8)], axis=0)
    raw = raw + scalars(bias_ref)
    step = jnp.maximum(raw, 0.0) + jnp.log1p(jnp.exp(-jnp.abs(raw)))
    decay = jnp.exp(-step * jnp.exp(scalars(a_ref)))
    ones = jnp.ones((8, 16), F32)
    since = decay * jnp.concatenate([ones, decay[:, 0:16]], axis=1)
    for j in range(8):
        act = both[64 * j : 64 * j + 64, 0:32]
        u = step[j : j + 1, :] * act
        u1, u2 = u[:, 0:16], u[:, 16:32]
        col_ref[j] = jnp.concatenate(
            [
                jnp.broadcast_to(since[j : j + 1, :], (64, 32)),
                u1, decay[j : j + 1, 16:32] * u1,
                jnp.zeros((64, 16), F32), u2,
                skip_ref[head + 16 * j] * act,
                both[64 * j : 64 * j + 64, 32:64],
                jnp.zeros((64, 96), F32),
            ],
            axis=1,
        )


def heads_part(head_map, pos, a_log, dt_bias, skip_coef, conv_x, norm_gain, xz, x_hist):
    return pl.pallas_call(
        heads_kernel,
        in_specs=[SMEM] * 5 + [VMEM] * 4,
        out_specs=(VMEM,) * 3,
        out_shape=(
            jax.ShapeDtypeStruct((8, 64, 256), F32),
            jax.ShapeDtypeStruct(x_hist.shape, F32),
            jax.ShapeDtypeStruct((1, 512), F32),
        ),
        compiler_params=pltpu.CompilerParams(vmem_limit_bytes=16 * MIB),
        cost_estimate=pl.CostEstimate(flops=2_000_000, bytes_accessed=1_000_000, transcendentals=50_000),
        name="heads_part",
    )(head_map, pos, a_log, dt_bias, skip_coef, conv_x, norm_gain[None], xz, x_hist)


def mixer_kernel(
    gain_ref, col_ref, bc_ref, bc_taps_ref, bc_hist_ref, state_ref, g_ref, b_ref, s_ref, sem,
):
    copies = [
        pltpu.make_async_copy(
            state_ref.at[pl.ds(PART * k, PART), pl.ds(2 * g, 2)],
            s_ref.at[g, pl.ds(PART * k, PART)],
            sem.at[g, k],
        )
        for g in range(4)
        for k in range(16 // PART)
    ]
    for copy in copies:
        copy.start()
    bc = jnp.transpose(bc_ref[...].astype(F32), (1, 0, 2))
    one, two = (
        jnp.concatenate([bc[2 * k + step] for k in range(16)], axis=1) for step in range(2)
    )
    act1, act2 = conv(bc_hist_ref, one, two, bc_taps_ref[...])
    lane = lax.broadcasted_iota(jnp.int32, (32, 128), 1)
    column = lax.broadcasted_iota(jnp.int32, (64, 32), 1)

    def dots(a, b):
        return jnp.sum(a * b, axis=1, keepdims=True)

    for g in range(4):
        at = 512 * g
        b1, c1 = act1[:, at : at + 256], act1[:, at + 256 : at + 512]
        b2, c2 = act2[:, at : at + 256], act2[:, at + 256 : at + 512]
        b_ref[g, 0:16, :] = b1
        b_ref[g, 16:32, :] = b2
        with_first = jnp.concatenate([dots(b1, c1), dots(b1, c2)], axis=0)
        with_second = jnp.concatenate([jnp.zeros((16, 1), F32), dots(b2, c2)], axis=0)
        pairs = jnp.where(lane == 0, with_first, with_second).T
        gated = []
        for copy in copies[g * 16 // PART : (g + 1) * 16 // PART]:
            copy.wait()
        for j in (2 * g, 2 * g + 1):
            decay, first, second, skip, gate = (
                col_ref[j, :, k : k + 32] for k in (DECAY, FIRST, SECOND, SKIP, GATE)
            )
            q = jnp.zeros((64, 32), F32)
            for r in range(16):
                state = s_ref[g, r, j - 2 * g]
                q = jnp.where(column == r, dots(state, c1[r : r + 1, :]), q)
                q = jnp.where(column == r + 16, dots(state, c2[r : r + 1, :]), q)
            y = decay * q + first * pairs[0:1, :] + second * pairs[1:2, :]
            gated.append((y + skip) * gate)
        total = sum(jnp.sum(v * v, axis=0, keepdims=True) for v in gated)
        total = jnp.concatenate([total, jnp.zeros((1, 96), F32)], axis=1)
        high = total.astype(BF16).astype(F32)
        tail = jnp.concatenate([high, total - high, jnp.zeros((6, 128), F32)], axis=0)
        rows = jnp.concatenate(gated, axis=0).T * gain_ref[0:1, 128 * g : 128 * g + 128]
        for j in range(2):
            lanes = slice(64 * j, 64 * j + 64)
            block = jnp.concatenate(
                [jnp.concatenate([rows[0:16, lanes], rows[16:32, lanes]], axis=1), tail], axis=0
            ).astype(BF16)
            for chip in range(8):
                g_ref[chip, 2 * g + j] = block


def mixer(gain, cols, bc, bc_taps, bc_hist, state):
    return pl.pallas_call(
        mixer_kernel,
        in_specs=[VMEM] * 5 + [HBM],
        out_specs=(VMEM,) * 2,
        out_shape=(
            jax.ShapeDtypeStruct((8, 8, 24, 128), BF16),
            jax.ShapeDtypeStruct((4, 32, 256), F32),
        ),
        scratch_shapes=[pltpu.VMEM((4, 16, 2, 64, 256), F32), pltpu.SemaphoreType.DMA((4, 16 // PART))],
        compiler_params=pltpu.CompilerParams(vmem_limit_bytes=STATE_MIB * MIB),
        cost_estimate=pl.CostEstimate(flops=20_000_000, bytes_accessed=9_000_000, transcendentals=100_000),
        name="mixer",
    )(gain, cols, bc, bc_taps, bc_hist, state)


def advance_kernel(start, col_ref, b_ref, state_ref, *refs):
    def body(col_ref, b_ref, s_ref, out_ref):
        for j in range(2):
            cols = col_ref[j]
            for r in range(16):
                k = 16 + r
                out_ref[r, j] = (
                    cols[0:1, DECAY + k : DECAY + k + 1] * s_ref[r, j]
                    + cols[:, FIRST + k : FIRST + k + 1] * b_ref[r : r + 1, :]
                    + cols[:, SECOND + k : SECOND + k + 1] * b_ref[k : k + 1, :]
                )

    pltpu.emit_pipeline(
        body,
        grid=(2,),
        in_specs=[
            pl.BlockSpec((2, 64, 256), lambda g: (g + start, 0, 0)),
            pl.BlockSpec((None, 32, 256), lambda g: (g + start, 0, 0)),
            pl.BlockSpec((16, 2, 64, 256), lambda g: (0, g + start, 0, 0)),
        ],
        out_specs=[pl.BlockSpec((16, 2, 64, 256), lambda g: (0, g + start, 0, 0))],
    )(col_ref, b_ref, state_ref, refs[-1])


def advance(cols, b, state, start, into):
    more = [] if into is None else [into]
    return pl.pallas_call(
        functools.partial(advance_kernel, start),
        in_specs=[pl.BlockSpec(memory_space=pl.ANY)] * 2 + [HBM] * (1 + len(more)),
        out_specs=HBM,
        out_shape=jax.ShapeDtypeStruct(state.shape, F32),
        input_output_aliases={3: 0} if more else {},
        compiler_params=pltpu.CompilerParams(vmem_limit_bytes=STATE_MIB * MIB),
        cost_estimate=pl.CostEstimate(flops=6_000_000, bytes_accessed=8_500_000, transcendentals=0),
        name="advance",
    )(cols, b, state, *more)


def output_kernel(map_ref, pos_ref, g1_ref, g2_ref, w_ref, o_ref, w_scr, l_scr):
    sums = jnp.zeros((8, 8, 128), F32)
    core = pos_ref[1]
    for s in range(16):
        which = core if s % 2 == 0 else 1 - core
        w_scr[64 * s : 64 * s + 64, :] = w_ref[map_ref[s // 2 * 2 + which]]
    for m in range(8):
        even, odd = g1_ref[m].astype(F32), g2_ref[m].astype(F32)
        sums += even[:, 16:24, :] + odd[:, 16:24, :]
        even = even[:, 0:16, :].reshape(128, 128)
        odd = odd[:, 0:16, :].reshape(128, 128)
        cols = slice(128 * m, 128 * m + 128)
        l_scr[0:128, cols] = jnp.concatenate([even[:, 0:64], odd[:, 0:64]], axis=1).astype(BF16)
        l_scr[128:256, cols] = jnp.concatenate([even[:, 64:], odd[:, 64:]], axis=1).astype(BF16)
    total = sums[:, 0, :] + sums[:, 1, :]
    scale = lax.rsqrt(total / 2048.0 + EPSILON).T
    out = jnp.dot(l_scr[...], w_scr[...], preferred_element_type=F32)
    for t in range(8):
        one = slice(16 * t, 16 * t + 16)
        two = slice(128 + 16 * t, 144 + 16 * t)
        o_ref[t, 0:16, :] = (out[one] * scale[0:16, t : t + 1]).astype(BF16)
        o_ref[t, 16:32, :] = (out[two] * scale[16:32, t : t + 1]).astype(BF16)


def output(head_map, pos, gathered, other, w_out):
    return pl.pallas_call(
        output_kernel,
        in_specs=[SMEM] * 2 + [VMEM] * 3,
        out_specs=VMEM,
        out_shape=jax.ShapeDtypeStruct((8, 32, 512), BF16),
        scratch_shapes=[pltpu.VMEM((1024, 512), BF16), pltpu.VMEM((256, 1024), BF16)],
        compiler_params=pltpu.CompilerParams(vmem_limit_bytes=16 * MIB),
        cost_estimate=pl.CostEstimate(flops=270_000_000, bytes_accessed=2_500_000, transcendentals=0),
        name="output",
    )(head_map, pos, gathered, other, w_out)


def per_device(
    inputs, w_xz, w_dt, w_bc, w_out, head_map, a_log, dt_bias, skip_coef,
    conv_x, conv_bc, norm_gain, ssm_state, conv_x_state, conv_bc_state,
):
    chip, core = lax.axis_index("chip"), lax.axis_index("core")
    pos = jnp.stack([chip, core]).astype(jnp.int32)

    def swap(v):
        return lax.ppermute(v, "core", [(0, 1), (1, 0)])

    w = w_xz.reshape(512, 2048)
    wbd = jnp.concatenate([w_bc, w_dt, jnp.zeros((512, 112), BF16)], axis=1)
    w2, wbd2 = swap(w_xz).reshape(512, 2048), swap(wbd)
    x = lax.dynamic_slice_in_dim(inputs.reshape(32, 8192), chip * 1024, 1024, axis=1)
    x = lax.all_to_all(jnp.broadcast_to(x[None], (8, 32, 1024)), "tp", 0, 0, tiled=True)
    partial = project(head_map, pos, x.reshape(256, 1024), w, w2, wbd, wbd2)
    received = lax.all_to_all(partial.reshape(64, 48, 128), ("chip", "tp"), 0, 0, tiled=True)
    summed = jnp.sum(received.reshape(8, 8, 48, 128).astype(F32), axis=0)
    cols, x_hist, gain = heads_part(
        head_map, pos, a_log, dt_bias, skip_coef, conv_x, norm_gain, summed,
        conv_x_state.transpose(1, 0, 2),
    )
    low = (summed[:, 32:36, :] + summed[:, 36:40, :]).astype(BF16).reshape(32, 128)
    low = lax.all_to_all(
        jnp.broadcast_to(low[None], (16, 32, 128)), ("chip", "core"), 0, 0, tiled=True
    )

    gated, b = mixer(gain, cols, low, conv_bc, conv_bc_state.transpose(1, 0, 2), ssm_state)
    gathered = lax.all_to_all(gated.reshape(64, 24, 128), ("chip", "tp"), 0, 0, tiled=True).reshape(8, 8, 24, 128)
    fresh = low.reshape(16, 8, 2, 2, 128).transpose(3, 0, 1, 2, 4).reshape(2, 16, 2048)
    bc_hist = jnp.concatenate([conv_bc_state.transpose(1, 0, 2)[2:], fresh.astype(F32)], axis=0)
    state = advance(cols, b, ssm_state, 0, None)
    gathered, state = lax.optimization_barrier((gathered, state))
    state = advance(cols, b, ssm_state, 2, state)
    shares = output(head_map, pos, gathered, swap(gathered), w_out)
    shares = lax.all_to_all(shares, "tp", 0, 0, tiled=True)
    mixed = jnp.sum(shares.astype(F32), axis=0).astype(BF16).reshape(2, 16, 512)
    return mixed, state, x_hist.transpose(1, 0, 2), bc_hist.transpose(1, 0, 2)


def solution(mesh):
    pairs = Mesh(mesh.devices.reshape(8, 2, 8), ("chip", "core", "tp"))
    fsdp = ("chip", "core")
    return jax.shard_map(
        per_device,
        mesh=pairs,
        in_specs=(
            P(None, "tp", None),
            P(fsdp, "tp", None),
            P(fsdp, "tp"),
            P(fsdp, "tp"),
            P("tp", None, fsdp),
            P(), P(), P(), P(), P(), P(), P(),
            P("tp", fsdp, None, None),
            P("tp", None, fsdp),
            P("tp", None, None),
        ),
        out_specs=(
            P(None, "tp", fsdp),
            P("tp", fsdp, None, None),
            P("tp", None, fsdp),
            P("tp", None, None),
        ),
        check_vma=False,
    )
```

time: 127 us -> 102 us (0.80)
  blocking collectives: 61.5 us -> 23.5 us
  Pallas kernels: 18.8 us -> 23.5 us
  starting transfers between devices: 15.3 us -> 19.5 us
  local copies, waits for them, and re-layouts: 10 us -> 13.9 us
  between operations: 2.78 us -> 0.89 us
  waiting for transfers between devices: 17.2 us -> 18.5 us
    all_to_all x2 -> x1, blocking collectives: 61.5 us -> 23.5 us  [per_device(): lax.all_to_all(partial.reshape(64, 48, 128), ('chip', 'tp'), 0, 0, tiled=...]
    unnamed x28 -> x33, local copies, waits for them, and re-layouts: 6.03 us -> 11 us
    pallas_call x3 -> x6, Pallas kernels: 18.8 us -> 23.5 us  [the longest x2 9.55 us: advance(): pl.pallas_call(functools.partial(advance_kernel, start), in_specs=[pl.Blo...]
    all_to_all x3 -> x4, starting transfers between devices: 15.3 us -> 19.3 us  [the longest x1 7.01 us: per_device(): lax.all_to_all(jnp.broadcast_to(x[None], (8, 32, 1024)), 'tp', 0, 0, tile...]
    all_to_all x3 -> x4, waiting for transfers between devices: 17.2 us -> 18.1 us  [the longest x1 7.17 us: per_device(): lax.all_to_all(gated.reshape(64, 24, 128), ('chip', 'tp'), 0, 0, tiled=True)]
  transfers between devices with their start and end apart: 3 -> 7, of which waited for: 3 -> 5; matrix products, arithmetic and copies ran while one was open for 6% -> 9% of each run, Pallas kernels for 0% -> 12%
where the time goes in v2:
time: 102 us; the launch traced here: 101 us
  Pallas kernels  23.5 us (23%)
  blocking collectives  23.5 us (23%)
  starting transfers between devices  19.5 us (19%)
  waiting for transfers between devices  18.5 us (18%)
  local copies, waits for them, and re-layouts  13.9 us (14%)
  other arithmetic  1.72 us (2%)
    all_to_all x1, blocking collectives, per_device(): lax.all_to_all(partial.reshape(64, 48, 128), ('chip', 'tp'), 0, 0, tiled=...  23.5 us
    unnamed x33, local copies, waits for them, and re-layouts  11 us
    pallas_call x2, Pallas kernels, advance(): pl.pallas_call(functools.partial(advance_kernel, start), in_specs=[pl.Blo...  9.55 us
    pallas_call x1, Pallas kernels, mixer(): pl.pallas_call(mixer_kernel, in_specs=[VMEM] * 5 + [HBM], out_specs=(VMEM...  7.66 us
    all_to_all x1, waiting for transfers between devices, per_device(): lax.all_to_all(gated.reshape(64, 24, 128), ('chip', 'tp'), 0, 0, tiled=True)  7.17 us
    all_to_all x1, starting transfers between devices, per_device(): lax.all_to_all(jnp.broadcast_to(x[None], (8, 32, 1024)), 'tp', 0, 0, tile...  7.01 us
    all_to_all x1, starting transfers between devices, per_device(): lax.all_to_all(gated.reshape(64, 24, 128), ('chip', 'tp'), 0, 0, tiled=True)  5.29 us
    all_to_all x1, waiting for transfers between devices, per_device(): lax.all_to_all(jnp.broadcast_to(x[None], (8, 32, 1024)), 'tp', 0, 0, tile...  4.25 us
  transfers between devices with their start and end apart: 7, of which 5 were waited for; matrix products, arithmetic and copies ran while one was open for 9% of the time, Pallas kernels for 12%

profile of v2, /device:TPU:0, one launch (start us, length us, event | category | flops | bytes accessed | tf_op | source)
XLA Modules:
  0.0 101.4 jit_solution(3898642966302490066)
XLA Ops:
  0.8 0.9 copy-done
  1.7 0.8 broadcast_in_dim.20
  2.5 7.0 %all-to-all-start = ((bf16[8,32,1024]{2,1,0:T(8,128)(2,1)}), bf16[8,32,1024]{2,1,0:T(8,128)(2,1)S(1)}, u32[]{:S(2)}, u32[]{:S(2)}) async-start(bf16[8,32,1024]{2,1,0:T(8,128)(2,1)} %broadcast_in_dim.20), calls=%async_computation | async-start | bytes 1048576 | tf_op jit(solution)/shard_map/all_to_all | solution.py:331
  9.5 0.8 copy.20
  10.7 2.1 %copy.27 = bf16[64,8,16,128]{3,1,2,0:T(8,128)(2,1)S(1)} copy(bf16[64,8,16,128]{3,2,1,0:T(8,128)(2,1)} %bitcast.41) | data formatting | bytes 4194304
  12.9 3.5 %copy.26 = bf16[64,8,16,128]{3,1,2,0:T(8,128)(2,1)} copy(bf16[64,8,16,128]{3,2,1,0:T(8,128)(2,1)} %bitcast.21) | data formatting | bytes 4194304
  16.4 4.3 %all-to-all-done = bf16[8,32,1024]{2,1,0:T(8,128)(2,1)S(1)} async-done(((bf16[8,32,1024]{2,1,0:T(8,128)(2,1)}), bf16[8,32,1024]{2,1,0:T(8,128)(2,1)S(1)}, u32[]{:S(2)}, u32[]{:S(2)}) %all-to-all-start) | async-done | bytes 524320 | tf_op jit(solution)/shard_map/all_to_all | solution.py:331
  20.6 1.6 %copy-done.1 = bf16[64,8,16,128]{3,1,2,0:T(8,128)(2,1)S(1)} copy-done((bf16[64,8,16,128]{3,1,2,0:T(8,128)(2,1)S(1)}, bf16[64,8,16,128]{3,1,2,0:T(8,128)(2,1)}, u32[]{:S(2)}) %copy-start.1) | copy-done | bytes 2097176
  22.2 2.3 %project.1 = bf16[8,8,48,128]{3,2,1,0:T(8,128)(2,1)S(1)} custom-call(s32[16]{0:T(128)S(1)} %copy-done.7, s32[2]{0:T(128)S(1)} %pad_add_fusion.pos_ref, bf16[256,1024]{1,0:T(8,128)(2,1)S(1)} %bitcast.35, bf16[512,2048]{1,0:T(8,128)(2,1)S(1)} %bitcast.32, bf16[512,2048]{1,0:T(8,128)(2,1)S(1)} %bitcast.33, bf16[512,384]{1,0:T(8,128)(2,1)S(1)} %maximum_maximum_fusion.wbd_ref, ...), custom_call_target="tpu_custom_call" | custom-call | flops 600000000 | bytes 5500000 | tf_op jit(solution)/shard_map/project/pallas_call | solution.py:77
  24.6 23.5 %all_to_all.25 = bf16[64,48,128]{2,1,0:T(8,128)(2,1)S(1)} all-to-all(bf16[64,48,128]{2,1,0:T(8,128)(2,1)S(1)} %bitcast.34), channel_id=1, replica_groups=mesh['chip'=8,'core'=2,'tp'=8] {'chip','tp'}, dimensions={0} | all-to-all | bytes 1572864 | tf_op jit(solution)/shard_map/all_to_all | solution.py:333
  48.0 0.1 convert_reduce_fusion.xz_ref
  48.2 0.7 broadcast_in_dim.23
  48.8 3.5 %all-to-all-start.2 = ((bf16[16,32,128]{2,1,0:T(8,128)(2,1)}), bf16[16,32,128]{2,1,0:T(8,128)(2,1)S(1)}, u32[]{:S(2)}, u32[]{:S(2)}) async-start(bf16[16,32,128]{2,1,0:T(8,128)(2,1)} %broadcast_in_dim.23), calls=%async_computation.2 | async-start | bytes 262144 | tf_op jit(solution)/shard_map/all_to_all | solution.py:340
  52.4 2.2 %heads_part.1 = (f32[8,64,256]{2,1,0:T(8,128)S(1)}, f32[3,16,512]{2,1,0:T(8,128)}, f32[1,512]{1,0:T(1,128)S(1)}) custom-call(s32[16]{0:T(128)S(1)} %copy-done.7, s32[2]{0:T(128)S(1)} %pad_add_fusion.pos_ref, f32[128]{0:T(128)S(1)} %copy-done.9, f32[128]{0:T(128)S(1)} %copy-done.10, f32[128]{0:T(128)S(1)} %copy-done.11, f32[5,8192]{1,0:T(8,128)S(1)} %copy-done.4, ...), custom_call_target="tpu_custom_call" | custom-call | flops 2000000 | bytes 1000000 | tf_op jit(solution)/shard_map/heads_part/pallas_call | solution.py:149
  54.6 0.8 copy-done.2
  55.4 0.6 copy-done.8
  56.0 3.0 %all-to-all-done.2.bc_ref = bf16[16,32,128]{2,1,0:T(8,128)(2,1)S(1)} async-done(((bf16[16,32,128]{2,1,0:T(8,128)(2,1)}), bf16[16,32,128]{2,1,0:T(8,128)(2,1)S(1)}, u32[]{:S(2)}, u32[]{:S(2)}) %all-to-all-start.2) | async-done | bytes 131104 | tf_op jit(solution)/shard_map/all_to_all | solution.py:340
  59.0 0.7 copy-done.12
  59.7 7.7 %mixer.1 = (bf16[8,8,24,128]{3,2,1,0:T(8,128)(2,1)}, f32[4,32,256]{2,1,0:T(8,128)}) custom-call(f32[1,512]{1,0:T(1,128)} %copy-done.8, f32[8,64,256]{2,1,0:T(8,128)} %copy-done.2, bf16[16,32,128]{2,1,0:T(8,128)(2,1)} %copy-done.12, f32[5,2048]{1,0:T(8,128)} %bc_taps_ref.1, f32[3,16,2048]{2,1,0:T(8,128)} %bitcast.43, f32[16,8,64,256]{3,2,1,0:T(8,128)} %state_ref.5), custom_call_target="tpu_custom_call" | custom-call | flops 20000000 | bytes 9000000 | tf_op jit(solution)/shard_map/mixer/pallas_call | solution.py:227
  67.3 5.3 %all-to-all-start.3 = ((bf16[64,24,128]{2,1,0:T(8,128)(2,1)}), bf16[64,24,128]{2,1,0:T(8,128)(2,1)S(1)}, u32[]{:S(2)}, u32[]{:S(2)}) async-start(bf16[64,24,128]{2,1,0:T(8,128)(2,1)} %bitcast.45), calls=%async_computation.3 | async-start | bytes 786432 | tf_op jit(solution)/shard_map/all_to_all | solution.py:345
  72.7 4.8 %advance.2.refs_0_ = f32[16,8,64,256]{3,2,1,0:T(8,128)} custom-call(f32[8,64,256]{2,1,0:T(8,128)} %copy-done.2, f32[4,32,256]{2,1,0:T(8,128)} %get-tuple-element.14.b_ref, f32[16,8,64,256]{3,2,1,0:T(8,128)} %state_ref.5), custom_call_target="tpu_custom_call" | custom-call | flops 6000000 | bytes 8500000 | tf_op jit(solution)/shard_map/advance/pallas_call | solution.py:268
  77.5 7.2 %all-to-all-done.3 = bf16[64,24,128]{2,1,0:T(8,128)(2,1)S(1)} async-done(((bf16[64,24,128]{2,1,0:T(8,128)(2,1)}), bf16[64,24,128]{2,1,0:T(8,128)(2,1)S(1)}, u32[]{:S(2)}, u32[]{:S(2)}) %all-to-all-start.3) | async-done | bytes 393248 | tf_op jit(solution)/shard_map/all_to_all | solution.py:345
  84.6 0.9 slice.14
  85.6 0.1 copy.21
  85.7 0.2 reshape.52
  85.9 0.4 collective-permute-done.2.g2_ref
  86.3 1.8 %output.1 = bf16[8,32,512]{2,1,0:T(8,128)(2,1)} custom-call(s32[16]{0:T(128)S(1)} %copy-done.7, s32[2]{0:T(128)S(1)} %pad_add_fusion.pos_ref, bf16[8,8,24,128]{3,2,1,0:T(8,128)(2,1)S(1)} %bitcast.37, bf16[8,8,24,128]{3,2,1,0:T(8,128)(2,1)S(1)} %collective-permute-done.2.g2_ref, bf16[16,64,512]{2,1,0:T(8,128)(2,1)S(1)} %copy-done.3), custom_call_target="tpu_custom_call" | custom-call | flops 270000000 | bytes 2500000 | tf_op jit(solution)/shard_map/output/pallas_call | solution.py:305
  88.1 3.5 %all-to-all-start.4 = ((bf16[8,32,512]{2,1,0:T(8,128)(2,1)}), bf16[8,32,512]{2,1,0:T(8,128)(2,1)S(1)}, u32[]{:S(2)}, u32[]{:S(2)}) async-start(bf16[8,32,512]{2,1,0:T(8,128)(2,1)} %output.1), calls=%async_computation.4 | async-start | bytes 524288 | tf_op jit(solution)/shard_map/all_to_all | solution.py:352
  91.6 0.8 maximum_bitcast_fusion
  92.4 4.8 %advance.3 = f32[16,8,64,256]{3,2,1,0:T(8,128)} custom-call(f32[8,64,256]{2,1,0:T(8,128)} %copy-done.2, f32[4,32,256]{2,1,0:T(8,128)} %get-tuple-element.14.b_ref, f32[16,8,64,256]{3,2,1,0:T(8,128)} %state_ref.5, f32[16,8,64,256]{3,2,1,0:T(8,128)} %advance.2.refs_0_), custom_call_target="tpu_custom_call", output_to_operand_aliasing={{}: (3, {})} | custom-call | flops 6000000 | bytes 8500000 | tf_op jit(solution)/shard_map/advance/pallas_call | solution.py:268
  97.1 3.6 %all-to-all-done.4 = bf16[8,32,512]{2,1,0:T(8,128)(2,1)S(1)} async-done(((bf16[8,32,512]{2,1,0:T(8,128)(2,1)}), bf16[8,32,512]{2,1,0:T(8,128)(2,1)S(1)}, u32[]{:S(2)}, u32[]{:S(2)}) %all-to-all-start.4) | async-done | bytes 262176 | tf_op jit(solution)/shard_map/all_to_all | solution.py:352
  100.7 0.7 reduce_sum.22
  (37 shorter events, 0.5 us)
Async XLA Ops:
  0.6 1.0 %copy-start = (bf16[2,16,8192]{2,1,0:T(8,128)(2,1)S(1)}, bf16[2,16,8192]{2,1,0:T(8,128)(2,1)}, u32[]{:S(2)}) copy-start(bf16[2,16,8192]{2,1,0:T(8,128)(2,1)} %param.15) | copy-start | bytes 1572868
  0.6 9.8 %copy-start.14 = (bf16[512,256]{1,0:T(8,128)(2,1)S(1)}, bf16[512,256]{1,0:T(8,128)(2,1)}, u32[]{:S(2)}) copy-start(bf16[512,256]{1,0:T(8,128)(2,1)} %param.18) | copy-start | bytes 786436
  0.7 12.2 %collective-permute-start = (bf16[512,16,128]{2,1,0:T(8,128)(2,1)}, bf16[512,16,128]{2,1,0:T(8,128)(2,1)}, u32[]{:S(2)}, u32[]{:S(2)}) collective-permute-start(bf16[512,16,128]{2,1,0:T(8,128)(2,1)} %param.16), channel_id=1, source_target_pairs={{0,8},{8,0},{1,9},{9,1},{2,10},{10,2},{3,11},{11,3},{4,12},{12,4},... | collective-permute-start | bytes 6291464 | tf_op jit(solution)/shard_map/ppermute | solution.py:325
  2.5 18.1 %all-to-all-start = ((bf16[8,32,1024]{2,1,0:T(8,128)(2,1)}), bf16[8,32,1024]{2,1,0:T(8,128)(2,1)S(1)}, u32[]{:S(2)}, u32[]{:S(2)}) async-start(bf16[8,32,1024]{2,1,0:T(8,128)(2,1)} %broadcast_in_dim.20), calls=%async_computation | async-start | bytes 1048576 | tf_op jit(solution)/shard_map/all_to_all | solution.py:331
  10.6 5.8 %collective-permute-start.1 = (bf16[512,384]{1,0:T(8,128)(2,1)S(1)}, bf16[512,384]{1,0:T(8,128)(2,1)}, u32[]{:S(2)}, u32[]{:S(2)}) collective-permute-start(bf16[512,384]{1,0:T(8,128)(2,1)S(1)} %maximum_maximum_fusion.wbd_ref), channel_id=1, source_target_pairs={{0,8},{8,0},{1,9},{9,1},{2,10},{10,2},{3,11},{11,3},{4,12},{12,4},... | collective-permute-start | bytes 1179656 | tf_op jit(solution)/shard_map/ppermute | solution.py:325
  12.9 7.7 %copy-start.7 = (s32[16]{0:T(128)S(1)}, s32[16]{0:T(128)}, u32[]{:S(2)}) copy-start(s32[16]{0:T(128)} %map_ref.5) | copy-start | bytes 196
  20.6 1.6 %copy-start.1 = (bf16[64,8,16,128]{3,1,2,0:T(8,128)(2,1)S(1)}, bf16[64,8,16,128]{3,1,2,0:T(8,128)(2,1)}, u32[]{:S(2)}) copy-start(bf16[64,8,16,128]{3,1,2,0:T(8,128)(2,1)} %copy.26) | copy-start | bytes 6291460
  24.5 27.9 %copy-start.4 = (f32[5,8192]{1,0:T(8,128)S(1)}, f32[5,8192]{1,0:T(8,128)}, u32[]{:S(2)}) copy-start(f32[5,8192]{1,0:T(8,128)} %taps_ref.1) | copy-start | bytes 491524
  24.5 27.8 %copy-start.5 = (f32[16,3,512]{2,0,1:T(8,128)S(1)}, f32[16,3,512]{2,0,1:T(8,128)}, u32[]{:S(2)}) copy-start(f32[16,3,512]{2,0,1:T(8,128)} %param.28) | copy-start | bytes 294916
  24.5 27.8 %copy-start.6 = (f32[8192]{0:T(1024)S(1)}, f32[8192]{0:T(1024)}, u32[]{:S(2)}) copy-start(f32[8192]{0:T(1024)} %param.26) | copy-start | bytes 98308
  24.5 27.8 %copy-start.9 = (f32[128]{0:T(128)S(1)}, f32[128]{0:T(128)}, u32[]{:S(2)}) copy-start(f32[128]{0:T(128)} %a_ref.1) | copy-start | bytes 1540
  24.5 27.8 %copy-start.10 = (f32[128]{0:T(128)S(1)}, f32[128]{0:T(128)}, u32[]{:S(2)}) copy-start(f32[128]{0:T(128)} %bias_ref.1) | copy-start | bytes 1540
  24.6 27.8 %copy-start.11 = (f32[128]{0:T(128)S(1)}, f32[128]{0:T(128)}, u32[]{:S(2)}) copy-start(f32[128]{0:T(128)} %skip_ref.1) | copy-start | bytes 1540
  48.8 10.2 %all-to-all-start.2 = ((bf16[16,32,128]{2,1,0:T(8,128)(2,1)}), bf16[16,32,128]{2,1,0:T(8,128)(2,1)S(1)}, u32[]{:S(2)}, u32[]{:S(2)}) async-start(bf16[16,32,128]{2,1,0:T(8,128)(2,1)} %broadcast_in_dim.23), calls=%async_computation.2 | async-start | bytes 262144 | tf_op jit(solution)/shard_map/all_to_all | solution.py:340
  54.6 0.8 copy-start.2
  55.4 0.6 copy-start.8
  59.0 0.7 copy-start.12
  67.3 17.3 %all-to-all-start.3 = ((bf16[64,24,128]{2,1,0:T(8,128)(2,1)}), bf16[64,24,128]{2,1,0:T(8,128)(2,1)S(1)}, u32[]{:S(2)}, u32[]{:S(2)}) async-start(bf16[64,24,128]{2,1,0:T(8,128)(2,1)} %bitcast.45), calls=%async_computation.3 | async-start | bytes 786432 | tf_op jit(solution)/shard_map/all_to_all | solution.py:345
  72.6 12.9 %copy-start.13 = (bf16[16,32,128]{2,1,0:T(8,128)(2,1)S(1)}, bf16[16,32,128]{2,1,0:T(8,128)(2,1)}, u32[]{:S(2)}) copy-start(bf16[16,32,128]{2,1,0:T(8,128)(2,1)} %copy-done.12) | copy-start | bytes 393220
  77.4 8.9 %copy-start.3 = (bf16[16,64,512]{2,1,0:T(8,128)(2,1)S(1)}, bf16[16,64,512]{2,1,0:T(8,128)(2,1)}, u32[]{:S(2)}) copy-start(bf16[16,64,512]{2,1,0:T(8,128)(2,1)} %w_ref.1) | copy-start | bytes 3145732
  84.6 1.7 %collective-permute-start.2 = (bf16[8,8,24,128]{3,2,1,0:T(8,128)(2,1)S(1)}, bf16[8,8,24,128]{3,2,1,0:T(8,128)(2,1)S(1)}, u32[]{:S(2)}, u32[]{:S(2)}) collective-permute-start(bf16[8,8,24,128]{3,2,1,0:T(8,128)(2,1)S(1)} %bitcast.36), channel_id=1, source_target_pairs={{0,8},{8,0},{1,9},{9,1},{2,10},{10,2},{3,11},{11,3},{4,12},{12,4},... | collective-permute-start | bytes 1179656 | tf_op jit(solution)/shard_map/ppermute | solution.py:325
  88.1 12.6 %all-to-all-start.4 = ((bf16[8,32,512]{2,1,0:T(8,128)(2,1)}), bf16[8,32,512]{2,1,0:T(8,128)(2,1)S(1)}, u32[]{:S(2)}, u32[]{:S(2)}) async-start(bf16[8,32,512]{2,1,0:T(8,128)(2,1)} %output.1), calls=%async_computation.4 | async-start | bytes 524288 | tf_op jit(solution)/shard_map/all_to_all | solution.py:352

commit v3 on v2

--- a/solution.py
+++ b/solution.py
@@ -12,7 +12,7 @@
 F32 = jnp.float32
 BF16 = jnp.bfloat16
 MIB = 2**20
-STATE_MIB = 56
+STATE_MIB = 50
 PART = 4
 
 
@@ -240,41 +240,83 @@
 
 
 def advance_kernel(start, col_ref, b_ref, state_ref, *refs):
-    def body(col_ref, b_ref, s_ref, out_ref):
+    out_ref, s_ref, n_ref, in_sem, out_sem = refs[-5:]
+    chunks = [(g, k) for g in range(2) for k in range(16 // PART)]
+
+    def piece(ref, g, k):
+        return ref.at[pl.ds(PART * k, PART), pl.ds(2 * (start + g), 2)]
+
+    def held(ref, g, k):
+        return ref.at[g, pl.ds(PART * k, PART)]
+
+    loads = [
+        pltpu.make_async_copy(piece(state_ref, g, k), held(s_ref, g, k), in_sem.at[g, k])
+        for g, k in chunks
+    ]
+    stores = [
+        pltpu.make_async_copy(held(n_ref, g, k), piece(out_ref, g, k), out_sem.at[g, k])
+        for g, k in chunks
+    ]
+    for load in loads:
+        load.start()
+    for (g, k), load, store in zip(chunks, loads, stores):
+        load.wait()
         for j in range(2):
-            cols = col_ref[j]
-            for r in range(16):
-                k = 16 + r
-                out_ref[r, j] = (
-                    cols[0:1, DECAY + k : DECAY + k + 1] * s_ref[r, j]
-                    + cols[:, FIRST + k : FIRST + k + 1] * b_ref[r : r + 1, :]
-                    + cols[:, SECOND + k : SECOND + k + 1] * b_ref[k : k + 1, :]
+            cols = col_ref[2 * g + j]
+            for r in range(PART * k, PART * k + PART):
+                i = 16 + r
+                n_ref[g, r, j] = (
+                    cols[0:1, DECAY + i : DECAY + i + 1] * s_ref[g, r, j]
+                    + cols[:, FIRST + i : FIRST + i + 1] * b_ref[g, r : r + 1, :]
+                    + cols[:, SECOND + i : SECOND + i + 1] * b_ref[g, i : i + 1, :]
                 )
-
-    pltpu.emit_pipeline(
-        body,
-        grid=(2,),
-        in_specs=[
-            pl.BlockSpec((2, 64, 256), lambda g: (g + start, 0, 0)),
-            pl.BlockSpec((None, 32, 256), lambda g: (g + start, 0, 0)),
-            pl.BlockSpec((16, 2, 64, 256), lambda g: (0, g + start, 0, 0)),
-        ],
-        out_specs=[pl.BlockSpec((16, 2, 64, 256), lambda g: (0, g + start, 0, 0))],
-    )(col_ref, b_ref, state_ref, refs[-1])
+        store.start()
+    for store in stores:
+        store.wait()
 
 
 def advance(cols, b, state, start, into):
     more = [] if into is None else [into]
     return pl.pallas_call(
         functools.partial(advance_kernel, start),
-        in_specs=[pl.BlockSpec(memory_space=pl.ANY)] * 2 + [HBM] * (1 + len(more)),
+        grid=(1,),
+        in_specs=[
+            pl.BlockSpec((4, 64, 256), lambda i: (start // 2, 0, 0)),
+            pl.BlockSpec((2, 32, 256), lambda i: (start // 2, 0, 0)),
+        ] + [HBM] * (1 + len(more)),
         out_specs=HBM,
         out_shape=jax.ShapeDtypeStruct(state.shape, F32),
+        scratch_shapes=[
+            pltpu.VMEM((2, 16, 2, 64, 256), F32),
+            pltpu.VMEM((2, 16, 2, 64, 256), F32),
+            pltpu.SemaphoreType.DMA((2, 16 // PART)),
+            pltpu.SemaphoreType.DMA((2, 16 // PART)),
+        ],
         input_output_aliases={3: 0} if more else {},
         compiler_params=pltpu.CompilerParams(vmem_limit_bytes=STATE_MIB * MIB),
         cost_estimate=pl.CostEstimate(flops=6_000_000, bytes_accessed=8_500_000, transcendentals=0),
         name="advance",
     )(cols, b, state, *more)
+
+
+def history_kernel(bc_ref, bc_hist_ref, out_ref):
+    bc = jnp.transpose(bc_ref[...].astype(F32), (1, 0, 2))
+    out_ref[0] = bc_hist_ref[2]
+    for step in range(2):
+        for k in range(16):
+            out_ref[1 + step, :, 128 * k : 128 * k + 128] = bc[2 * k + step]
+
+
+def history(bc, bc_hist):
+    return pl.pallas_call(
+        history_kernel,
+        in_specs=[VMEM] * 2,
+        out_specs=VMEM,
+        out_shape=jax.ShapeDtypeStruct(bc_hist.shape, F32),
+        compiler_params=pltpu.CompilerParams(vmem_limit_bytes=16 * MIB),
+        cost_estimate=pl.CostEstimate(flops=0, bytes_accessed=900_000, transcendentals=0),
+        name="history",
+    )(bc, bc_hist)
 
 
 def output_kernel(map_ref, pos_ref, g1_ref, g2_ref, w_ref, o_ref, w_scr, l_scr):
@@ -343,10 +385,9 @@
 
     gated, b = mixer(gain, cols, low, conv_bc, conv_bc_state.transpose(1, 0, 2), ssm_state)
     gathered = lax.all_to_all(gated.reshape(64, 24, 128), ("chip", "tp"), 0, 0, tiled=True).reshape(8, 8, 24, 128)
-    fresh = low.reshape(16, 8, 2, 2, 128).transpose(3, 0, 1, 2, 4).reshape(2, 16, 2048)
-    bc_hist = jnp.concatenate([conv_bc_state.transpose(1, 0, 2)[2:], fresh.astype(F32)], axis=0)
+    bc_hist = history(low, conv_bc_state.transpose(1, 0, 2))
     state = advance(cols, b, ssm_state, 0, None)
-    gathered, state = lax.optimization_barrier((gathered, state))
+    gathered, state, bc_hist = lax.optimization_barrier((gathered, state, bc_hist))
     state = advance(cols, b, ssm_state, 2, state)
     shares = output(head_map, pos, gathered, swap(gathered), w_out)
     shares = lax.all_to_all(shares, "tp", 0, 0, tiled=True)

time: 102 us -> 100 us (0.980)
  waiting for transfers between devices: 18.5 us -> 22.4 us
  local copies, waits for them, and re-layouts: 13.9 us -> 10.6 us
  Pallas kernels: 23.5 us -> 21.8 us
    unnamed x33 -> x29, local copies, waits for them, and re-layouts: 11 us -> 9.02 us
    all_to_all x1, waiting for transfers between devices: 3.64 us -> 5.06 us  [per_device(): shares = lax.all_to_all(shares, 'tp', 0, 0, tiled=True)]
    all_to_all x1, waiting for transfers between devices: 3 us -> 4.39 us  [per_device(): lax.all_to_all(jnp.broadcast_to(low[None], (16, 32, 128)), ('chip', 'core...]
    ppermute x3, waiting for transfers between devices: 0.41 us -> 1.73 us  [swap(): return lax.ppermute(v, 'core', [(0, 1), (1, 0)])]
    pallas_call x1, Pallas kernels: 7.66 us -> 6.47 us  [mixer(): pl.pallas_call(mixer_kernel, in_specs=[VMEM] * 5 + [HBM], out_specs=(VMEM...]
    pallas_call x2 -> x3, Pallas kernels: 9.55 us -> 9.09 us  [the longest x2 8.27 us: advance(): pl.pallas_call(functools.partial(advance_kernel, start), grid=(1,), in_sp...]
  transfers between devices with their start and end apart: 7 -> 7, of which waited for: 5 -> 5; matrix products, arithmetic and copies ran while one was open for 9% -> 8% of each run, Pallas kernels for 12% -> 11%
where the time goes in v3:
time: 100 us; the launch traced here: 99.6 us
  blocking collectives  23.4 us (23%)
  waiting for transfers between devices  22.4 us (22%)
  Pallas kernels  21.8 us (22%)
  starting transfers between devices  19.5 us (20%)
  local copies, waits for them, and re-layouts  10.6 us (11%)
    all_to_all x1, blocking collectives, per_device(): lax.all_to_all(partial.reshape(64, 48, 128), ('chip', 'tp'), 0, 0, tiled=...  23.4 us
    unnamed x29, local copies, waits for them, and re-layouts  9.02 us
    pallas_call x2, Pallas kernels, advance(): pl.pallas_call(functools.partial(advance_kernel, start), grid=(1,), in_sp...  8.27 us
    all_to_all x1, starting transfers between devices, per_device(): lax.all_to_all(jnp.broadcast_to(x[None], (8, 32, 1024)), 'tp', 0, 0, tile...  7.01 us
    all_to_all x1, waiting for transfers between devices, per_device(): lax.all_to_all(gated.reshape(64, 24, 128), ('chip', 'tp'), 0, 0, tiled=True)  6.97 us
    pallas_call x1, Pallas kernels, mixer(): pl.pallas_call(mixer_kernel, in_specs=[VMEM] * 5 + [HBM], out_specs=(VMEM...  6.47 us
    all_to_all x1, starting transfers between devices, per_device(): lax.all_to_all(gated.reshape(64, 24, 128), ('chip', 'tp'), 0, 0, tiled=True)  5.29 us
    all_to_all x1, waiting for transfers between devices, per_device(): shares = lax.all_to_all(shares, 'tp', 0, 0, tiled=True)  5.06 us
  transfers between devices with their start and end apart: 7, of which 5 were waited for; matrix products, arithmetic and copies ran while one was open for 8% of the time, Pallas kernels for 11%

profile of v3, /device:TPU:0, one launch (start us, length us, event | category | flops | bytes accessed | tf_op | source)
XLA Modules:
  0.0 99.6 jit_solution(15900439839253292412)
XLA Ops:
  0.6 0.0 copy-start
  0.7 0.1 collective-permute-start
  0.8 0.9 copy-done
  1.7 0.9 broadcast_in_dim.20
  2.5 7.0 %all-to-all-start = ((bf16[8,32,1024]{2,1,0:T(8,128)(2,1)}), bf16[8,32,1024]{2,1,0:T(8,128)(2,1)S(1)}, u32[]{:S(2)}, u32[]{:S(2)}) async-start(bf16[8,32,1024]{2,1,0:T(8,128)(2,1)} %broadcast_in_dim.20), calls=%async_computation | async-start | bytes 1048576 | tf_op jit(solution)/shard_map/all_to_all | solution.py:373
  9.6 0.8 copy.20
  10.4 0.1 pad.2.clone
  10.5 0.1 maximum_maximum_fusion.wbd_ref
  10.6 0.1 collective-permute-start.1
  10.7 2.1 %copy.26 = bf16[64,8,16,128]{3,1,2,0:T(8,128)(2,1)S(1)} copy(bf16[64,8,16,128]{3,2,1,0:T(8,128)(2,1)} %bitcast.36) | data formatting | bytes 4194304
  12.8 0.1 pad_add_fusion.pos_ref
  12.9 3.5 %copy.25 = bf16[64,8,16,128]{3,1,2,0:T(8,128)(2,1)} copy(bf16[64,8,16,128]{3,2,1,0:T(8,128)(2,1)} %bitcast.18) | data formatting | bytes 4194304
  16.4 4.3 %all-to-all-done = bf16[8,32,1024]{2,1,0:T(8,128)(2,1)S(1)} async-done(((bf16[8,32,1024]{2,1,0:T(8,128)(2,1)}), bf16[8,32,1024]{2,1,0:T(8,128)(2,1)S(1)}, u32[]{:S(2)}, u32[]{:S(2)}) %all-to-all-start) | async-done | bytes 524320 | tf_op jit(solution)/shard_map/all_to_all | solution.py:373
  20.6 1.6 %copy-done.1 = bf16[64,8,16,128]{3,1,2,0:T(8,128)(2,1)S(1)} copy-done((bf16[64,8,16,128]{3,1,2,0:T(8,128)(2,1)S(1)}, bf16[64,8,16,128]{3,1,2,0:T(8,128)(2,1)}, u32[]{:S(2)}) %copy-start.1) | copy-done | bytes 2097176
  22.2 2.3 %project.1 = bf16[8,8,48,128]{3,2,1,0:T(8,128)(2,1)S(1)} custom-call(s32[16]{0:T(128)S(1)} %copy-done.8, s32[2]{0:T(128)S(1)} %pad_add_fusion.pos_ref, bf16[256,1024]{1,0:T(8,128)(2,1)S(1)} %bitcast.28, bf16[512,2048]{1,0:T(8,128)(2,1)S(1)} %bitcast.25, bf16[512,2048]{1,0:T(8,128)(2,1)S(1)} %bitcast.26, bf16[512,384]{1,0:T(8,128)(2,1)S(1)} %maximum_maximum_fusion.wbd_ref, ...), custom_call_target="tpu_custom_call" | custom-call | flops 600000000 | bytes 5500000 | tf_op jit(solution)/shard_map/project/pallas_call | solution.py:77
  24.6 23.4 %all_to_all.25 = bf16[64,48,128]{2,1,0:T(8,128)(2,1)S(1)} all-to-all(bf16[64,48,128]{2,1,0:T(8,128)(2,1)S(1)} %bitcast.27), channel_id=1, replica_groups=mesh['chip'=8,'core'=2,'tp'=8] {'chip','tp'}, dimensions={0} | all-to-all | bytes 1572864 | tf_op jit(solution)/shard_map/all_to_all | solution.py:375
  48.0 0.1 convert_reduce_fusion.xz_ref
  48.2 0.7 broadcast_in_dim.23
  48.8 3.5 %all-to-all-start.2 = ((bf16[16,32,128]{2,1,0:T(8,128)(2,1)}), bf16[16,32,128]{2,1,0:T(8,128)(2,1)S(1)}, u32[]{:S(2)}, u32[]{:S(2)}) async-start(bf16[16,32,128]{2,1,0:T(8,128)(2,1)} %broadcast_in_dim.23), calls=%async_computation.2 | async-start | bytes 262144 | tf_op jit(solution)/shard_map/all_to_all | solution.py:382
  52.4 2.2 %heads_part.1 = (f32[8,64,256]{2,1,0:T(8,128)S(1)}, f32[3,16,512]{2,1,0:T(8,128)}, f32[1,512]{1,0:T(1,128)S(1)}) custom-call(s32[16]{0:T(128)S(1)} %copy-done.8, s32[2]{0:T(128)S(1)} %pad_add_fusion.pos_ref, f32[128]{0:T(128)S(1)} %copy-done.9, f32[128]{0:T(128)S(1)} %copy-done.10, f32[128]{0:T(128)S(1)} %copy-done.11, f32[5,8192]{1,0:T(8,128)S(1)} %copy-done.4, ...), custom_call_target="tpu_custom_call" | custom-call | flops 2000000 | bytes 1000000 | tf_op jit(solution)/shard_map/heads_part/pallas_call | solution.py:149
  54.6 4.4 %all-to-all-done.2.bc_ref = bf16[16,32,128]{2,1,0:T(8,128)(2,1)S(1)} async-done(((bf16[16,32,128]{2,1,0:T(8,128)(2,1)}), bf16[16,32,128]{2,1,0:T(8,128)(2,1)S(1)}, u32[]{:S(2)}, u32[]{:S(2)}) %all-to-all-start.2) | async-done | bytes 131104 | tf_op jit(solution)/shard_map/all_to_all | solution.py:382
  59.0 6.5 %mixer.1 = (bf16[8,8,24,128]{3,2,1,0:T(8,128)(2,1)}, f32[4,32,256]{2,1,0:T(8,128)S(1)}) custom-call(f32[1,512]{1,0:T(1,128)S(1)} %get-tuple-element.12.gain_ref, f32[8,64,256]{2,1,0:T(8,128)S(1)} %get-tuple-element.13.col_ref, bf16[16,32,128]{2,1,0:T(8,128)(2,1)S(1)} %all-to-all-done.2.bc_ref, f32[5,2048]{1,0:T(8,128)S(1)} %copy-done.6, ...), custom_call_target="tpu_custom_call" | custom-call | flops 20000000 | bytes 9000000 | tf_op jit(solution)/shard_map/mixer/pallas_call | solution.py:227
  65.5 5.3 %all-to-all-start.3 = ((bf16[64,24,128]{2,1,0:T(8,128)(2,1)}), bf16[64,24,128]{2,1,0:T(8,128)(2,1)S(1)}, u32[]{:S(2)}, u32[]{:S(2)}) async-start(bf16[64,24,128]{2,1,0:T(8,128)(2,1)} %bitcast.10), calls=%async_computation.3 | async-start | bytes 786432 | tf_op jit(solution)/shard_map/all_to_all | solution.py:387
  70.8 0.8 history.1
  71.6 4.2 %advance.2.refs_0_ = f32[16,8,64,256]{3,2,1,0:T(8,128)} custom-call(f32[8,64,256]{2,1,0:T(8,128)S(1)} %get-tuple-element.13.col_ref, f32[4,32,256]{2,1,0:T(8,128)S(1)} %get-tuple-element.15.b_ref, f32[16,8,64,256]{3,2,1,0:T(8,128)} %state_ref.5), custom_call_target="tpu_custom_call" | custom-call | flops 6000000 | bytes 8500000 | tf_op jit(solution)/shard_map/advance/pallas_call | solution.py:280
  75.8 7.0 %all-to-all-done.3 = bf16[64,24,128]{2,1,0:T(8,128)(2,1)S(1)} async-done(((bf16[64,24,128]{2,1,0:T(8,128)(2,1)}), bf16[64,24,128]{2,1,0:T(8,128)(2,1)S(1)}, u32[]{:S(2)}, u32[]{:S(2)}) %all-to-all-start.3) | async-done | bytes 393248 | tf_op jit(solution)/shard_map/all_to_all | solution.py:387
  82.8 1.7 %collective-permute-done.2.g2_ref = bf16[8,8,24,128]{3,2,1,0:T(8,128)(2,1)S(1)} collective-permute-done((bf16[8,8,24,128]{3,2,1,0:T(8,128)(2,1)S(1)}, bf16[8,8,24,128]{3,2,1,0:T(8,128)(2,1)S(1)}, u32[]{:S(2)}, u32[]{:S(2)}) %collective-permute-start.2) | collective-permute-done | bytes 393248 | tf_op jit(solution)/shard_map/ppermute | solution.py:367
  84.5 1.8 %output.1 = bf16[8,32,512]{2,1,0:T(8,128)(2,1)} custom-call(s32[16]{0:T(128)S(1)} %copy-done.8, s32[2]{0:T(128)S(1)} %pad_add_fusion.pos_ref, bf16[8,8,24,128]{3,2,1,0:T(8,128)(2,1)S(1)} %bitcast.30, bf16[8,8,24,128]{3,2,1,0:T(8,128)(2,1)S(1)} %collective-permute-done.2.g2_ref, bf16[16,64,512]{2,1,0:T(8,128)(2,1)S(1)} %copy-done.3), custom_call_target="tpu_custom_call" | custom-call | flops 270000000 | bytes 2500000 | tf_op jit(solution)/shard_map/output/pallas_call | solution.py:347
  86.3 3.5 %all-to-all-start.4 = ((bf16[8,32,512]{2,1,0:T(8,128)(2,1)}), bf16[8,32,512]{2,1,0:T(8,128)(2,1)S(1)}, u32[]{:S(2)}, u32[]{:S(2)}) async-start(bf16[8,32,512]{2,1,0:T(8,128)(2,1)} %output.1), calls=%async_computation.4 | async-start | bytes 524288 | tf_op jit(solution)/shard_map/all_to_all | solution.py:393
  89.8 4.1 %advance.3 = f32[16,8,64,256]{3,2,1,0:T(8,128)} custom-call(f32[8,64,256]{2,1,0:T(8,128)S(1)} %get-tuple-element.13.col_ref, f32[4,32,256]{2,1,0:T(8,128)S(1)} %get-tuple-element.15.b_ref, f32[16,8,64,256]{3,2,1,0:T(8,128)} %state_ref.5, f32[16,8,64,256]{3,2,1,0:T(8,128)} %advance.2.refs_0_), custom_call_target="tpu_custom_call", output_to_operand_aliasing={{}: (3, {})} | custom-call | flops 6000000 | bytes 8500000 | tf_op jit(solution)/shard_map/advance/pallas_call | solution.py:280
  93.9 5.1 %all-to-all-done.4 = bf16[8,32,512]{2,1,0:T(8,128)(2,1)S(1)} async-done(((bf16[8,32,512]{2,1,0:T(8,128)(2,1)}), bf16[8,32,512]{2,1,0:T(8,128)(2,1)S(1)}, u32[]{:S(2)}, u32[]{:S(2)}) %all-to-all-start.4) | async-done | bytes 262176 | tf_op jit(solution)/shard_map/all_to_all | solution.py:393
  98.9 0.7 reduce_sum.22
  (29 shorter events, 0.1 us)
Async XLA Ops:
  0.6 1.0 %copy-start = (bf16[2,16,8192]{2,1,0:T(8,128)(2,1)S(1)}, bf16[2,16,8192]{2,1,0:T(8,128)(2,1)}, u32[]{:S(2)}) copy-start(bf16[2,16,8192]{2,1,0:T(8,128)(2,1)} %param.15) | copy-start | bytes 1572868
  0.6 9.8 %copy-start.12 = (bf16[512,256]{1,0:T(8,128)(2,1)S(1)}, bf16[512,256]{1,0:T(8,128)(2,1)}, u32[]{:S(2)}) copy-start(bf16[512,256]{1,0:T(8,128)(2,1)} %param.18) | copy-start | bytes 786436
  0.7 12.2 %collective-permute-start = (bf16[512,16,128]{2,1,0:T(8,128)(2,1)}, bf16[512,16,128]{2,1,0:T(8,128)(2,1)}, u32[]{:S(2)}, u32[]{:S(2)}) collective-permute-start(bf16[512,16,128]{2,1,0:T(8,128)(2,1)} %param.16), channel_id=1, source_target_pairs={{0,8},{8,0},{1,9},{9,1},{2,10},{10,2},{3,11},{11,3},{4,12},{12,4},... | collective-permute-start | bytes 6291464 | tf_op jit(solution)/shard_map/ppermute | solution.py:367
  2.5 18.1 %all-to-all-start = ((bf16[8,32,1024]{2,1,0:T(8,128)(2,1)}), bf16[8,32,1024]{2,1,0:T(8,128)(2,1)S(1)}, u32[]{:S(2)}, u32[]{:S(2)}) async-start(bf16[8,32,1024]{2,1,0:T(8,128)(2,1)} %broadcast_in_dim.20), calls=%async_computation | async-start | bytes 1048576 | tf_op jit(solution)/shard_map/all_to_all | solution.py:373
  10.6 5.8 %collective-permute-start.1 = (bf16[512,384]{1,0:T(8,128)(2,1)S(1)}, bf16[512,384]{1,0:T(8,128)(2,1)}, u32[]{:S(2)}, u32[]{:S(2)}) collective-permute-start(bf16[512,384]{1,0:T(8,128)(2,1)S(1)} %maximum_maximum_fusion.wbd_ref), channel_id=1, source_target_pairs={{0,8},{8,0},{1,9},{9,1},{2,10},{10,2},{3,11},{11,3},{4,12},{12,4},... | collective-permute-start | bytes 1179656 | tf_op jit(solution)/shard_map/ppermute | solution.py:367
  12.9 7.7 %copy-start.8 = (s32[16]{0:T(128)S(1)}, s32[16]{0:T(128)}, u32[]{:S(2)}) copy-start(s32[16]{0:T(128)} %map_ref.5) | copy-start | bytes 196
  20.6 1.6 %copy-start.1 = (bf16[64,8,16,128]{3,1,2,0:T(8,128)(2,1)S(1)}, bf16[64,8,16,128]{3,1,2,0:T(8,128)(2,1)}, u32[]{:S(2)}) copy-start(bf16[64,8,16,128]{3,1,2,0:T(8,128)(2,1)} %copy.25) | copy-start | bytes 6291460
  24.5 27.9 %copy-start.4 = (f32[5,8192]{1,0:T(8,128)S(1)}, f32[5,8192]{1,0:T(8,128)}, u32[]{:S(2)}) copy-start(f32[5,8192]{1,0:T(8,128)} %taps_ref.1) | copy-start | bytes 491524
  24.5 27.9 %copy-start.5 = (f32[16,3,512]{2,0,1:T(8,128)S(1)}, f32[16,3,512]{2,0,1:T(8,128)}, u32[]{:S(2)}) copy-start(f32[16,3,512]{2,0,1:T(8,128)} %param.28) | copy-start | bytes 294916
  24.5 27.9 %copy-start.7 = (f32[8192]{0:T(1024)S(1)}, f32[8192]{0:T(1024)}, u32[]{:S(2)}) copy-start(f32[8192]{0:T(1024)} %param.26) | copy-start | bytes 98308
  24.5 27.9 %copy-start.9 = (f32[128]{0:T(128)S(1)}, f32[128]{0:T(128)}, u32[]{:S(2)}) copy-start(f32[128]{0:T(128)} %a_ref.1) | copy-start | bytes 1540
  24.6 27.8 %copy-start.10 = (f32[128]{0:T(128)S(1)}, f32[128]{0:T(128)}, u32[]{:S(2)}) copy-start(f32[128]{0:T(128)} %bias_ref.1) | copy-start | bytes 1540
  24.6 27.8 %copy-start.11 = (f32[128]{0:T(128)S(1)}, f32[128]{0:T(128)}, u32[]{:S(2)}) copy-start(f32[128]{0:T(128)} %skip_ref.1) | copy-start | bytes 1540
  24.6 34.5 %copy-start.2 = (f32[16,3,2048]{2,0,1:T(8,128)S(1)}, f32[16,3,2048]{2,0,1:T(8,128)}, u32[]{:S(2)}) copy-start(f32[16,3,2048]{2,0,1:T(8,128)} %param.29) | copy-start | bytes 1179652
  24.6 34.4 %copy-start.6 = (f32[5,2048]{1,0:T(8,128)S(1)}, f32[5,2048]{1,0:T(8,128)}, u32[]{:S(2)}) copy-start(f32[5,2048]{1,0:T(8,128)} %bc_taps_ref.1) | copy-start | bytes 122884
  48.8 10.2 %all-to-all-start.2 = ((bf16[16,32,128]{2,1,0:T(8,128)(2,1)}), bf16[16,32,128]{2,1,0:T(8,128)(2,1)S(1)}, u32[]{:S(2)}, u32[]{:S(2)}) async-start(bf16[16,32,128]{2,1,0:T(8,128)(2,1)} %broadcast_in_dim.23), calls=%async_computation.2 | async-start | bytes 262144 | tf_op jit(solution)/shard_map/all_to_all | solution.py:382
  65.5 17.3 %all-to-all-start.3 = ((bf16[64,24,128]{2,1,0:T(8,128)(2,1)}), bf16[64,24,128]{2,1,0:T(8,128)(2,1)S(1)}, u32[]{:S(2)}, u32[]{:S(2)}) async-start(bf16[64,24,128]{2,1,0:T(8,128)(2,1)} %bitcast.10), calls=%async_computation.3 | async-start | bytes 786432 | tf_op jit(solution)/shard_map/all_to_all | solution.py:387
  71.6 12.9 %copy-start.3 = (bf16[16,64,512]{2,1,0:T(8,128)(2,1)S(1)}, bf16[16,64,512]{2,1,0:T(8,128)(2,1)}, u32[]{:S(2)}) copy-start(bf16[16,64,512]{2,1,0:T(8,128)(2,1)} %w_ref.1) | copy-start | bytes 3145732
  82.8 1.7 %collective-permute-start.2 = (bf16[8,8,24,128]{3,2,1,0:T(8,128)(2,1)S(1)}, bf16[8,8,24,128]{3,2,1,0:T(8,128)(2,1)S(1)}, u32[]{:S(2)}, u32[]{:S(2)}) collective-permute-start(bf16[8,8,24,128]{3,2,1,0:T(8,128)(2,1)S(1)} %bitcast.29), channel_id=1, source_target_pairs={{0,8},{8,0},{1,9},{9,1},{2,10},{10,2},{3,11},{11,3},{4,12},{12,4},... | collective-permute-start | bytes 1179656 | tf_op jit(solution)/shard_map/ppermute | solution.py:367
  86.3 12.6 %all-to-all-start.4 = ((bf16[8,32,512]{2,1,0:T(8,128)(2,1)}), bf16[8,32,512]{2,1,0:T(8,128)(2,1)S(1)}, u32[]{:S(2)}, u32[]{:S(2)}) async-start(bf16[8,32,512]{2,1,0:T(8,128)(2,1)} %output.1), calls=%async_computation.4 | async-start | bytes 524288 | tf_op jit(solution)/shard_map/all_to_all | solution.py:393

commit v4 on v3

--- a/solution.py
+++ b/solution.py
@@ -11,6 +11,8 @@
 EPSILON = 1e-05
 F32 = jnp.float32
 BF16 = jnp.bfloat16
+F16 = jnp.float16
+SCALE = 128.0
 MIB = 2**20
 STATE_MIB = 50
 PART = 4
@@ -30,42 +32,27 @@
             x2, w2, preferred_element_type=F32
         )
 
-    def split(v):
-        high = v.astype(BF16).astype(F32)
-        return high, v - high
-
-    y = dot(wbd_ref[...], wbd2_ref[...])
+    y = SCALE * dot(wbd_ref[...], wbd2_ref[...])
     dt_scr[...] = y[:, 256:384].T
-    bc_high, bc_low = split(y[:, 0:256])
-    none = jnp.zeros((7, 128), F32)
+    bc = jnp.where(core == 0, y[:, 0:128], y[:, 128:256])
+    none = jnp.zeros((8, 96), F32)
+    first = lax.broadcasted_iota(jnp.int32, (8, 32), 0) == 0
     for i in range(0, 8, 2):
         heads = [map_ref[2 * k + core] for k in (i, i + 1)]
         cols = [pl.ds(pl.multiple_of(head * 128, 128), 128) for head in heads]
-        both = dot(
+        both = SCALE * dot(
             jnp.concatenate([w_ref[:, c] for c in cols], axis=1),
             jnp.concatenate([w2_ref[:, c] for c in cols], axis=1),
-        ).astype(BF16)
+        )
         for k in range(2):
-            dt_high, dt_low = split(dt_scr[pl.ds(heads[k], 1), :])
+            dt = dt_scr[pl.ds(heads[k], 1), :]
             for t in range(8):
-                o_ref[i + k, t, 0:32, :] = both[32 * t : 32 * t + 32, 128 * k : 128 * k + 128]
-                at = 32 * t + 2 * (i + k)
-                high, low = (
-                    jnp.concatenate(
-                        [
-                            jnp.where(core == 0, v[b : b + 1], v[b + 1 : b + 2])
-                            for b in (at, at + 16)
-                        ],
-                        axis=0,
-                    )
-                    for v in (bc_high, bc_low)
+                rows = slice(32 * t, 32 * t + 32)
+                o_ref[i + k, t, 0:32, :] = both[rows, 128 * k : 128 * k + 128]
+                o_ref[i + k, t, 32:64, :] = bc[rows]
+                o_ref[i + k, t, 64:72, :] = jnp.concatenate(
+                    [jnp.where(first, dt[:, rows], 0.0), none], axis=1
                 )
-                lanes = slice(32 * t, 32 * t + 32)
-                dt = jnp.concatenate([dt_high[:, lanes], dt_low[:, lanes], none[0:1, 0:64]], axis=1)
-                o_ref[i + k, t, 32:48, :] = jnp.concatenate(
-                    [high[:, 0:128], high[:, 128:256], low[:, 0:128], low[:, 128:256], dt, none],
-                    axis=0,
-                ).astype(BF16)
 
 
 HBM = pl.BlockSpec(memory_space=pltpu.HBM)
@@ -78,7 +65,7 @@
         project_kernel,
         in_specs=[SMEM] * 2 + [VMEM] * 5,
         out_specs=VMEM,
-        out_shape=jax.ShapeDtypeStruct((8, 8, 48, 128), BF16),
+        out_shape=jax.ShapeDtypeStruct((8, 8, 72, 128), F32),
         scratch_shapes=[pltpu.VMEM((128, 256), F32)],
         compiler_params=pltpu.CompilerParams(vmem_limit_bytes=16 * MIB),
         cost_estimate=pl.CostEstimate(flops=600_000_000, bytes_accessed=5_500_000, transcendentals=0),
@@ -122,7 +109,7 @@
     x_out_ref[2] = x[16:32]
     x_act = jnp.concatenate(conv(x_hist_ref, x[0:16], x[16:32], local(taps_ref)), axis=0)
     both = jnp.concatenate([x_act, silu(z)], axis=0).T
-    raw = jnp.concatenate([xz_ref[j, 40:41, 0:32] + xz_ref[j, 40:41, 32:64] for j in range(8)], axis=0)
+    raw = jnp.concatenate([xz_ref[j, 64:65, 0:32] for j in range(8)], axis=0)
     raw = raw + scalars(bias_ref)
     step = jnp.maximum(raw, 0.0) + jnp.log1p(jnp.exp(-jnp.abs(raw)))
     decay = jnp.exp(-step * jnp.exp(scalars(a_ref)))
@@ -161,8 +148,18 @@
     )(head_map, pos, a_log, dt_bias, skip_coef, conv_x, norm_gain[None], xz, x_hist)
 
 
+def projections(pos_ref, bc_ref, bc2_ref):
+    mine, other = bc_ref[...].astype(F32), bc2_ref[...].astype(F32)
+    low = jnp.where(pos_ref[1] == 0, mine, other)
+    high = jnp.where(pos_ref[1] == 0, other, mine)
+    return [
+        jnp.concatenate([v[t, 16 * step : 16 * step + 16] for t in range(8) for v in (low, high)], axis=1)
+        for step in range(2)
+    ]
+
+
 def mixer_kernel(
-    gain_ref, col_ref, bc_ref, bc_taps_ref, bc_hist_ref, state_ref, g_ref, b_ref, s_ref, sem,
+    pos_ref, gain_ref, col_ref, bc_ref, bc2_ref, bc_taps_ref, bc_hist_ref, state_ref, g_ref, b_ref, s_ref, sem,
 ):
     copies = [
         pltpu.make_async_copy(
@@ -175,10 +172,7 @@
     ]
     for copy in copies:
         copy.start()
-    bc = jnp.transpose(bc_ref[...].astype(F32), (1, 0, 2))
-    one, two = (
-        jnp.concatenate([bc[2 * k + step] for k in range(16)], axis=1) for step in range(2)
-    )
+    one, two = projections(pos_ref, bc_ref, bc2_ref)
     act1, act2 = conv(bc_hist_ref, one, two, bc_taps_ref[...])
     lane = lax.broadcasted_iota(jnp.int32, (32, 128), 1)
     column = lax.broadcasted_iota(jnp.int32, (64, 32), 1)
@@ -223,10 +217,10 @@
                 g_ref[chip, 2 * g + j] = block
 
 
-def mixer(gain, cols, bc, bc_taps, bc_hist, state):
+def mixer(pos, gain, cols, bc, bc2, bc_taps, bc_hist, state):
     return pl.pallas_call(
         mixer_kernel,
-        in_specs=[VMEM] * 5 + [HBM],
+        in_specs=[SMEM] + [VMEM] * 6 + [HBM],
         out_specs=(VMEM,) * 2,
         out_shape=(
             jax.ShapeDtypeStruct((8, 8, 24, 128), BF16),
@@ -236,7 +230,7 @@
         compiler_params=pltpu.CompilerParams(vmem_limit_bytes=STATE_MIB * MIB),
         cost_estimate=pl.CostEstimate(flops=20_000_000, bytes_accessed=9_000_000, transcendentals=100_000),
         name="mixer",
-    )(gain, cols, bc, bc_taps, bc_hist, state)
+    )(pos, gain, cols, bc, bc2, bc_taps, bc_hist, state)
 
 
 def advance_kernel(start, col_ref, b_ref, state_ref, *refs):
@@ -299,24 +293,21 @@
     )(cols, b, state, *more)
 
 
-def history_kernel(bc_ref, bc_hist_ref, out_ref):
-    bc = jnp.transpose(bc_ref[...].astype(F32), (1, 0, 2))
+def history_kernel(pos_ref, bc_ref, bc2_ref, bc_hist_ref, out_ref):
     out_ref[0] = bc_hist_ref[2]
-    for step in range(2):
-        for k in range(16):
-            out_ref[1 + step, :, 128 * k : 128 * k + 128] = bc[2 * k + step]
-
-
-def history(bc, bc_hist):
+    out_ref[1], out_ref[2] = projections(pos_ref, bc_ref, bc2_ref)
+
+
+def history(pos, bc, bc2, bc_hist):
     return pl.pallas_call(
         history_kernel,
-        in_specs=[VMEM] * 2,
+        in_specs=[SMEM] + [VMEM] * 3,
         out_specs=VMEM,
         out_shape=jax.ShapeDtypeStruct(bc_hist.shape, F32),
         compiler_params=pltpu.CompilerParams(vmem_limit_bytes=16 * MIB),
         cost_estimate=pl.CostEstimate(flops=0, bytes_accessed=900_000, transcendentals=0),
         name="history",
-    )(bc, bc_hist)
+    )(pos, bc, bc2, bc_hist)
 
 
 def output_kernel(map_ref, pos_ref, g1_ref, g2_ref, w_ref, o_ref, w_scr, l_scr):
@@ -372,20 +363,20 @@
     x = lax.dynamic_slice_in_dim(inputs.reshape(32, 8192), chip * 1024, 1024, axis=1)
     x = lax.all_to_all(jnp.broadcast_to(x[None], (8, 32, 1024)), "tp", 0, 0, tiled=True)
     partial = project(head_map, pos, x.reshape(256, 1024), w, w2, wbd, wbd2)
-    received = lax.all_to_all(partial.reshape(64, 48, 128), ("chip", "tp"), 0, 0, tiled=True)
-    summed = jnp.sum(received.reshape(8, 8, 48, 128).astype(F32), axis=0)
+    partial = partial.reshape(64, 72, 128).astype(F16)
+    received = lax.all_to_all(partial, ("chip", "tp"), 0, 0, tiled=True)
+    summed = jnp.sum(received.reshape(8, 8, 72, 128).astype(F32), axis=0) * (1.0 / SCALE)
+    low = summed[:, 32:64, :].astype(BF16)
+    low2 = swap(low)
     cols, x_hist, gain = heads_part(
         head_map, pos, a_log, dt_bias, skip_coef, conv_x, norm_gain, summed,
         conv_x_state.transpose(1, 0, 2),
     )
-    low = (summed[:, 32:36, :] + summed[:, 36:40, :]).astype(BF16).reshape(32, 128)
-    low = lax.all_to_all(
-        jnp.broadcast_to(low[None], (16, 32, 128)), ("chip", "core"), 0, 0, tiled=True
+    gated, b = mixer(
+        pos, gain, cols, low, low2, conv_bc, conv_bc_state.transpose(1, 0, 2), ssm_state,
     )
-
-    gated, b = mixer(gain, cols, low, conv_bc, conv_bc_state.transpose(1, 0, 2), ssm_state)
     gathered = lax.all_to_all(gated.reshape(64, 24, 128), ("chip", "tp"), 0, 0, tiled=True).reshape(8, 8, 24, 128)
-    bc_hist = history(low, conv_bc_state.transpose(1, 0, 2))
+    bc_hist = history(pos, low, low2, conv_bc_state.transpose(1, 0, 2))
     state = advance(cols, b, ssm_state, 0, None)
     gathered, state, bc_hist = lax.optimization_barrier((gathered, state, bc_hist))
     state = advance(cols, b, ssm_state, 2, state)

time: 100 us -> 96.7 us (0.967)
  waiting for transfers between devices: 22.4 us -> 17.8 us
  blocking collectives: 23.4 us -> 27.1 us
  starting transfers between devices: 19.5 us -> 16.6 us
    all_to_all x1 -> x0, waiting for transfers between devices: 4.39 us -> none  [per_device(): lax.all_to_all(jnp.broadcast_to(low[None], (16, 32, 128)), ('chip', 'core...]
    all_to_all x1, blocking collectives: 23.4 us -> 27.1 us  [per_device(): received = lax.all_to_all(partial, ('chip', 'tp'), 0, 0, tiled=True)]
    all_to_all x1 -> x0, starting transfers between devices: 3.51 us -> none  [per_device(): lax.all_to_all(jnp.broadcast_to(low[None], (16, 32, 128)), ('chip', 'core...]
    pallas_call x2, Pallas kernels: 7.28 us -> 8.32 us  [the longest x1 7.01 us: mixer(): pl.pallas_call(mixer_kernel, in_specs=[SMEM] + [VMEM] * 6 + [HBM], out_sp...]
  transfers between devices with their start and end apart: 7 -> 7, of which waited for: 5 -> 4; matrix products, arithmetic and copies ran while one was open for 8% -> 8% of each run, Pallas kernels for 11% -> 12%
where the time goes in v4:
time: 96.7 us; the launch traced here: 96.1 us
  blocking collectives  27.1 us (28%)
  Pallas kernels  22.6 us (23%)
  waiting for transfers between devices  17.8 us (18%)
  starting transfers between devices  16.6 us (17%)
  local copies, waits for them, and re-layouts  9.97 us (10%)
  other arithmetic  1.16 us (1%)
    all_to_all x1, blocking collectives, per_device(): received = lax.all_to_all(partial, ('chip', 'tp'), 0, 0, tiled=True)  27.1 us
    unnamed x29, local copies, waits for them, and re-layouts  9.02 us
    pallas_call x2, Pallas kernels, advance(): pl.pallas_call(functools.partial(advance_kernel, start), grid=(1,), in_sp...  8.27 us
    all_to_all x1, starting transfers between devices, per_device(): lax.all_to_all(jnp.broadcast_to(x[None], (8, 32, 1024)), 'tp', 0, 0, tile...  7.01 us
    pallas_call x1, Pallas kernels, mixer(): pl.pallas_call(mixer_kernel, in_specs=[SMEM] + [VMEM] * 6 + [HBM], out_sp...  7.01 us
    all_to_all x1, waiting for transfers between devices, per_device(): lax.all_to_all(gated.reshape(64, 24, 128), ('chip', 'tp'), 0, 0, tiled=True)  6.76 us
    all_to_all x1, starting transfers between devices, per_device(): lax.all_to_all(gated.reshape(64, 24, 128), ('chip', 'tp'), 0, 0, tiled=True)  5.86 us
    all_to_all x1, waiting for transfers between devices, per_device(): shares = lax.all_to_all(shares, 'tp', 0, 0, tiled=True)  5.06 us
  transfers between devices with their start and end apart: 7, of which 4 were waited for; matrix products, arithmetic and copies ran while one was open for 8% of the time, Pallas kernels for 12%

profile of v4, /device:TPU:0, one launch (start us, length us, event | category | flops | bytes accessed | tf_op | source)
XLA Modules:
  0.0 96.1 jit_solution(55165807707729352)
XLA Ops:
  0.6 0.0 copy-start
  0.7 0.1 collective-permute-start
  0.8 0.9 copy-done
  1.7 0.9 broadcast_in_dim.13
  2.5 7.0 %all-to-all-start = ((bf16[8,32,1024]{2,1,0:T(8,128)(2,1)}), bf16[8,32,1024]{2,1,0:T(8,128)(2,1)S(1)}, u32[]{:S(2)}, u32[]{:S(2)}) async-start(bf16[8,32,1024]{2,1,0:T(8,128)(2,1)} %broadcast_in_dim.13), calls=%async_computation | async-start | bytes 1048576 | tf_op jit(solution)/shard_map/all_to_all | solution.py:364
  9.6 0.8 copy.20
  10.4 0.1 pad.2.clone
  10.5 0.1 maximum_maximum_fusion.wbd_ref
  10.6 0.1 collective-permute-start.1
  10.7 2.1 %copy.26 = bf16[64,8,16,128]{3,1,2,0:T(8,128)(2,1)S(1)} copy(bf16[64,8,16,128]{3,2,1,0:T(8,128)(2,1)} %bitcast.35) | data formatting | bytes 4194304
  12.8 0.1 pad_add_fusion.pos_ref
  12.9 3.5 %copy.25 = bf16[64,8,16,128]{3,1,2,0:T(8,128)(2,1)} copy(bf16[64,8,16,128]{3,2,1,0:T(8,128)(2,1)} %bitcast.17) | data formatting | bytes 4194304
  16.4 4.3 %all-to-all-done = bf16[8,32,1024]{2,1,0:T(8,128)(2,1)S(1)} async-done(((bf16[8,32,1024]{2,1,0:T(8,128)(2,1)}), bf16[8,32,1024]{2,1,0:T(8,128)(2,1)S(1)}, u32[]{:S(2)}, u32[]{:S(2)}) %all-to-all-start) | async-done | bytes 524320 | tf_op jit(solution)/shard_map/all_to_all | solution.py:364
  20.6 1.6 %copy-done.1 = bf16[64,8,16,128]{3,1,2,0:T(8,128)(2,1)S(1)} copy-done((bf16[64,8,16,128]{3,1,2,0:T(8,128)(2,1)S(1)}, bf16[64,8,16,128]{3,1,2,0:T(8,128)(2,1)}, u32[]{:S(2)}) %copy-start.1) | copy-done | bytes 2097176
  22.2 2.1 %project.1 = f32[8,8,72,128]{3,2,1,0:T(8,128)S(1)} custom-call(s32[16]{0:T(128)S(1)} %copy-done.8, s32[2]{0:T(128)S(1)} %pad_add_fusion.pos_ref, bf16[256,1024]{1,0:T(8,128)(2,1)S(1)} %bitcast.26, bf16[512,2048]{1,0:T(8,128)(2,1)S(1)} %bitcast.24, bf16[512,2048]{1,0:T(8,128)(2,1)S(1)} %bitcast.25, bf16[512,384]{1,0:T(8,128)(2,1)S(1)} %maximum_maximum_fusion.wbd_ref, ...), custom_call_target="tpu_custom_call" | custom-call | flops 600000000 | bytes 5500000 | tf_op jit(solution)/shard_map/project/pallas_call | solution.py:64
  24.3 0.2 convert_element_type.15
  24.5 0.0 copy-start.4
  24.6 27.1 %all_to_all.20 = f16[64,72,128]{2,1,0:T(8,128)(2,1)S(1)} all-to-all(f16[64,72,128]{2,1,0:T(8,128)(2,1)S(1)} %bitcast.33), channel_id=1, replica_groups=mesh['chip'=8,'core'=2,'tp'=8] {'chip','tp'}, dimensions={0} | all-to-all | bytes 2359296 | tf_op jit(solution)/shard_map/all_to_all | solution.py:367
  51.7 0.2 convert_reduce_fusion
  51.9 0.1 collective-permute-start.2
  52.0 2.1 %heads_part.1 = (f32[8,64,256]{2,1,0:T(8,128)S(1)}, f32[3,16,512]{2,1,0:T(8,128)}, f32[1,512]{1,0:T(1,128)S(1)}) custom-call(s32[16]{0:T(128)S(1)} %copy-done.8, s32[2]{0:T(128)S(1)} %pad_add_fusion.pos_ref, f32[128]{0:T(128)S(1)} %copy-done.9, f32[128]{0:T(128)S(1)} %copy-done.10, f32[128]{0:T(128)S(1)} %copy-done.11, f32[5,8192]{1,0:T(8,128)S(1)} %copy-done.4, ...), custom_call_target="tpu_custom_call" | custom-call | flops 2000000 | bytes 1000000 | tf_op jit(solution)/shard_map/heads_part/pallas_call | solution.py:136
  54.2 7.0 %mixer.1 = (bf16[8,8,24,128]{3,2,1,0:T(8,128)(2,1)}, f32[4,32,256]{2,1,0:T(8,128)S(1)}) custom-call(s32[2]{0:T(128)S(1)} %pad_add_fusion.pos_ref, f32[1,512]{1,0:T(1,128)S(1)} %get-tuple-element.12.gain_ref, f32[8,64,256]{2,1,0:T(8,128)S(1)} %get-tuple-element.13.col_ref, bf16[8,32,128]{2,1,0:T(8,128)(2,1)S(1)} %slice.7.bc_ref, ...), custom_call_target="tpu_custom_call" | custom-call | flops 20000000 | bytes 9000000 | tf_op jit(solution)/shard_map/mixer/pallas_call | solution.py:221
  61.2 5.9 %all-to-all-start.2 = ((bf16[64,24,128]{2,1,0:T(8,128)(2,1)}), bf16[64,24,128]{2,1,0:T(8,128)(2,1)S(1)}, u32[]{:S(2)}, u32[]{:S(2)}) async-start(bf16[64,24,128]{2,1,0:T(8,128)(2,1)} %bitcast.9), calls=%async_computation.2 | async-start | bytes 786432 | tf_op jit(solution)/shard_map/all_to_all | solution.py:378
  67.1 1.3 %history.1 = f32[3,16,2048]{2,1,0:T(8,128)} custom-call(s32[2]{0:T(128)S(1)} %pad_add_fusion.pos_ref, bf16[8,32,128]{2,1,0:T(8,128)(2,1)S(1)} %slice.7.bc_ref, bf16[8,32,128]{2,1,0:T(8,128)(2,1)S(1)} %collective-permute-done.2.bc2_ref, f32[3,16,2048]{2,1,0:T(8,128)S(1)} %bitcast.30), custom_call_target="tpu_custom_call" | custom-call | bytes 900000 | tf_op jit(solution)/shard_map/history/pallas_call | solution.py:302
  68.4 4.2 %advance.2.refs_0_ = f32[16,8,64,256]{3,2,1,0:T(8,128)} custom-call(f32[8,64,256]{2,1,0:T(8,128)S(1)} %get-tuple-element.13.col_ref, f32[4,32,256]{2,1,0:T(8,128)S(1)} %get-tuple-element.15.b_ref, f32[16,8,64,256]{3,2,1,0:T(8,128)} %state_ref.5), custom_call_target="tpu_custom_call" | custom-call | flops 6000000 | bytes 8500000 | tf_op jit(solution)/shard_map/advance/pallas_call | solution.py:274
  72.6 6.8 %all-to-all-done.2 = bf16[64,24,128]{2,1,0:T(8,128)(2,1)S(1)} async-done(((bf16[64,24,128]{2,1,0:T(8,128)(2,1)}), bf16[64,24,128]{2,1,0:T(8,128)(2,1)S(1)}, u32[]{:S(2)}, u32[]{:S(2)}) %all-to-all-start.2) | async-done | bytes 393248 | tf_op jit(solution)/shard_map/all_to_all | solution.py:378
  79.3 1.7 %collective-permute-done.3.g2_ref = bf16[8,8,24,128]{3,2,1,0:T(8,128)(2,1)S(1)} collective-permute-done((bf16[8,8,24,128]{3,2,1,0:T(8,128)(2,1)S(1)}, bf16[8,8,24,128]{3,2,1,0:T(8,128)(2,1)S(1)}, u32[]{:S(2)}, u32[]{:S(2)}) %collective-permute-start.3) | collective-permute-done | bytes 393248 | tf_op jit(solution)/shard_map/ppermute | solution.py:358
  81.1 1.8 %output.1 = bf16[8,32,512]{2,1,0:T(8,128)(2,1)} custom-call(s32[16]{0:T(128)S(1)} %copy-done.8, s32[2]{0:T(128)S(1)} %pad_add_fusion.pos_ref, bf16[8,8,24,128]{3,2,1,0:T(8,128)(2,1)S(1)} %bitcast.28, bf16[8,8,24,128]{3,2,1,0:T(8,128)(2,1)S(1)} %collective-permute-done.3.g2_ref, bf16[16,64,512]{2,1,0:T(8,128)(2,1)S(1)} %copy-done.3), custom_call_target="tpu_custom_call" | custom-call | flops 270000000 | bytes 2500000 | tf_op jit(solution)/shard_map/output/pallas_call | solution.py:338
  82.8 3.5 %all-to-all-start.3 = ((bf16[8,32,512]{2,1,0:T(8,128)(2,1)}), bf16[8,32,512]{2,1,0:T(8,128)(2,1)S(1)}, u32[]{:S(2)}, u32[]{:S(2)}) async-start(bf16[8,32,512]{2,1,0:T(8,128)(2,1)} %output.1), calls=%async_computation.3 | async-start | bytes 524288 | tf_op jit(solution)/shard_map/all_to_all | solution.py:384
  86.3 4.1 %advance.3 = f32[16,8,64,256]{3,2,1,0:T(8,128)} custom-call(f32[8,64,256]{2,1,0:T(8,128)S(1)} %get-tuple-element.13.col_ref, f32[4,32,256]{2,1,0:T(8,128)S(1)} %get-tuple-element.15.b_ref, f32[16,8,64,256]{3,2,1,0:T(8,128)} %state_ref.5, f32[16,8,64,256]{3,2,1,0:T(8,128)} %advance.2.refs_0_), custom_call_target="tpu_custom_call", output_to_operand_aliasing={{}: (3, {})} | custom-call | flops 6000000 | bytes 8500000 | tf_op jit(solution)/shard_map/advance/pallas_call | solution.py:274
  90.4 5.1 %all-to-all-done.3 = bf16[8,32,512]{2,1,0:T(8,128)(2,1)S(1)} async-done(((bf16[8,32,512]{2,1,0:T(8,128)(2,1)}), bf16[8,32,512]{2,1,0:T(8,128)(2,1)S(1)}, u32[]{:S(2)}, u32[]{:S(2)}) %all-to-all-start.3) | async-done | bytes 262176 | tf_op jit(solution)/shard_map/all_to_all | solution.py:384
  95.5 0.7 reduce_sum.22
  (30 shorter events, 0.1 us)
Async XLA Ops:
  0.6 1.0 %copy-start = (bf16[2,16,8192]{2,1,0:T(8,128)(2,1)S(1)}, bf16[2,16,8192]{2,1,0:T(8,128)(2,1)}, u32[]{:S(2)}) copy-start(bf16[2,16,8192]{2,1,0:T(8,128)(2,1)} %param.15) | copy-start | bytes 1572868
  0.6 9.8 %copy-start.12 = (bf16[512,256]{1,0:T(8,128)(2,1)S(1)}, bf16[512,256]{1,0:T(8,128)(2,1)}, u32[]{:S(2)}) copy-start(bf16[512,256]{1,0:T(8,128)(2,1)} %param.18) | copy-start | bytes 786436
  0.7 12.2 %collective-permute-start = (bf16[512,16,128]{2,1,0:T(8,128)(2,1)}, bf16[512,16,128]{2,1,0:T(8,128)(2,1)}, u32[]{:S(2)}, u32[]{:S(2)}) collective-permute-start(bf16[512,16,128]{2,1,0:T(8,128)(2,1)} %param.16), channel_id=1, source_target_pairs={{0,8},{8,0},{1,9},{9,1},{2,10},{10,2},{3,11},{11,3},{4,12},{12,4},... | collective-permute-start | bytes 6291464 | tf_op jit(solution)/shard_map/ppermute | solution.py:358
  2.5 18.1 %all-to-all-start = ((bf16[8,32,1024]{2,1,0:T(8,128)(2,1)}), bf16[8,32,1024]{2,1,0:T(8,128)(2,1)S(1)}, u32[]{:S(2)}, u32[]{:S(2)}) async-start(bf16[8,32,1024]{2,1,0:T(8,128)(2,1)} %broadcast_in_dim.13), calls=%async_computation | async-start | bytes 1048576 | tf_op jit(solution)/shard_map/all_to_all | solution.py:364
  10.6 5.8 %collective-permute-start.1 = (bf16[512,384]{1,0:T(8,128)(2,1)S(1)}, bf16[512,384]{1,0:T(8,128)(2,1)}, u32[]{:S(2)}, u32[]{:S(2)}) collective-permute-start(bf16[512,384]{1,0:T(8,128)(2,1)S(1)} %maximum_maximum_fusion.wbd_ref), channel_id=1, source_target_pairs={{0,8},{8,0},{1,9},{9,1},{2,10},{10,2},{3,11},{11,3},{4,12},{12,4},... | collective-permute-start | bytes 1179656 | tf_op jit(solution)/shard_map/ppermute | solution.py:358
  12.9 7.7 %copy-start.8 = (s32[16]{0:T(128)S(1)}, s32[16]{0:T(128)}, u32[]{:S(2)}) copy-start(s32[16]{0:T(128)} %map_ref.5) | copy-start | bytes 196
  20.6 1.6 %copy-start.1 = (bf16[64,8,16,128]{3,1,2,0:T(8,128)(2,1)S(1)}, bf16[64,8,16,128]{3,1,2,0:T(8,128)(2,1)}, u32[]{:S(2)}) copy-start(bf16[64,8,16,128]{3,1,2,0:T(8,128)(2,1)} %copy.25) | copy-start | bytes 6291460
  24.5 27.5 %copy-start.4 = (f32[5,8192]{1,0:T(8,128)S(1)}, f32[5,8192]{1,0:T(8,128)}, u32[]{:S(2)}) copy-start(f32[5,8192]{1,0:T(8,128)} %taps_ref.1) | copy-start | bytes 491524
  24.5 27.5 %copy-start.5 = (f32[16,3,512]{2,0,1:T(8,128)S(1)}, f32[16,3,512]{2,0,1:T(8,128)}, u32[]{:S(2)}) copy-start(f32[16,3,512]{2,0,1:T(8,128)} %param.28) | copy-start | bytes 294916
  24.5 27.5 %copy-start.7 = (f32[8192]{0:T(1024)S(1)}, f32[8192]{0:T(1024)}, u32[]{:S(2)}) copy-start(f32[8192]{0:T(1024)} %param.26) | copy-start | bytes 98308
  24.5 27.5 %copy-start.9 = (f32[128]{0:T(128)S(1)}, f32[128]{0:T(128)}, u32[]{:S(2)}) copy-start(f32[128]{0:T(128)} %a_ref.1) | copy-start | bytes 1540
  24.5 27.5 %copy-start.10 = (f32[128]{0:T(128)S(1)}, f32[128]{0:T(128)}, u32[]{:S(2)}) copy-start(f32[128]{0:T(128)} %bias_ref.1) | copy-start | bytes 1540
  24.5 27.5 %copy-start.11 = (f32[128]{0:T(128)S(1)}, f32[128]{0:T(128)}, u32[]{:S(2)}) copy-start(f32[128]{0:T(128)} %skip_ref.1) | copy-start | bytes 1540
  24.5 29.6 %copy-start.2 = (f32[16,3,2048]{2,0,1:T(8,128)S(1)}, f32[16,3,2048]{2,0,1:T(8,128)}, u32[]{:S(2)}) copy-start(f32[16,3,2048]{2,0,1:T(8,128)} %param.29) | copy-start | bytes 1179652
  24.6 29.6 %copy-start.6 = (f32[5,2048]{1,0:T(8,128)S(1)}, f32[5,2048]{1,0:T(8,128)}, u32[]{:S(2)}) copy-start(f32[5,2048]{1,0:T(8,128)} %bc_taps_ref.1) | copy-start | bytes 122884
  51.9 2.3 %collective-permute-start.2 = (bf16[8,32,128]{2,1,0:T(8,128)(2,1)S(1)}, bf16[8,32,128]{2,1,0:T(8,128)(2,1)S(1)}, u32[]{:S(2)}, u32[]{:S(2)}) collective-permute-start(bf16[8,32,128]{2,1,0:T(8,128)(2,1)S(1)} %slice.7.bc_ref), channel_id=1, source_target_pairs={{0,8},{8,0},{1,9},{9,1},{2,10},{10,2},{3,11},{11,3},{4,12},{12,4},... | collective-permute-start | bytes 196616 | tf_op jit(solution)/shard_map/ppermute | solution.py:358
  61.2 18.1 %all-to-all-start.2 = ((bf16[64,24,128]{2,1,0:T(8,128)(2,1)}), bf16[64,24,128]{2,1,0:T(8,128)(2,1)S(1)}, u32[]{:S(2)}, u32[]{:S(2)}) async-start(bf16[64,24,128]{2,1,0:T(8,128)(2,1)} %bitcast.9), calls=%async_computation.2 | async-start | bytes 786432 | tf_op jit(solution)/shard_map/all_to_all | solution.py:378
  68.4 12.7 %copy-start.3 = (bf16[16,64,512]{2,1,0:T(8,128)(2,1)S(1)}, bf16[16,64,512]{2,1,0:T(8,128)(2,1)}, u32[]{:S(2)}) copy-start(bf16[16,64,512]{2,1,0:T(8,128)(2,1)} %w_ref.1) | copy-start | bytes 3145732
  79.3 1.7 %collective-permute-start.3 = (bf16[8,8,24,128]{3,2,1,0:T(8,128)(2,1)S(1)}, bf16[8,8,24,128]{3,2,1,0:T(8,128)(2,1)S(1)}, u32[]{:S(2)}, u32[]{:S(2)}) collective-permute-start(bf16[8,8,24,128]{3,2,1,0:T(8,128)(2,1)S(1)} %bitcast.27), channel_id=1, source_target_pairs={{0,8},{8,0},{1,9},{9,1},{2,10},{10,2},{3,11},{11,3},{4,12},{12,4},... | collective-permute-start | bytes 1179656 | tf_op jit(solution)/shard_map/ppermute | solution.py:358
  82.8 12.6 %all-to-all-start.3 = ((bf16[8,32,512]{2,1,0:T(8,128)(2,1)}), bf16[8,32,512]{2,1,0:T(8,128)(2,1)S(1)}, u32[]{:S(2)}, u32[]{:S(2)}) async-start(bf16[8,32,512]{2,1,0:T(8,128)(2,1)} %output.1), calls=%async_computation.3 | async-start | bytes 524288 | tf_op jit(solution)/shard_map/all_to_all | solution.py:384

commit v5 on v4

--- a/solution.py
+++ b/solution.py
@@ -22,10 +22,9 @@
     return v * jax.nn.sigmoid(v)
 
 
-def project_kernel(map_ref, pos_ref, x_ref, w_ref, w2_ref, wbd_ref, wbd2_ref, o_ref, dt_scr):
+def project_kernel(map_ref, pos_ref, x_ref, x2_ref, w_ref, w2_ref, wbd_ref, wbd2_ref, o_ref, dt_scr):
     core = pos_ref[1]
-    x1 = x_ref[:, pl.ds(pl.multiple_of(core * 512, 512), 512)]
-    x2 = x_ref[:, pl.ds(pl.multiple_of((1 - core) * 512, 512), 512)]
+    x1, x2 = x_ref[...], x2_ref[...]
 
     def dot(w1, w2):
         return jnp.dot(x1, w1, preferred_element_type=F32) + jnp.dot(
@@ -60,17 +59,17 @@
 VMEM = pl.BlockSpec(memory_space=pltpu.VMEM)
 
 
-def project(head_map, pos, x, w, w2, wbd, wbd2):
+def project(head_map, pos, x, x2, w, w2, wbd, wbd2):
     return pl.pallas_call(
         project_kernel,
-        in_specs=[SMEM] * 2 + [VMEM] * 5,
+        in_specs=[SMEM] * 2 + [VMEM] * 6,
         out_specs=VMEM,
         out_shape=jax.ShapeDtypeStruct((8, 8, 72, 128), F32),
         scratch_shapes=[pltpu.VMEM((128, 256), F32)],
         compiler_params=pltpu.CompilerParams(vmem_limit_bytes=16 * MIB),
         cost_estimate=pl.CostEstimate(flops=600_000_000, bytes_accessed=5_500_000, transcendentals=0),
         name="project",
-    )(head_map, pos, x, w, w2, wbd, wbd2)
+    )(head_map, pos, x, x2, w, w2, wbd, wbd2)
 
 
 def conv(hist_ref, one, two, taps):
@@ -310,23 +309,31 @@
     )(pos, bc, bc2, bc_hist)
 
 
-def output_kernel(map_ref, pos_ref, g1_ref, g2_ref, w_ref, o_ref, w_scr, l_scr):
+def share_kernel(mine, map_ref, pos_ref, g_ref, w_ref, *refs):
+    w_scr, l_scr = refs[-2:]
+    which = pos_ref[1] if mine else 1 - pos_ref[1]
     sums = jnp.zeros((8, 8, 128), F32)
-    core = pos_ref[1]
-    for s in range(16):
-        which = core if s % 2 == 0 else 1 - core
-        w_scr[64 * s : 64 * s + 64, :] = w_ref[map_ref[s // 2 * 2 + which]]
-    for m in range(8):
-        even, odd = g1_ref[m].astype(F32), g2_ref[m].astype(F32)
+    for s in range(8):
+        w_scr[64 * s : 64 * s + 64, :] = w_ref[map_ref[2 * s + which]]
+    for m in range(4):
+        even, odd = g_ref[2 * m].astype(F32), g_ref[2 * m + 1].astype(F32)
         sums += even[:, 16:24, :] + odd[:, 16:24, :]
         even = even[:, 0:16, :].reshape(128, 128)
         odd = odd[:, 0:16, :].reshape(128, 128)
         cols = slice(128 * m, 128 * m + 128)
         l_scr[0:128, cols] = jnp.concatenate([even[:, 0:64], odd[:, 0:64]], axis=1).astype(BF16)
         l_scr[128:256, cols] = jnp.concatenate([even[:, 64:], odd[:, 64:]], axis=1).astype(BF16)
+    out = jnp.dot(l_scr[...], w_scr[...], preferred_element_type=F32)
+    if mine:
+        out_ref, sums_ref = refs[:2]
+        out_ref[...] = out
+        sums_ref[...] = sums
+        return
+    out1_ref, sums1_ref, o_ref = refs[:3]
+    out += out1_ref[...]
+    sums += sums1_ref[...]
     total = sums[:, 0, :] + sums[:, 1, :]
     scale = lax.rsqrt(total / 2048.0 + EPSILON).T
-    out = jnp.dot(l_scr[...], w_scr[...], preferred_element_type=F32)
     for t in range(8):
         one = slice(16 * t, 16 * t + 16)
         two = slice(128 + 16 * t, 144 + 16 * t)
@@ -334,17 +341,21 @@
         o_ref[t, 16:32, :] = (out[two] * scale[16:32, t : t + 1]).astype(BF16)
 
 
-def output(head_map, pos, gathered, other, w_out):
-    return pl.pallas_call(
-        output_kernel,
-        in_specs=[SMEM] * 2 + [VMEM] * 3,
-        out_specs=VMEM,
-        out_shape=jax.ShapeDtypeStruct((8, 32, 512), BF16),
-        scratch_shapes=[pltpu.VMEM((1024, 512), BF16), pltpu.VMEM((256, 1024), BF16)],
+def share(mine, head_map, pos, gathered, w_out, *first):
+    if mine:
+        shapes = (jax.ShapeDtypeStruct((256, 512), F32), jax.ShapeDtypeStruct((8, 8, 128), F32))
+    else:
+        shapes = jax.ShapeDtypeStruct((8, 32, 512), BF16)
+    return pl.pallas_call(
+        functools.partial(share_kernel, mine),
+        in_specs=[SMEM] * 2 + [VMEM] * (2 + len(first)),
+        out_specs=(VMEM, VMEM) if mine else VMEM,
+        out_shape=shapes,
+        scratch_shapes=[pltpu.VMEM((512, 512), BF16), pltpu.VMEM((256, 512), BF16)],
         compiler_params=pltpu.CompilerParams(vmem_limit_bytes=16 * MIB),
-        cost_estimate=pl.CostEstimate(flops=270_000_000, bytes_accessed=2_500_000, transcendentals=0),
-        name="output",
-    )(head_map, pos, gathered, other, w_out)
+        cost_estimate=pl.CostEstimate(flops=140_000_000, bytes_accessed=1_500_000, transcendentals=0),
+        name="share",
+    )(head_map, pos, gathered, w_out, *first)
 
 
 def per_device(
@@ -360,9 +371,10 @@
     w = w_xz.reshape(512, 2048)
     wbd = jnp.concatenate([w_bc, w_dt, jnp.zeros((512, 112), BF16)], axis=1)
     w2, wbd2 = swap(w_xz).reshape(512, 2048), swap(wbd)
-    x = lax.dynamic_slice_in_dim(inputs.reshape(32, 8192), chip * 1024, 1024, axis=1)
-    x = lax.all_to_all(jnp.broadcast_to(x[None], (8, 32, 1024)), "tp", 0, 0, tiled=True)
-    partial = project(head_map, pos, x.reshape(256, 1024), w, w2, wbd, wbd2)
+    x = lax.dynamic_slice_in_dim(inputs.reshape(32, 8192), chip * 1024 + core * 512, 512, axis=1)
+    x = lax.all_to_all(jnp.broadcast_to(x[None], (8, 32, 512)), "tp", 0, 0, tiled=True)
+    x, w = lax.optimization_barrier((x.reshape(256, 512), w))
+    partial = project(head_map, pos, x, swap(x), w, w2, wbd, wbd2)
     partial = partial.reshape(64, 72, 128).astype(F16)
     received = lax.all_to_all(partial, ("chip", "tp"), 0, 0, tiled=True)
     summed = jnp.sum(received.reshape(8, 8, 72, 128).astype(F32), axis=0) * (1.0 / SCALE)
@@ -380,7 +392,9 @@
     state = advance(cols, b, ssm_state, 0, None)
     gathered, state, bc_hist = lax.optimization_barrier((gathered, state, bc_hist))
     state = advance(cols, b, ssm_state, 2, state)
-    shares = output(head_map, pos, gathered, swap(gathered), w_out)
+    other = swap(gathered)
+    first = share(True, head_map, pos, gathered, w_out)
+    shares = share(False, head_map, pos, other, w_out, *first)
     shares = lax.all_to_all(shares, "tp", 0, 0, tiled=True)
     mixed = jnp.sum(shares.astype(F32), axis=0).astype(BF16).reshape(2, 16, 512)
     return mixed, state, x_hist.transpose(1, 0, 2), bc_hist.transpose(1, 0, 2)

time: 96.7 us -> 94.7 us (0.979)
  local copies, waits for them, and re-layouts: 9.97 us -> 6.93 us
    unnamed x29 -> x25, local copies, waits for them, and re-layouts: 9.02 us -> 6.11 us
    pallas_call x2 -> x3, Pallas kernels: 3.86 us -> 4.59 us  [the longest x2 2.48 us: share(): pl.pallas_call(functools.partial(share_kernel, mine), in_specs=[SMEM] * 2...]
  transfers between devices with their start and end apart: 7 -> 8, of which waited for: 4 -> 4; matrix products, arithmetic and copies ran while one was open for 8% -> 7% of each run, Pallas kernels for 12% -> 13%
where the time goes in v5:
time: 94.7 us; the launch traced here: 94 us
  blocking collectives  26.9 us (28%)
  Pallas kernels  23.3 us (25%)
  waiting for transfers between devices  17.2 us (18%)
  starting transfers between devices  16.7 us (18%)
  local copies, waits for them, and re-layouts  6.93 us (7%)
  other arithmetic  2.1 us (2%)
    all_to_all x1, blocking collectives, per_device(): received = lax.all_to_all(partial, ('chip', 'tp'), 0, 0, tiled=True)  26.9 us
    pallas_call x2, Pallas kernels, advance(): pl.pallas_call(functools.partial(advance_kernel, start), grid=(1,), in_sp...  8.23 us
    all_to_all x1, starting transfers between devices, per_device(): lax.all_to_all(jnp.broadcast_to(x[None], (8, 32, 512)), 'tp', 0, 0, tiled...  7.01 us
    pallas_call x1, Pallas kernels, mixer(): pl.pallas_call(mixer_kernel, in_specs=[SMEM] + [VMEM] * 6 + [HBM], out_sp...  7.01 us
    all_to_all x1, waiting for transfers between devices, per_device(): lax.all_to_all(gated.reshape(64, 24, 128), ('chip', 'tp'), 0, 0, tiled=True)  6.79 us
    unnamed x25, local copies, waits for them, and re-layouts  6.11 us
    all_to_all x1, starting transfers between devices, per_device(): lax.all_to_all(gated.reshape(64, 24, 128), ('chip', 'tp'), 0, 0, tiled=True)  5.92 us
    all_to_all x1, waiting for transfers between devices, per_device(): shares = lax.all_to_all(shares, 'tp', 0, 0, tiled=True)  5.08 us
  transfers between devices with their start and end apart: 8, of which 4 were waited for; matrix products, arithmetic and copies ran while one was open for 7% of the time, Pallas kernels for 13%

profile of v5, /device:TPU:0, one launch (start us, length us, event | category | flops | bytes accessed | tf_op | source)
XLA Modules:
  0.0 94.0 jit_solution(7628536820363875094)
XLA Ops:
  0.6 0.0 copy-start
  0.6 0.1 collective-permute-start.1
  0.8 0.9 copy-done
  1.7 0.7 broadcast_in_dim.13
  2.4 7.0 %all-to-all-start = ((bf16[8,32,512]{2,1,0:T(8,128)(2,1)}), bf16[8,32,512]{2,1,0:T(8,128)(2,1)S(1)}, u32[]{:S(2)}, u32[]{:S(2)}) async-start(bf16[8,32,512]{2,1,0:T(8,128)(2,1)} %broadcast_in_dim.13), calls=%async_computation | async-start | bytes 524288 | tf_op jit(solution)/shard_map/all_to_all | solution.py:375
  9.4 0.8 copy.20
  10.3 0.1 pad.2.clone
  10.3 1.0 %maximum_maximum_fusion.wbd_ref = bf16[512,384]{1,0:T(8,128)(2,1)S(1)} fusion(bf16[512,16]{1,0:T(8,128)(2,1)S(1)} %copy.20, bf16[512,256]{1,0:T(8,128)(2,1)} %param.18, bf16[384]{0:T(512)(128)(2,1)S(1)} %pad.2.clone), kind=kLoop, calls=%fused_computation.3 | loop fusion | flops 1179648 | bytes 672512 | tf_op jit(solution)/shard_map/concatenate | solution.py:372
  11.4 0.1 collective-permute-start.2
  11.5 2.1 %copy.26 = bf16[64,8,16,128]{3,1,2,0:T(8,128)(2,1)S(1)} copy(bf16[64,8,16,128]{3,2,1,0:T(8,128)(2,1)} %bitcast.36) | data formatting | bytes 4194304
  13.6 4.5 %all-to-all-done = bf16[8,32,512]{2,1,0:T(8,128)(2,1)S(1)} async-done(((bf16[8,32,512]{2,1,0:T(8,128)(2,1)}), bf16[8,32,512]{2,1,0:T(8,128)(2,1)S(1)}, u32[]{:S(2)}, u32[]{:S(2)}) %all-to-all-start) | async-done | bytes 262176 | tf_op jit(solution)/shard_map/all_to_all | solution.py:375
  18.2 0.1 pad_add_fusion.pos_ref
  18.2 2.1 %copy.25 = bf16[64,8,16,128]{3,1,2,0:T(8,128)(2,1)S(1)} copy(bf16[64,8,16,128]{3,2,1,0:T(8,128)(2,1)} %bitcast.17) | data formatting | bytes 4194304
  20.4 2.1 %project.1 = f32[8,8,72,128]{3,2,1,0:T(8,128)S(1)} custom-call(s32[16]{0:T(128)S(1)} %copy-done.7, s32[2]{0:T(128)S(1)} %pad_add_fusion.pos_ref, bf16[256,512]{1,0:T(8,128)(2,1)S(1)} %bitcast.31, bf16[256,512]{1,0:T(8,128)(2,1)S(1)} %collective-permute-done.x2_ref, bf16[512,2048]{1,0:T(8,128)(2,1)S(1)} %bitcast.24, bf16[512,2048]{1,0:T(8,128)(2,1)S(1)} %bitcast.25, ...), custom_call_target="tpu_custom_call" | custom-call | flops 600000000 | bytes 5500000 | tf_op jit(solution)/shard_map/project/pallas_call | solution.py:63
  22.5 0.2 convert_element_type.15
  22.7 0.0 copy-start.3
  22.8 26.9 %all_to_all.20 = f16[64,72,128]{2,1,0:T(8,128)(2,1)S(1)} all-to-all(f16[64,72,128]{2,1,0:T(8,128)(2,1)S(1)} %bitcast.34), channel_id=1, replica_groups=mesh['chip'=8,'core'=2,'tp'=8] {'chip','tp'}, dimensions={0} | all-to-all | bytes 2359296 | tf_op jit(solution)/shard_map/all_to_all | solution.py:379
  49.7 0.2 convert_reduce_fusion
  49.9 0.1 collective-permute-start.3
  50.1 2.1 %heads_part.1 = (f32[8,64,256]{2,1,0:T(8,128)S(1)}, f32[3,16,512]{2,1,0:T(8,128)}, f32[1,512]{1,0:T(1,128)S(1)}) custom-call(s32[16]{0:T(128)S(1)} %copy-done.7, s32[2]{0:T(128)S(1)} %pad_add_fusion.pos_ref, f32[128]{0:T(128)S(1)} %copy-done.8, f32[128]{0:T(128)S(1)} %copy-done.9, f32[128]{0:T(128)S(1)} %copy-done.10, f32[5,8192]{1,0:T(8,128)S(1)} %copy-done.3, ...), custom_call_target="tpu_custom_call" | custom-call | flops 2000000 | bytes 1000000 | tf_op jit(solution)/shard_map/heads_part/pallas_call | solution.py:135
  52.2 7.0 %mixer.1 = (bf16[8,8,24,128]{3,2,1,0:T(8,128)(2,1)}, f32[4,32,256]{2,1,0:T(8,128)S(1)}) custom-call(s32[2]{0:T(128)S(1)} %pad_add_fusion.pos_ref, f32[1,512]{1,0:T(1,128)S(1)} %get-tuple-element.18.gain_ref, f32[8,64,256]{2,1,0:T(8,128)S(1)} %get-tuple-element.19.col_ref, bf16[8,32,128]{2,1,0:T(8,128)(2,1)S(1)} %slice.7.bc_ref, ...), custom_call_target="tpu_custom_call" | custom-call | flops 20000000 | bytes 9000000 | tf_op jit(solution)/shard_map/mixer/pallas_call | solution.py:220
  59.2 5.9 %all-to-all-start.2 = ((bf16[64,24,128]{2,1,0:T(8,128)(2,1)}), bf16[64,24,128]{2,1,0:T(8,128)(2,1)S(1)}, u32[]{:S(2)}, u32[]{:S(2)}) async-start(bf16[64,24,128]{2,1,0:T(8,128)(2,1)} %bitcast.9), calls=%async_computation.2 | async-start | bytes 786432 | tf_op jit(solution)/shard_map/all_to_all | solution.py:390
  65.2 1.3 %history.1 = f32[3,16,2048]{2,1,0:T(8,128)} custom-call(s32[2]{0:T(128)S(1)} %pad_add_fusion.pos_ref, bf16[8,32,128]{2,1,0:T(8,128)(2,1)S(1)} %slice.7.bc_ref, bf16[8,32,128]{2,1,0:T(8,128)(2,1)S(1)} %collective-permute-done.3.bc2_ref, f32[3,16,2048]{2,1,0:T(8,128)S(1)} %bitcast.29), custom_call_target="tpu_custom_call" | custom-call | bytes 900000 | tf_op jit(solution)/shard_map/history/pallas_call | solution.py:301
  66.5 4.2 %advance.2.refs_0_ = f32[16,8,64,256]{3,2,1,0:T(8,128)} custom-call(f32[8,64,256]{2,1,0:T(8,128)S(1)} %get-tuple-element.19.col_ref, f32[4,32,256]{2,1,0:T(8,128)S(1)} %get-tuple-element.21.b_ref, f32[16,8,64,256]{3,2,1,0:T(8,128)} %state_ref.5), custom_call_target="tpu_custom_call" | custom-call | flops 6000000 | bytes 8500000 | tf_op jit(solution)/shard_map/advance/pallas_call | solution.py:273
  70.6 6.8 %all-to-all-done.2 = bf16[64,24,128]{2,1,0:T(8,128)(2,1)S(1)} async-done(((bf16[64,24,128]{2,1,0:T(8,128)(2,1)}), bf16[64,24,128]{2,1,0:T(8,128)(2,1)S(1)}, u32[]{:S(2)}, u32[]{:S(2)}) %all-to-all-start.2) | async-done | bytes 393248 | tf_op jit(solution)/shard_map/all_to_all | solution.py:390
  77.4 0.9 share.2
  78.3 0.8 collective-permute-done.4.g_ref
  79.1 1.6 %share.3 = bf16[8,32,512]{2,1,0:T(8,128)(2,1)} custom-call(s32[16]{0:T(128)S(1)} %copy-done.7, s32[2]{0:T(128)S(1)} %pad_add_fusion.pos_ref, bf16[8,8,24,128]{3,2,1,0:T(8,128)(2,1)S(1)} %collective-permute-done.4.g_ref, bf16[16,64,512]{2,1,0:T(8,128)(2,1)S(1)} %copy-done.1, f32[256,512]{1,0:T(8,128)S(1)} %get-tuple-element.23.refs_0_, ...), custom_call_target="tpu_custom_call" | custom-call | flops 140000000 | bytes 1500000 | tf_op jit(solution)/shard_map/share/pallas_call | solution.py:349
  80.7 3.5 %all-to-all-start.3 = ((bf16[8,32,512]{2,1,0:T(8,128)(2,1)}), bf16[8,32,512]{2,1,0:T(8,128)(2,1)S(1)}, u32[]{:S(2)}, u32[]{:S(2)}) async-start(bf16[8,32,512]{2,1,0:T(8,128)(2,1)} %share.3), calls=%async_computation.3 | async-start | bytes 524288 | tf_op jit(solution)/shard_map/all_to_all | solution.py:398
  84.2 4.1 %advance.3 = f32[16,8,64,256]{3,2,1,0:T(8,128)} custom-call(f32[8,64,256]{2,1,0:T(8,128)S(1)} %get-tuple-element.19.col_ref, f32[4,32,256]{2,1,0:T(8,128)S(1)} %get-tuple-element.21.b_ref, f32[16,8,64,256]{3,2,1,0:T(8,128)} %state_ref.5, f32[16,8,64,256]{3,2,1,0:T(8,128)} %advance.2.refs_0_), custom_call_target="tpu_custom_call", output_to_operand_aliasing={{}: (3, {})} | custom-call | flops 6000000 | bytes 8500000 | tf_op jit(solution)/shard_map/advance/pallas_call | solution.py:273
  88.3 5.1 %all-to-all-done.3 = bf16[8,32,512]{2,1,0:T(8,128)(2,1)S(1)} async-done(((bf16[8,32,512]{2,1,0:T(8,128)(2,1)}), bf16[8,32,512]{2,1,0:T(8,128)(2,1)S(1)}, u32[]{:S(2)}, u32[]{:S(2)}) %all-to-all-start.3) | async-done | bytes 262176 | tf_op jit(solution)/shard_map/all_to_all | solution.py:398
  93.4 0.7 reduce_sum.22
  (29 shorter events, 0.1 us)
Async XLA Ops:
  0.6 1.0 %copy-start = (bf16[2,16,8192]{2,1,0:T(8,128)(2,1)S(1)}, bf16[2,16,8192]{2,1,0:T(8,128)(2,1)}, u32[]{:S(2)}) copy-start(bf16[2,16,8192]{2,1,0:T(8,128)(2,1)} %param.15) | copy-start | bytes 1572868
  0.6 17.6 %collective-permute-start.1 = (bf16[512,16,128]{2,1,0:T(8,128)(2,1)}, bf16[512,16,128]{2,1,0:T(8,128)(2,1)}, u32[]{:S(2)}, u32[]{:S(2)}) collective-permute-start(bf16[512,16,128]{2,1,0:T(8,128)(2,1)} %param.16), channel_id=1, source_target_pairs={{0,8},{8,0},{1,9},{9,1},{2,10},{10,2},{3,11},{11,3},{4,12},{12,4},... | collective-permute-start | bytes 6291464 | tf_op jit(solution)/shard_map/ppermute | solution.py:369
  2.4 15.7 %all-to-all-start = ((bf16[8,32,512]{2,1,0:T(8,128)(2,1)}), bf16[8,32,512]{2,1,0:T(8,128)(2,1)S(1)}, u32[]{:S(2)}, u32[]{:S(2)}) async-start(bf16[8,32,512]{2,1,0:T(8,128)(2,1)} %broadcast_in_dim.13), calls=%async_computation | async-start | bytes 524288 | tf_op jit(solution)/shard_map/all_to_all | solution.py:375
  11.4 9.0 %collective-permute-start.2 = (bf16[512,384]{1,0:T(8,128)(2,1)S(1)}, bf16[512,384]{1,0:T(8,128)(2,1)}, u32[]{:S(2)}, u32[]{:S(2)}) collective-permute-start(bf16[512,384]{1,0:T(8,128)(2,1)S(1)} %maximum_maximum_fusion.wbd_ref), channel_id=1, source_target_pairs={{0,8},{8,0},{1,9},{9,1},{2,10},{10,2},{3,11},{11,3},{4,12},{12,4},... | collective-permute-start | bytes 1179656 | tf_op jit(solution)/shard_map/ppermute | solution.py:369
  18.2 2.2 %collective-permute-start = (bf16[256,512]{1,0:T(8,128)(2,1)S(1)}, bf16[256,512]{1,0:T(8,128)(2,1)S(1)}, u32[]{:S(2)}, u32[]{:S(2)}) collective-permute-start(bf16[256,512]{1,0:T(8,128)(2,1)S(1)} %bitcast.30), channel_id=1, source_target_pairs={{0,8},{8,0},{1,9},{9,1},{2,10},{10,2},{3,11},{11,3},{4,12},{12,4},... | collective-permute-start | bytes 786440 | tf_op jit(solution)/shard_map/ppermute | solution.py:369
  18.2 2.2 %copy-start.7 = (s32[16]{0:T(128)S(1)}, s32[16]{0:T(128)}, u32[]{:S(2)}) copy-start(s32[16]{0:T(128)} %map_ref.7) | copy-start | bytes 196
  22.7 27.3 %copy-start.3 = (f32[5,8192]{1,0:T(8,128)S(1)}, f32[5,8192]{1,0:T(8,128)}, u32[]{:S(2)}) copy-start(f32[5,8192]{1,0:T(8,128)} %taps_ref.1) | copy-start | bytes 491524
  22.7 27.3 %copy-start.4 = (f32[16,3,512]{2,0,1:T(8,128)S(1)}, f32[16,3,512]{2,0,1:T(8,128)}, u32[]{:S(2)}) copy-start(f32[16,3,512]{2,0,1:T(8,128)} %param.28) | copy-start | bytes 294916
  22.7 27.3 %copy-start.6 = (f32[8192]{0:T(1024)S(1)}, f32[8192]{0:T(1024)}, u32[]{:S(2)}) copy-start(f32[8192]{0:T(1024)} %param.26) | copy-start | bytes 98308
  22.7 27.3 %copy-start.8 = (f32[128]{0:T(128)S(1)}, f32[128]{0:T(128)}, u32[]{:S(2)}) copy-start(f32[128]{0:T(128)} %a_ref.1) | copy-start | bytes 1540
  22.8 27.3 %copy-start.9 = (f32[128]{0:T(128)S(1)}, f32[128]{0:T(128)}, u32[]{:S(2)}) copy-start(f32[128]{0:T(128)} %bias_ref.1) | copy-start | bytes 1540
  22.8 27.3 %copy-start.10 = (f32[128]{0:T(128)S(1)}, f32[128]{0:T(128)}, u32[]{:S(2)}) copy-start(f32[128]{0:T(128)} %skip_ref.1) | copy-start | bytes 1540
  22.8 29.4 %copy-start.2 = (f32[16,3,2048]{2,0,1:T(8,128)S(1)}, f32[16,3,2048]{2,0,1:T(8,128)}, u32[]{:S(2)}) copy-start(f32[16,3,2048]{2,0,1:T(8,128)} %param.29) | copy-start | bytes 1179652
  22.8 29.4 %copy-start.5 = (f32[5,2048]{1,0:T(8,128)S(1)}, f32[5,2048]{1,0:T(8,128)}, u32[]{:S(2)}) copy-start(f32[5,2048]{1,0:T(8,128)} %bc_taps_ref.1) | copy-start | bytes 122884
  49.9 2.3 %collective-permute-start.3 = (bf16[8,32,128]{2,1,0:T(8,128)(2,1)S(1)}, bf16[8,32,128]{2,1,0:T(8,128)(2,1)S(1)}, u32[]{:S(2)}, u32[]{:S(2)}) collective-permute-start(bf16[8,32,128]{2,1,0:T(8,128)(2,1)S(1)} %slice.7.bc_ref), channel_id=1, source_target_pairs={{0,8},{8,0},{1,9},{9,1},{2,10},{10,2},{3,11},{11,3},{4,12},{12,4},... | collective-permute-start | bytes 196616 | tf_op jit(solution)/shard_map/ppermute | solution.py:369
  59.2 18.2 %all-to-all-start.2 = ((bf16[64,24,128]{2,1,0:T(8,128)(2,1)}), bf16[64,24,128]{2,1,0:T(8,128)(2,1)S(1)}, u32[]{:S(2)}, u32[]{:S(2)}) async-start(bf16[64,24,128]{2,1,0:T(8,128)(2,1)} %bitcast.9), calls=%async_computation.2 | async-start | bytes 786432 | tf_op jit(solution)/shard_map/all_to_all | solution.py:390
  66.5 11.0 %copy-start.1 = (bf16[16,64,512]{2,1,0:T(8,128)(2,1)S(1)}, bf16[16,64,512]{2,1,0:T(8,128)(2,1)}, u32[]{:S(2)}) copy-start(bf16[16,64,512]{2,1,0:T(8,128)(2,1)} %w_ref.3) | copy-start | bytes 3145732
  77.4 1.7 %collective-permute-start.4 = (bf16[8,8,24,128]{3,2,1,0:T(8,128)(2,1)S(1)}, bf16[8,8,24,128]{3,2,1,0:T(8,128)(2,1)S(1)}, u32[]{:S(2)}, u32[]{:S(2)}) collective-permute-start(bf16[8,8,24,128]{3,2,1,0:T(8,128)(2,1)S(1)} %bitcast.26), channel_id=1, source_target_pairs={{0,8},{8,0},{1,9},{9,1},{2,10},{10,2},{3,11},{11,3},{4,12},{12,4},... | collective-permute-start | bytes 1179656 | tf_op jit(solution)/shard_map/ppermute | solution.py:369
  80.7 12.6 %all-to-all-start.3 = ((bf16[8,32,512]{2,1,0:T(8,128)(2,1)}), bf16[8,32,512]{2,1,0:T(8,128)(2,1)S(1)}, u32[]{:S(2)}, u32[]{:S(2)}) async-start(bf16[8,32,512]{2,1,0:T(8,128)(2,1)} %share.3), calls=%async_computation.3 | async-start | bytes 524288 | tf_op jit(solution)/shard_map/all_to_all | solution.py:398

commit v6 on v5

--- a/solution.py
+++ b/solution.py
@@ -83,9 +83,9 @@
 DECAY, FIRST, SECOND, SKIP, GATE = range(0, 160, 32)
 
 
-def heads_kernel(
+def heads_part(
     map_ref, pos_ref, a_ref, bias_ref, skip_ref, taps_ref, gain_ref, xz_ref, x_hist_ref,
-    col_ref, x_out_ref, gain_out_ref,
+    col_ref, x_out_ref,
 ):
     head = map_ref[2 * pos_ref[0] + pos_ref[1]]
 
@@ -99,7 +99,6 @@
     def scalars(ref):
         return jnp.concatenate([jnp.full((1, 32), ref[head + 16 * j], F32) for j in range(8)], axis=0)
 
-    gain_out_ref[...] = local(gain_ref)
     rows = [xz_ref[j, 0:32, :] for j in range(8)]
     x = jnp.concatenate([v[:, 0:64] for v in rows], axis=1)
     z = jnp.concatenate([v[:, 64:128] for v in rows], axis=1)
@@ -129,22 +128,7 @@
             ],
             axis=1,
         )
-
-
-def heads_part(head_map, pos, a_log, dt_bias, skip_coef, conv_x, norm_gain, xz, x_hist):
-    return pl.pallas_call(
-        heads_kernel,
-        in_specs=[SMEM] * 5 + [VMEM] * 4,
-        out_specs=(VMEM,) * 3,
-        out_shape=(
-            jax.ShapeDtypeStruct((8, 64, 256), F32),
-            jax.ShapeDtypeStruct(x_hist.shape, F32),
-            jax.ShapeDtypeStruct((1, 512), F32),
-        ),
-        compiler_params=pltpu.CompilerParams(vmem_limit_bytes=16 * MIB),
-        cost_estimate=pl.CostEstimate(flops=2_000_000, bytes_accessed=1_000_000, transcendentals=50_000),
-        name="heads_part",
-    )(head_map, pos, a_log, dt_bias, skip_coef, conv_x, norm_gain[None], xz, x_hist)
+    return local(gain_ref)
 
 
 def projections(pos_ref, bc_ref, bc2_ref):
@@ -158,7 +142,9 @@
 
 
 def mixer_kernel(
-    pos_ref, gain_ref, col_ref, bc_ref, bc2_ref, bc_taps_ref, bc_hist_ref, state_ref, g_ref, b_ref, s_ref, sem,
+    map_ref, pos_ref, a_ref, bias_ref, skip_ref, taps_ref, gain_ref, xz_ref, x_hist_ref,
+    bc_ref, bc2_ref, bc_taps_ref, bc_hist_ref, state_ref,
+    g_ref, b_ref, col_ref, x_out_ref, s_ref, sem,
 ):
     copies = [
         pltpu.make_async_copy(
@@ -171,6 +157,10 @@
     ]
     for copy in copies:
         copy.start()
+    gain = heads_part(
+        map_ref, pos_ref, a_ref, bias_ref, skip_ref, taps_ref, gain_ref, xz_ref, x_hist_ref,
+        col_ref, x_out_ref,
+    )
     one, two = projections(pos_ref, bc_ref, bc2_ref)
     act1, act2 = conv(bc_hist_ref, one, two, bc_taps_ref[...])
     lane = lax.broadcasted_iota(jnp.int32, (32, 128), 1)
@@ -206,7 +196,7 @@
         total = jnp.concatenate([total, jnp.zeros((1, 96), F32)], axis=1)
         high = total.astype(BF16).astype(F32)
         tail = jnp.concatenate([high, total - high, jnp.zeros((6, 128), F32)], axis=0)
-        rows = jnp.concatenate(gated, axis=0).T * gain_ref[0:1, 128 * g : 128 * g + 128]
+        rows = jnp.concatenate(gated, axis=0).T * gain[:, 128 * g : 128 * g + 128]
         for j in range(2):
             lanes = slice(64 * j, 64 * j + 64)
             block = jnp.concatenate(
@@ -216,20 +206,28 @@
                 g_ref[chip, 2 * g + j] = block
 
 
-def mixer(pos, gain, cols, bc, bc2, bc_taps, bc_hist, state):
+def mixer(
+    head_map, pos, a_log, dt_bias, skip_coef, conv_x, norm_gain, xz, x_hist,
+    bc, bc2, bc_taps, bc_hist, state,
+):
     return pl.pallas_call(
         mixer_kernel,
-        in_specs=[SMEM] + [VMEM] * 6 + [HBM],
-        out_specs=(VMEM,) * 2,
+        in_specs=[SMEM] * 5 + [VMEM] * 8 + [HBM],
+        out_specs=(VMEM,) * 4,
         out_shape=(
             jax.ShapeDtypeStruct((8, 8, 24, 128), BF16),
             jax.ShapeDtypeStruct((4, 32, 256), F32),
+            jax.ShapeDtypeStruct((8, 64, 256), F32),
+            jax.ShapeDtypeStruct(x_hist.shape, F32),
         ),
         scratch_shapes=[pltpu.VMEM((4, 16, 2, 64, 256), F32), pltpu.SemaphoreType.DMA((4, 16 // PART))],
         compiler_params=pltpu.CompilerParams(vmem_limit_bytes=STATE_MIB * MIB),
         cost_estimate=pl.CostEstimate(flops=20_000_000, bytes_accessed=9_000_000, transcendentals=100_000),
         name="mixer",
-    )(pos, gain, cols, bc, bc2, bc_taps, bc_hist, state)
+    )(
+        head_map, pos, a_log, dt_bias, skip_coef, conv_x, norm_gain[None], xz, x_hist,
+        bc, bc2, bc_taps, bc_hist, state,
+    )
 
 
 def advance_kernel(start, col_ref, b_ref, state_ref, *refs):
@@ -380,12 +378,10 @@
     summed = jnp.sum(received.reshape(8, 8, 72, 128).astype(F32), axis=0) * (1.0 / SCALE)
     low = summed[:, 32:64, :].astype(BF16)
     low2 = swap(low)
-    cols, x_hist, gain = heads_part(
+    gated, b, cols, x_hist = mixer(
         head_map, pos, a_log, dt_bias, skip_coef, conv_x, norm_gain, summed,
-        conv_x_state.transpose(1, 0, 2),
-    )
-    gated, b = mixer(
-        pos, gain, cols, low, low2, conv_bc, conv_bc_state.transpose(1, 0, 2), ssm_state,
+        conv_x_state.transpose(1, 0, 2), low, low2, conv_bc, conv_bc_state.transpose(1, 0, 2),
+        ssm_state,
     )
     gathered = lax.all_to_all(gated.reshape(64, 24, 128), ("chip", "tp"), 0, 0, tiled=True).reshape(8, 8, 24, 128)
     bc_hist = history(pos, low, low2, conv_bc_state.transpose(1, 0, 2))

time: 94.7 us -> 94.5 us (level)
  Pallas kernels: 23.3 us -> 22.2 us
  waiting for transfers between devices: 17.2 us -> 18.2 us
    ppermute x5, waiting for transfers between devices: 0.83 us -> 2.07 us  [swap(): return lax.ppermute(v, 'core', [(0, 1), (1, 0)])]
    pallas_call x2 -> x1, Pallas kernels: 9.15 us -> 8 us  [mixer(): pl.pallas_call(mixer_kernel, in_specs=[SMEM] * 5 + [VMEM] * 8 + [HBM], ou...]
  transfers between devices with their start and end apart: 8 -> 8, of which waited for: 4 -> 5; matrix products, arithmetic and copies ran while one was open for 7% -> 8% of each run, Pallas kernels for 13% -> 11%
where the time goes in v6:
time: 94.5 us; the launch traced here: 93.8 us
  blocking collectives  26.9 us (28%)
  Pallas kernels  22.2 us (23%)
  waiting for transfers between devices  18.2 us (19%)
  starting transfers between devices  16.6 us (18%)
  local copies, waits for them, and re-layouts  6.93 us (7%)
  other arithmetic  2.1 us (2%)
    all_to_all x1, blocking collectives, per_device(): received = lax.all_to_all(partial, ('chip', 'tp'), 0, 0, tiled=True)  26.9 us
    pallas_call x2, Pallas kernels, advance(): pl.pallas_call(functools.partial(advance_kernel, start), grid=(1,), in_sp...  8.23 us
    pallas_call x1, Pallas kernels, mixer(): pl.pallas_call(mixer_kernel, in_specs=[SMEM] * 5 + [VMEM] * 8 + [HBM], ou...  8 us
    all_to_all x1, starting transfers between devices, per_device(): lax.all_to_all(jnp.broadcast_to(x[None], (8, 32, 512)), 'tp', 0, 0, tiled...  7.01 us
    all_to_all x1, waiting for transfers between devices, per_device(): lax.all_to_all(gated.reshape(64, 24, 128), ('chip', 'tp'), 0, 0, tiled=True)  6.47 us
    unnamed x25, local copies, waits for them, and re-layouts  6.11 us
    all_to_all x1, starting transfers between devices, per_device(): lax.all_to_all(gated.reshape(64, 24, 128), ('chip', 'tp'), 0, 0, tiled=True)  5.92 us
    all_to_all x1, waiting for transfers between devices, per_device(): shares = lax.all_to_all(shares, 'tp', 0, 0, tiled=True)  5.08 us
  transfers between devices with their start and end apart: 8, of which 5 were waited for; matrix products, arithmetic and copies ran while one was open for 8% of the time, Pallas kernels for 11%

profile of v6, /device:TPU:0, one launch (start us, length us, event | category | flops | bytes accessed | tf_op | source)
XLA Modules:
  0.0 93.8 jit_solution(9902166930416251022)
XLA Ops:
  0.6 0.0 copy-start
  0.6 0.1 collective-permute-start.1
  0.8 0.9 copy-done
  1.7 0.7 broadcast_in_dim.13
  2.4 7.0 %all-to-all-start = ((bf16[8,32,512]{2,1,0:T(8,128)(2,1)}), bf16[8,32,512]{2,1,0:T(8,128)(2,1)S(1)}, u32[]{:S(2)}, u32[]{:S(2)}) async-start(bf16[8,32,512]{2,1,0:T(8,128)(2,1)} %broadcast_in_dim.13), calls=%async_computation | async-start | bytes 524288 | tf_op jit(solution)/shard_map/all_to_all | solution.py:373
  9.4 0.8 copy.20
  10.3 0.1 pad.2.clone
  10.3 1.0 %maximum_maximum_fusion.wbd_ref = bf16[512,384]{1,0:T(8,128)(2,1)S(1)} fusion(bf16[512,16]{1,0:T(8,128)(2,1)S(1)} %copy.20, bf16[512,256]{1,0:T(8,128)(2,1)} %param.18, bf16[384]{0:T(512)(128)(2,1)S(1)} %pad.2.clone), kind=kLoop, calls=%fused_computation.3 | loop fusion | flops 1179648 | bytes 672512 | tf_op jit(solution)/shard_map/concatenate | solution.py:370
  11.4 0.1 collective-permute-start.2
  11.5 2.1 %copy.26 = bf16[64,8,16,128]{3,1,2,0:T(8,128)(2,1)S(1)} copy(bf16[64,8,16,128]{3,2,1,0:T(8,128)(2,1)} %bitcast.36) | data formatting | bytes 4194304
  13.6 4.5 %all-to-all-done = bf16[8,32,512]{2,1,0:T(8,128)(2,1)S(1)} async-done(((bf16[8,32,512]{2,1,0:T(8,128)(2,1)}), bf16[8,32,512]{2,1,0:T(8,128)(2,1)S(1)}, u32[]{:S(2)}, u32[]{:S(2)}) %all-to-all-start) | async-done | bytes 262176 | tf_op jit(solution)/shard_map/all_to_all | solution.py:373
  18.2 0.1 pad_add_fusion.pos_ref
  18.2 2.1 %copy.25 = bf16[64,8,16,128]{3,1,2,0:T(8,128)(2,1)S(1)} copy(bf16[64,8,16,128]{3,2,1,0:T(8,128)(2,1)} %bitcast.17) | data formatting | bytes 4194304
  20.4 2.1 %project.1 = f32[8,8,72,128]{3,2,1,0:T(8,128)S(1)} custom-call(s32[16]{0:T(128)S(1)} %copy-done.7, s32[2]{0:T(128)S(1)} %pad_add_fusion.pos_ref, bf16[256,512]{1,0:T(8,128)(2,1)S(1)} %bitcast.31, bf16[256,512]{1,0:T(8,128)(2,1)S(1)} %collective-permute-done.x2_ref, bf16[512,2048]{1,0:T(8,128)(2,1)S(1)} %bitcast.24, bf16[512,2048]{1,0:T(8,128)(2,1)S(1)} %bitcast.25, ...), custom_call_target="tpu_custom_call" | custom-call | flops 600000000 | bytes 5500000 | tf_op jit(solution)/shard_map/project/pallas_call | solution.py:63
  22.5 0.2 convert_element_type.15
  22.7 0.0 copy-start.4
  22.8 26.9 %all_to_all.20 = f16[64,72,128]{2,1,0:T(8,128)(2,1)S(1)} all-to-all(f16[64,72,128]{2,1,0:T(8,128)(2,1)S(1)} %bitcast.34), channel_id=1, replica_groups=mesh['chip'=8,'core'=2,'tp'=8] {'chip','tp'}, dimensions={0} | all-to-all | bytes 2359296 | tf_op jit(solution)/shard_map/all_to_all | solution.py:377
  49.7 0.2 convert_reduce_fusion
  49.9 0.1 collective-permute-start.3
  50.0 1.2 %collective-permute-done.3.bc2_ref = bf16[8,32,128]{2,1,0:T(8,128)(2,1)S(1)} collective-permute-done((bf16[8,32,128]{2,1,0:T(8,128)(2,1)S(1)}, bf16[8,32,128]{2,1,0:T(8,128)(2,1)S(1)}, u32[]{:S(2)}, u32[]{:S(2)}) %collective-permute-start.3) | collective-permute-done | bytes 65568 | tf_op jit(solution)/shard_map/ppermute | solution.py:367
  51.3 8.0 %mixer.1 = (bf16[8,8,24,128]{3,2,1,0:T(8,128)(2,1)}, f32[4,32,256]{2,1,0:T(8,128)S(1)}, f32[8,64,256]{2,1,0:T(8,128)S(1)}, f32[3,16,512]{2,1,0:T(8,128)}) custom-call(s32[16]{0:T(128)S(1)} %copy-done.7, s32[2]{0:T(128)S(1)} %pad_add_fusion.pos_ref, f32[128]{0:T(128)S(1)} %copy-done.8, f32[128]{0:T(128)S(1)} %copy-done.9, f32[128]{0:T(128)S(1)} %copy-done.10, ...), custom_call_target="tpu_custom_call" | custom-call | flops 20000000 | bytes 9000000 | tf_op jit(solution)/shard_map/mixer/pallas_call | solution.py:213
  59.3 5.9 %all-to-all-start.2 = ((bf16[64,24,128]{2,1,0:T(8,128)(2,1)}), bf16[64,24,128]{2,1,0:T(8,128)(2,1)S(1)}, u32[]{:S(2)}, u32[]{:S(2)}) async-start(bf16[64,24,128]{2,1,0:T(8,128)(2,1)} %bitcast.9), calls=%async_computation.2 | async-start | bytes 786432 | tf_op jit(solution)/shard_map/all_to_all | solution.py:386
  65.2 1.3 %history.1 = f32[3,16,2048]{2,1,0:T(8,128)} custom-call(s32[2]{0:T(128)S(1)} %pad_add_fusion.pos_ref, bf16[8,32,128]{2,1,0:T(8,128)(2,1)S(1)} %slice.7.bc_ref, bf16[8,32,128]{2,1,0:T(8,128)(2,1)S(1)} %collective-permute-done.3.bc2_ref, f32[3,16,2048]{2,1,0:T(8,128)S(1)} %bitcast.27), custom_call_target="tpu_custom_call" | custom-call | bytes 900000 | tf_op jit(solution)/shard_map/history/pallas_call | solution.py:299
  66.6 4.2 %advance.2.refs_0_ = f32[16,8,64,256]{3,2,1,0:T(8,128)} custom-call(f32[8,64,256]{2,1,0:T(8,128)S(1)} %get-tuple-element.18.col_ref, f32[4,32,256]{2,1,0:T(8,128)S(1)} %get-tuple-element.19.b_ref, f32[16,8,64,256]{3,2,1,0:T(8,128)} %state_ref.5), custom_call_target="tpu_custom_call" | custom-call | flops 6000000 | bytes 8500000 | tf_op jit(solution)/shard_map/advance/pallas_call | solution.py:271
  70.7 6.5 %all-to-all-done.2 = bf16[64,24,128]{2,1,0:T(8,128)(2,1)S(1)} async-done(((bf16[64,24,128]{2,1,0:T(8,128)(2,1)}), bf16[64,24,128]{2,1,0:T(8,128)(2,1)S(1)}, u32[]{:S(2)}, u32[]{:S(2)}) %all-to-all-start.2) | async-done | bytes 393248 | tf_op jit(solution)/shard_map/all_to_all | solution.py:386
  77.2 0.9 share.2
  78.1 0.8 collective-permute-done.4.g_ref
  78.9 1.6 %share.3 = bf16[8,32,512]{2,1,0:T(8,128)(2,1)} custom-call(s32[16]{0:T(128)S(1)} %copy-done.7, s32[2]{0:T(128)S(1)} %pad_add_fusion.pos_ref, bf16[8,8,24,128]{3,2,1,0:T(8,128)(2,1)S(1)} %collective-permute-done.4.g_ref, bf16[16,64,512]{2,1,0:T(8,128)(2,1)S(1)} %copy-done.1, f32[256,512]{1,0:T(8,128)S(1)} %get-tuple-element.21.refs_0_, ...), custom_call_target="tpu_custom_call" | custom-call | flops 140000000 | bytes 1500000 | tf_op jit(solution)/shard_map/share/pallas_call | solution.py:347
  80.5 3.5 %all-to-all-start.3 = ((bf16[8,32,512]{2,1,0:T(8,128)(2,1)}), bf16[8,32,512]{2,1,0:T(8,128)(2,1)S(1)}, u32[]{:S(2)}, u32[]{:S(2)}) async-start(bf16[8,32,512]{2,1,0:T(8,128)(2,1)} %share.3), calls=%async_computation.3 | async-start | bytes 524288 | tf_op jit(solution)/shard_map/all_to_all | solution.py:394
  84.0 4.1 %advance.3 = f32[16,8,64,256]{3,2,1,0:T(8,128)} custom-call(f32[8,64,256]{2,1,0:T(8,128)S(1)} %get-tuple-element.18.col_ref, f32[4,32,256]{2,1,0:T(8,128)S(1)} %get-tuple-element.19.b_ref, f32[16,8,64,256]{3,2,1,0:T(8,128)} %state_ref.5, f32[16,8,64,256]{3,2,1,0:T(8,128)} %advance.2.refs_0_), custom_call_target="tpu_custom_call", output_to_operand_aliasing={{}: (3, {})} | custom-call | flops 6000000 | bytes 8500000 | tf_op jit(solution)/shard_map/advance/pallas_call | solution.py:271
  88.1 5.1 %all-to-all-done.3 = bf16[8,32,512]{2,1,0:T(8,128)(2,1)S(1)} async-done(((bf16[8,32,512]{2,1,0:T(8,128)(2,1)}), bf16[8,32,512]{2,1,0:T(8,128)(2,1)S(1)}, u32[]{:S(2)}, u32[]{:S(2)}) %all-to-all-start.3) | async-done | bytes 262176 | tf_op jit(solution)/shard_map/all_to_all | solution.py:394
  93.2 0.7 reduce_sum.22
  (28 shorter events, 0.1 us)
Async XLA Ops:
  0.6 1.0 %copy-start = (bf16[2,16,8192]{2,1,0:T(8,128)(2,1)S(1)}, bf16[2,16,8192]{2,1,0:T(8,128)(2,1)}, u32[]{:S(2)}) copy-start(bf16[2,16,8192]{2,1,0:T(8,128)(2,1)} %param.15) | copy-start | bytes 1572868
  0.6 17.6 %collective-permute-start.1 = (bf16[512,16,128]{2,1,0:T(8,128)(2,1)}, bf16[512,16,128]{2,1,0:T(8,128)(2,1)}, u32[]{:S(2)}, u32[]{:S(2)}) collective-permute-start(bf16[512,16,128]{2,1,0:T(8,128)(2,1)} %param.16), channel_id=1, source_target_pairs={{0,8},{8,0},{1,9},{9,1},{2,10},{10,2},{3,11},{11,3},{4,12},{12,4},... | collective-permute-start | bytes 6291464 | tf_op jit(solution)/shard_map/ppermute | solution.py:367
  2.4 15.7 %all-to-all-start = ((bf16[8,32,512]{2,1,0:T(8,128)(2,1)}), bf16[8,32,512]{2,1,0:T(8,128)(2,1)S(1)}, u32[]{:S(2)}, u32[]{:S(2)}) async-start(bf16[8,32,512]{2,1,0:T(8,128)(2,1)} %broadcast_in_dim.13), calls=%async_computation | async-start | bytes 524288 | tf_op jit(solution)/shard_map/all_to_all | solution.py:373
  11.4 9.0 %collective-permute-start.2 = (bf16[512,384]{1,0:T(8,128)(2,1)S(1)}, bf16[512,384]{1,0:T(8,128)(2,1)}, u32[]{:S(2)}, u32[]{:S(2)}) collective-permute-start(bf16[512,384]{1,0:T(8,128)(2,1)S(1)} %maximum_maximum_fusion.wbd_ref), channel_id=1, source_target_pairs={{0,8},{8,0},{1,9},{9,1},{2,10},{10,2},{3,11},{11,3},{4,12},{12,4},... | collective-permute-start | bytes 1179656 | tf_op jit(solution)/shard_map/ppermute | solution.py:367
  18.2 2.2 %collective-permute-start = (bf16[256,512]{1,0:T(8,128)(2,1)S(1)}, bf16[256,512]{1,0:T(8,128)(2,1)S(1)}, u32[]{:S(2)}, u32[]{:S(2)}) collective-permute-start(bf16[256,512]{1,0:T(8,128)(2,1)S(1)} %bitcast.30), channel_id=1, source_target_pairs={{0,8},{8,0},{1,9},{9,1},{2,10},{10,2},{3,11},{11,3},{4,12},{12,4},... | collective-permute-start | bytes 786440 | tf_op jit(solution)/shard_map/ppermute | solution.py:367
  18.2 2.2 %copy-start.7 = (s32[16]{0:T(128)S(1)}, s32[16]{0:T(128)}, u32[]{:S(2)}) copy-start(s32[16]{0:T(128)} %map_ref.7) | copy-start | bytes 196
  22.7 28.6 %copy-start.2 = (f32[16,3,2048]{2,0,1:T(8,128)S(1)}, f32[16,3,2048]{2,0,1:T(8,128)}, u32[]{:S(2)}) copy-start(f32[16,3,2048]{2,0,1:T(8,128)} %param.29) | copy-start | bytes 1179652
  22.7 28.6 %copy-start.3 = (f32[5,8192]{1,0:T(8,128)S(1)}, f32[5,8192]{1,0:T(8,128)}, u32[]{:S(2)}) copy-start(f32[5,8192]{1,0:T(8,128)} %taps_ref.1) | copy-start | bytes 491524
  22.7 28.5 %copy-start.4 = (f32[16,3,512]{2,0,1:T(8,128)S(1)}, f32[16,3,512]{2,0,1:T(8,128)}, u32[]{:S(2)}) copy-start(f32[16,3,512]{2,0,1:T(8,128)} %param.28) | copy-start | bytes 294916
  22.7 28.5 %copy-start.5 = (f32[5,2048]{1,0:T(8,128)S(1)}, f32[5,2048]{1,0:T(8,128)}, u32[]{:S(2)}) copy-start(f32[5,2048]{1,0:T(8,128)} %bc_taps_ref.1) | copy-start | bytes 122884
  22.7 28.5 %copy-start.6 = (f32[8192]{0:T(1024)S(1)}, f32[8192]{0:T(1024)}, u32[]{:S(2)}) copy-start(f32[8192]{0:T(1024)} %param.26) | copy-start | bytes 98308
  22.8 28.5 %copy-start.8 = (f32[128]{0:T(128)S(1)}, f32[128]{0:T(128)}, u32[]{:S(2)}) copy-start(f32[128]{0:T(128)} %a_ref.1) | copy-start | bytes 1540
  22.8 28.5 %copy-start.9 = (f32[128]{0:T(128)S(1)}, f32[128]{0:T(128)}, u32[]{:S(2)}) copy-start(f32[128]{0:T(128)} %bias_ref.1) | copy-start | bytes 1540
  22.8 28.5 %copy-start.10 = (f32[128]{0:T(128)S(1)}, f32[128]{0:T(128)}, u32[]{:S(2)}) copy-start(f32[128]{0:T(128)} %skip_ref.1) | copy-start | bytes 1540
  49.9 1.3 %collective-permute-start.3 = (bf16[8,32,128]{2,1,0:T(8,128)(2,1)S(1)}, bf16[8,32,128]{2,1,0:T(8,128)(2,1)S(1)}, u32[]{:S(2)}, u32[]{:S(2)}) collective-permute-start(bf16[8,32,128]{2,1,0:T(8,128)(2,1)S(1)} %slice.7.bc_ref), channel_id=1, source_target_pairs={{0,8},{8,0},{1,9},{9,1},{2,10},{10,2},{3,11},{11,3},{4,12},{12,4},... | collective-permute-start | bytes 196616 | tf_op jit(solution)/shard_map/ppermute | solution.py:367
  59.3 17.9 %all-to-all-start.2 = ((bf16[64,24,128]{2,1,0:T(8,128)(2,1)}), bf16[64,24,128]{2,1,0:T(8,128)(2,1)S(1)}, u32[]{:S(2)}, u32[]{:S(2)}) async-start(bf16[64,24,128]{2,1,0:T(8,128)(2,1)} %bitcast.9), calls=%async_computation.2 | async-start | bytes 786432 | tf_op jit(solution)/shard_map/all_to_all | solution.py:386
  66.6 10.6 %copy-start.1 = (bf16[16,64,512]{2,1,0:T(8,128)(2,1)S(1)}, bf16[16,64,512]{2,1,0:T(8,128)(2,1)}, u32[]{:S(2)}) copy-start(bf16[16,64,512]{2,1,0:T(8,128)(2,1)} %w_ref.3) | copy-start | bytes 3145732
  77.2 1.7 %collective-permute-start.4 = (bf16[8,8,24,128]{3,2,1,0:T(8,128)(2,1)S(1)}, bf16[8,8,24,128]{3,2,1,0:T(8,128)(2,1)S(1)}, u32[]{:S(2)}, u32[]{:S(2)}) collective-permute-start(bf16[8,8,24,128]{3,2,1,0:T(8,128)(2,1)S(1)} %bitcast.28), channel_id=1, source_target_pairs={{0,8},{8,0},{1,9},{9,1},{2,10},{10,2},{3,11},{11,3},{4,12},{12,4},... | collective-permute-start | bytes 1179656 | tf_op jit(solution)/shard_map/ppermute | solution.py:367
  80.5 12.6 %all-to-all-start.3 = ((bf16[8,32,512]{2,1,0:T(8,128)(2,1)}), bf16[8,32,512]{2,1,0:T(8,128)(2,1)S(1)}, u32[]{:S(2)}, u32[]{:S(2)}) async-start(bf16[8,32,512]{2,1,0:T(8,128)(2,1)} %share.3), calls=%async_computation.3 | async-start | bytes 524288 | tf_op jit(solution)/shard_map/all_to_all | solution.py:394
